TPU v7x, 32 devices: a whole 2x2x4 slice. The times are simulated.
32 devices in a mesh: org: 8 (over y, x, core), dst: 4 (over z).
Axes of the slice: x: 2, y: 2, z: 4, core: 2. Of those that a mesh axis runs over, the one named last changes fastest.
Arguments:
- counts: int32 [8, 4096, 4096], P(None, 'org', 'dst'), may hold values from 0 to 127, as said below
- block_scales: float32 [8, 32, 32], P(None, 'org', 'dst'), may hold values from 0.05 to 12.5, as said below
- anchor_factor: float32 [64, 4096], P(None, 'org'), may hold values from 0.2 to 9, as said below
- dest_factor: float32 [64, 4096], P(None, 'dst'), may hold values from 0.2 to 9, as said below
- hour_factor: float32 [8, 64], replicated, may hold values from 0.5 to 2
Outputs:
- anchor_updated: float32 [64, 4096], P(None, 'org')
- dest_updated: float32 [64, 4096], P(None, 'dst')
Inputs may be any that keep to these rules, and one draw needn't show every extreme that they name: Whole trip counts. `block_scales`: positive. `anchor_factor`: positive. `dest_factor`: positive.
All inputs are finite; a program needn't handle non-finite values.
Results may differ from a plain program's by a relative error of at most 0.0003.
Values sent between devices are 32-bit elements; how exact they have to be, the bound alone decides.
No kernel may reach another device: no remote copies, remote signals or barrier semaphores. Data moves between devices by JAX's collectives and lax.ppermute only.
A program may use at most 128 MiB of HBM per device.

v0:
```python
import jax
import jax.numpy as jnp
from jax import lax
from jax.sharding import PartitionSpec as P

SCALE_BLOCK = 128
SWEEPS = 6


def dequantize(counts, scales):
    n_hours, row_count, col_count = counts.shape
    blocks = counts.reshape(
        n_hours, row_count // SCALE_BLOCK, SCALE_BLOCK, col_count // SCALE_BLOCK, SCALE_BLOCK
    ).astype(jnp.float32)
    values = blocks * scales[:, :, None, :, None]
    return values.reshape(n_hours, row_count, col_count).astype(jnp.bfloat16)


def anchor_products(tensor, dest_now, hour_factor):
    per_hour = jnp.einsum(
        "rj,hij->hri", dest_now.astype(jnp.bfloat16), tensor, preferred_element_type=jnp.float32
    )
    return jnp.einsum("hri,hr->ri", per_hour, hour_factor, precision=lax.Precision.HIGHEST)


def dest_products(tensor, anchor_now, hour_factor):
    per_hour = jnp.einsum(
        "ri,hij->hrj", anchor_now.astype(jnp.bfloat16), tensor, preferred_element_type=jnp.float32
    )
    return jnp.einsum("hrj,hr->rj", per_hour, hour_factor, precision=lax.Precision.HIGHEST)


def local_gram(factor):
    return jnp.dot(factor, factor.T, precision=lax.Precision.HIGHEST)


def update(factor, totals, gram_part):
    return factor * totals / jnp.dot(gram_part, factor, precision=lax.Precision.HIGHEST)


def anchor_step(anchor_now, totals, dest_now, hour_gram):
    own_gram = local_gram(dest_now)
    summed = lax.psum(totals, "dst")
    gram_part = lax.psum(own_gram, "dst") * hour_gram
    updated = update(anchor_now, summed, gram_part)
    return updated


def dest_step(dest_now, totals, anchor_now, hour_gram):
    own_gram = local_gram(anchor_now)
    summed = lax.psum(totals, "org")
    gram_part = lax.psum(own_gram, "org") * hour_gram
    updated = update(dest_now, summed, gram_part)
    return updated


def body(counts, block_scales, anchor_factor, dest_factor, hour_factor):
    tensor = dequantize(counts, block_scales)
    hour_gram = jnp.dot(hour_factor.T, hour_factor, precision=lax.Precision.HIGHEST)
    anchor_now = anchor_factor
    dest_now = dest_factor
    for sweep_index in range(SWEEPS):
        anchor_totals = anchor_products(tensor, dest_now, hour_factor)
        anchor_now = anchor_step(anchor_now, anchor_totals, dest_now, hour_gram)
        dest_totals = dest_products(tensor, anchor_now, hour_factor)
        dest_now = dest_step(dest_now, dest_totals, anchor_now, hour_gram)
    return (anchor_now, dest_now)


def solution(mesh):
    return jax.shard_map(
        body,
        mesh=mesh,
        in_specs=(
            P(None, "org", "dst"),
            P(None, "org", "dst"),
            P(None, "org"),
            P(None, "dst"),
            P(),
        ),
        out_specs=(P(None, "org"), P(None, "dst")),
        check_vma=False,
    )
```

profile of v0, /device:TPU:0, one launch (start us, length us, event | category | flops | bytes accessed | tf_op | source)
XLA Modules:
  0.0 699.3 jit_solution(12571238087752529404)
XLA Ops:
  7.2 7.6 %mul.83 = f32[8,4,128,8,128]{4,3,2,1,0:T(8,128)} broadcast(f32[8,4,8]{2,1,0:T(4,128)} %param.6), dimensions={0,1,3} | broadcast | bytes 16778240 | tf_op jit(solution)/shard_map/mul | solution.py:15
  14.8 18.0 %mul.84 = f32[8,512,1024]{2,1,0:T(8,128)} reshape(f32[8,4,128,8,128]{4,3,2,1,0:T(8,128)} %mul.83) | data formatting | bytes 33554432 | tf_op jit(solution)/shard_map/mul | solution.py:15
  32.9 12.0 %multiply_convert_fusion = bf16[8,512,1024]{2,1,0:T(8,128)(2,1)S(1)} fusion(f32[8,512,1024]{2,1,0:T(8,128)} %mul.84, s32[8,512,1024]{2,1,0:T(8,128)} %param.5), kind=kLoop, calls=%fused_computation | loop fusion | flops 12582912 | bytes 41943040 | tf_op jit(solution)/shard_map/convert_element_type | solution.py:16
  53.6 21.0 %psum.169 = f32[64,64]{1,0:T(8,128)S(1)} all-reduce(f32[64,64]{1,0:T(8,128)S(1)} %fusion.60), channel_id=1, replica_groups=mesh['org'=8,'dst'=4] {'dst'}, use_global_device_ids=true, to_apply=%region_1.0 | all-reduce | flops 4096 | bytes 32768 | tf_op jit(solution)/shard_map/psum | solution.py:44
  74.8 15.8 %all-reduce.13.cloned.1.call-done = f32[64,512]{1,0:T(8,128)} async-done(((f32[64,512]{1,0:T(8,128)}), f32[64,512]{1,0:T(8,128)}) %all-reduce.13.cloned.1.call-update) | async-done | bytes 131088 | tf_op jit(solution)/shard_map/psum | solution.py:43
  101.2 22.3 %psum.171 = f32[64,64]{1,0:T(8,128)S(1)} all-reduce(f32[64,64]{1,0:T(8,128)S(1)} %fusion.62), channel_id=1, replica_groups=mesh['org'=8,'dst'=4] {'org'}, use_global_device_ids=true, to_apply=%region_3.0 | all-reduce | flops 4096 | bytes 32768 | tf_op jit(solution)/shard_map/psum | solution.py:52
  123.5 30.5 %all-reduce.15.cloned.1.call-done = f32[64,1024]{1,0:T(8,128)} async-done(((f32[64,1024]{1,0:T(8,128)}), f32[64,1024]{1,0:T(8,128)}) %all-reduce.15.cloned.1.call-update) | async-done | bytes 262160 | tf_op jit(solution)/shard_map/psum | solution.py:51
  155.3 6.0 convolution_bitcast_fusion.10
  164.1 19.1 %psum.173 = f32[64,64]{1,0:T(8,128)S(1)} all-reduce(f32[64,64]{1,0:T(8,128)S(1)} %fusion.63), channel_id=1, replica_groups=mesh['org'=8,'dst'=4] {'dst'}, use_global_device_ids=true, to_apply=%region_5.0 | all-reduce | flops 4096 | bytes 32768 | tf_op jit(solution)/shard_map/psum | solution.py:44
  183.2 14.5 %all-reduce.17.cloned.1.call-done = f32[64,512]{1,0:T(8,128)} async-done(((f32[64,512]{1,0:T(8,128)}), f32[64,512]{1,0:T(8,128)}) %all-reduce.17.cloned.1.call-update) | async-done | bytes 131088 | tf_op jit(solution)/shard_map/psum | solution.py:43
  208.1 22.8 %psum.175 = f32[64,64]{1,0:T(8,128)S(1)} all-reduce(f32[64,64]{1,0:T(8,128)S(1)} %fusion.64), channel_id=1, replica_groups=mesh['org'=8,'dst'=4] {'org'}, use_global_device_ids=true, to_apply=%region_7.0 | all-reduce | flops 4096 | bytes 32768 | tf_op jit(solution)/shard_map/psum | solution.py:52
  231.0 30.2 %all-reduce.19.cloned.1.call-done = f32[64,1024]{1,0:T(8,128)} async-done(((f32[64,1024]{1,0:T(8,128)}), f32[64,1024]{1,0:T(8,128)}) %all-reduce.19.cloned.1.call-update) | async-done | bytes 262160 | tf_op jit(solution)/shard_map/psum | solution.py:51
  262.5 6.0 convolution_bitcast_fusion.9
  271.3 19.1 %psum.177 = f32[64,64]{1,0:T(8,128)S(1)} all-reduce(f32[64,64]{1,0:T(8,128)S(1)} %fusion.65), channel_id=1, replica_groups=mesh['org'=8,'dst'=4] {'dst'}, use_global_device_ids=true, to_apply=%region_9.0 | all-reduce | flops 4096 | bytes 32768 | tf_op jit(solution)/shard_map/psum | solution.py:44
  290.4 14.6 %all-reduce.21.cloned.1.call-done = f32[64,512]{1,0:T(8,128)} async-done(((f32[64,512]{1,0:T(8,128)}), f32[64,512]{1,0:T(8,128)}) %all-reduce.21.cloned.1.call-update) | async-done | bytes 131088 | tf_op jit(solution)/shard_map/psum | solution.py:43
  315.3 22.5 %psum.179 = f32[64,64]{1,0:T(8,128)S(1)} all-reduce(f32[64,64]{1,0:T(8,128)S(1)} %fusion.66), channel_id=1, replica_groups=mesh['org'=8,'dst'=4] {'org'}, use_global_device_ids=true, to_apply=%region_11.0 | all-reduce | flops 4096 | bytes 32768 | tf_op jit(solution)/shard_map/psum | solution.py:52
  337.9 30.5 %all-reduce.23.cloned.1.call-done = f32[64,1024]{1,0:T(8,128)} async-done(((f32[64,1024]{1,0:T(8,128)}), f32[64,1024]{1,0:T(8,128)}) %all-reduce.23.cloned.1.call-update) | async-done | bytes 262160 | tf_op jit(solution)/shard_map/psum | solution.py:51
  369.7 6.0 convolution_bitcast_fusion.8
  378.5 19.1 %psum.181 = f32[64,64]{1,0:T(8,128)S(1)} all-reduce(f32[64,64]{1,0:T(8,128)S(1)} %fusion.67), channel_id=1, replica_groups=mesh['org'=8,'dst'=4] {'dst'}, use_global_device_ids=true, to_apply=%region_13.0 | all-reduce | flops 4096 | bytes 32768 | tf_op jit(solution)/shard_map/psum | solution.py:44
  397.7 14.6 %all-reduce.25.cloned.1.call-done = f32[64,512]{1,0:T(8,128)} async-done(((f32[64,512]{1,0:T(8,128)}), f32[64,512]{1,0:T(8,128)}) %all-reduce.25.cloned.1.call-update) | async-done | bytes 131088 | tf_op jit(solution)/shard_map/psum | solution.py:43
  422.6 22.6 %psum.183 = f32[64,64]{1,0:T(8,128)S(1)} all-reduce(f32[64,64]{1,0:T(8,128)S(1)} %fusion.68), channel_id=1, replica_groups=mesh['org'=8,'dst'=4] {'org'}, use_global_device_ids=true, to_apply=%region_15.0 | all-reduce | flops 4096 | bytes 32768 | tf_op jit(solution)/shard_map/psum | solution.py:52
  445.2 30.4 %all-reduce.27.cloned.1.call-done = f32[64,1024]{1,0:T(8,128)} async-done(((f32[64,1024]{1,0:T(8,128)}), f32[64,1024]{1,0:T(8,128)}) %all-reduce.27.cloned.1.call-update) | async-done | bytes 262160 | tf_op jit(solution)/shard_map/psum | solution.py:51
  476.9 6.0 convolution_bitcast_fusion.7
  485.7 19.1 %psum.185 = f32[64,64]{1,0:T(8,128)S(1)} all-reduce(f32[64,64]{1,0:T(8,128)S(1)} %fusion.69), channel_id=1, replica_groups=mesh['org'=8,'dst'=4] {'dst'}, use_global_device_ids=true, to_apply=%region_17.0 | all-reduce | flops 4096 | bytes 32768 | tf_op jit(solution)/shard_map/psum | solution.py:44
  504.9 14.5 %all-reduce.29.cloned.1.call-done = f32[64,512]{1,0:T(8,128)} async-done(((f32[64,512]{1,0:T(8,128)}), f32[64,512]{1,0:T(8,128)}) %all-reduce.29.cloned.1.call-update) | async-done | bytes 131088 | tf_op jit(solution)/shard_map/psum | solution.py:43
  529.8 22.8 %psum.187 = f32[64,64]{1,0:T(8,128)S(1)} all-reduce(f32[64,64]{1,0:T(8,128)S(1)} %fusion.70), channel_id=1, replica_groups=mesh['org'=8,'dst'=4] {'org'}, use_global_device_ids=true, to_apply=%region_19.0 | all-reduce | flops 4096 | bytes 32768 | tf_op jit(solution)/shard_map/psum | solution.py:52
  552.5 30.3 %all-reduce.31.cloned.1.call-done = f32[64,1024]{1,0:T(8,128)} async-done(((f32[64,1024]{1,0:T(8,128)}), f32[64,1024]{1,0:T(8,128)}) %all-reduce.31.cloned.1.call-update) | async-done | bytes 262160 | tf_op jit(solution)/shard_map/psum | solution.py:51
  584.1 6.0 convolution_bitcast_fusion.6
  592.9 19.2 %psum.189 = f32[64,64]{1,0:T(8,128)S(1)} all-reduce(f32[64,64]{1,0:T(8,128)S(1)} %fusion.71), channel_id=1, replica_groups=mesh['org'=8,'dst'=4] {'dst'}, use_global_device_ids=true, to_apply=%region_21.0 | all-reduce | flops 4096 | bytes 32768 | tf_op jit(solution)/shard_map/psum | solution.py:44
  612.1 14.5 %all-reduce.33.cloned.1.call-done = f32[64,512]{1,0:T(8,128)} async-done(((f32[64,512]{1,0:T(8,128)}), f32[64,512]{1,0:T(8,128)}) %all-reduce.33.cloned.1.call-update) | async-done | bytes 131088 | tf_op jit(solution)/shard_map/psum | solution.py:43
  637.0 22.5 %psum.191 = f32[64,64]{1,0:T(8,128)S(1)} all-reduce(f32[64,64]{1,0:T(8,128)S(1)} %fusion.72), channel_id=1, replica_groups=mesh['org'=8,'dst'=4] {'org'}, use_global_device_ids=true, to_apply=%region_23.0 | all-reduce | flops 4096 | bytes 32768 | tf_op jit(solution)/shard_map/psum | solution.py:52
  659.4 30.6 %all-reduce.35.cloned.1.call-done = f32[64,1024]{1,0:T(8,128)} async-done(((f32[64,1024]{1,0:T(8,128)}), f32[64,1024]{1,0:T(8,128)}) %all-reduce.35.cloned.1.call-update) | async-done | bytes 262160 | tf_op jit(solution)/shard_map/psum | solution.py:51
  (91 shorter events, 93.2 us)
Async XLA Ops:
  7.2 83.4 %all-reduce.13.cloned.1.call-start = ((), (), s32[]{:S(2)}) async-start(), calls=%async_computation | async-start | bytes 262144 | tf_op jit(solution)/shard_map/psum | solution.py:43
  14.8 18.0 %copy-start.3 = (f32[8,64]{1,0:T(8,128)S(1)}, f32[8,64]{1,0:T(8,128)}, u32[]{:S(2)}) copy-start(f32[8,64]{1,0:T(8,128)} %param.9) | copy-start | bytes 6148
  32.9 15.3 %copy-start.1 = (f32[64,1024]{1,0:T(8,128)S(1)}, f32[64,1024]{1,0:T(8,128)}, u32[]{:S(2)}) copy-start(f32[64,1024]{1,0:T(8,128)} %param.8) | copy-start | bytes 786436
  44.9 3.2 copy-start
  48.2 42.5 %copy-start.4 = (f32[64,512]{1,0:T(8,128)S(1)}, f32[64,512]{1,0:T(8,128)}, u32[]{:S(2)}) copy-start(f32[64,512]{1,0:T(8,128)} %param.7) | copy-start | bytes 393220
  53.2 100.8 %all-reduce.15.cloned.1.call-start = ((), (), s32[]{:S(2)}) async-start(), calls=%async_computation.1 | async-start | bytes 524288 | tf_op jit(solution)/shard_map/psum | solution.py:51
  100.6 97.2 %all-reduce.17.cloned.1.call-start = ((), (), s32[]{:S(2)}) async-start(), calls=%async_computation.2 | async-start | bytes 262144 | tf_op jit(solution)/shard_map/psum | solution.py:43
  163.7 97.5 %all-reduce.19.cloned.1.call-start = ((), (), s32[]{:S(2)}) async-start(), calls=%async_computation.3 | async-start | bytes 524288 | tf_op jit(solution)/shard_map/psum | solution.py:51
  207.8 97.2 %all-reduce.21.cloned.1.call-start = ((), (), s32[]{:S(2)}) async-start(), calls=%async_computation.4 | async-start | bytes 262144 | tf_op jit(solution)/shard_map/psum | solution.py:43
  270.9 97.6 %all-reduce.23.cloned.1.call-start = ((), (), s32[]{:S(2)}) async-start(), calls=%async_computation.5 | async-start | bytes 524288 | tf_op jit(solution)/shard_map/psum | solution.py:51
  315.0 97.2 %all-reduce.25.cloned.1.call-start = ((), (), s32[]{:S(2)}) async-start(), calls=%async_computation.6 | async-start | bytes 262144 | tf_op jit(solution)/shard_map/psum | solution.py:43
  378.1 97.5 %all-reduce.27.cloned.1.call-start = ((), (), s32[]{:S(2)}) async-start(), calls=%async_computation.7 | async-start | bytes 524288 | tf_op jit(solution)/shard_map/psum | solution.py:51
  422.3 97.2 %all-reduce.29.cloned.1.call-start = ((), (), s32[]{:S(2)}) async-start(), calls=%async_computation.8 | async-start | bytes 262144 | tf_op jit(solution)/shard_map/psum | solution.py:43
  485.3 97.5 %all-reduce.31.cloned.1.call-start = ((), (), s32[]{:S(2)}) async-start(), calls=%async_computation.9 | async-start | bytes 524288 | tf_op jit(solution)/shard_map/psum | solution.py:51
  529.5 97.2 %all-reduce.33.cloned.1.call-start = ((), (), s32[]{:S(2)}) async-start(), calls=%async_computation.10 | async-start | bytes 262144 | tf_op jit(solution)/shard_map/psum | solution.py:43
  592.5 97.6 %all-reduce.35.cloned.1.call-start = ((), (), s32[]{:S(2)}) async-start(), calls=%async_computation.11 | async-start | bytes 524288 | tf_op jit(solution)/shard_map/psum | solution.py:51
  627.8 64.3 %copy-start.2 = (f32[64,512]{1,0:T(8,128)}, f32[64,512]{1,0:T(8,128)S(1)}, u32[]{:S(2)}) copy-start(f32[64,512]{1,0:T(8,128)S(1)} %convolution_divide_fusion.6) | copy-start | bytes 393220
Sparse Core Ops, SparseCore 0:
  53.3 37.2 all-reduce.12
  100.8 53.1 all-reduce.14
  163.8 33.9 all-reduce.16
  207.9 53.1 all-reduce.18
  271.0 33.9 all-reduce.20
  315.1 53.2 all-reduce.22
  378.2 33.9 all-reduce.24
  422.4 53.1 all-reduce.26
  485.4 33.9 all-reduce.28
  529.6 53.1 all-reduce.30
  592.6 33.9 all-reduce.32
  636.8 53.1 all-reduce.34
where the time goes:
time: 709 us; the launch traced here: 699 us
  waiting for transfers between devices  271 us (38%)
  blocking collectives  252 us (36%)
  matrix products  111 us (16%)
  local copies, waits for them, and re-layouts  37.4 us (5%)
  between operations  15 us (2%)
  other arithmetic  12 us (2%)
    psum x6, waiting for transfers between devices, dest_step(): summed = lax.psum(totals, 'org')  183 us
    psum x6, blocking collectives, dest_step(): gram_part = lax.psum(own_gram, 'org') * hour_gram  136 us
    psum x6, blocking collectives, anchor_step(): gram_part = lax.psum(own_gram, 'dst') * hour_gram  117 us
    psum x6, waiting for transfers between devices, anchor_step(): summed = lax.psum(totals, 'dst')  88.6 us
    dot_general x6, matrix products, anchor_products(): jnp.einsum('rj,hij->hri', dest_now.astype(jnp.bfloat16), tensor, preferre...  32.8 us
    dot_general x6, matrix products, dest_products(): jnp.einsum('ri,hij->hrj', anchor_now.astype(jnp.bfloat16), tensor, prefer...  29.7 us
    mul x2, local copies, waits for them, and re-layouts, dequantize(): values = blocks * scales[:, :, None, :, None]  25.6 us
    dot_general x6, matrix products, dest_products(): jnp.einsum('hrj,hr->rj', per_hour, hour_factor, precision=lax.Precision.H...  18.6 us
  transfers between devices with their start and end apart: 12, of which 12 were waited for; matrix products, arithmetic and copies ran while one was open for 1% of the time, Pallas kernels for 0%

commit v1 on v0

v1 whole, which is shorter than its diff:
```python
import functools

import jax
import jax.numpy as jnp
from jax import lax
from jax.experimental import pallas as pl
from jax.experimental.pallas import tpu as pltpu
from jax.sharding import PartitionSpec as P

SCALE_BLOCK = 128
SWEEPS = 6
LANES = 128
F32 = jnp.float32
BF16 = jnp.bfloat16
HIGHEST = lax.Precision.HIGHEST

WHOLE = pl.BlockSpec(memory_space=pltpu.VMEM)
SCALAR = pl.BlockSpec(memory_space=pltpu.SMEM)
PARAMS = pltpu.CompilerParams(vmem_limit_bytes=12 * 2**20)


def in_vmem(array):
    return pltpu.with_memory_space_constraint(array, pltpu.VMEM)


def gram_rows(rank, width):
    return 8 * -(-(rank // 8) // (width // LANES))


def gram_cells(rank, width):
    per_row = width // LANES
    for block in range(rank // 8):
        yield block, rank + 8 * (block // per_row), LANES * (block % per_row)


def put_gram(message, gram):
    rank = gram.shape[0]
    width = message.shape[1]
    message[rank:, :] = jnp.zeros((message.shape[0] - rank, width), F32)
    for block, row, lane in gram_cells(rank, width):
        message[row : row + 8, lane : lane + rank] = gram[8 * block : 8 * block + 8, :]


def get_gram(message, rank):
    width = message.shape[1]
    return jnp.concatenate(
        [message[row : row + 8, lane : lane + rank] for _, row, lane in gram_cells(rank, width)], axis=0
    )


def own_gram(factor):
    return lax.dot_general(factor, factor, (((1,), (1,)), ((), ())), precision=HIGHEST, preferred_element_type=F32)


def half(ref, core, flip, size):
    start = (1 - core if flip else core) * size
    return pl.ds(pl.multiple_of(start, size), size)


def hour_sum(parts, hour_t):
    total = None
    for hour, part in enumerate(parts):
        term = part * hour_t[:, hour : hour + 1]
        total = term if total is None else total + term
    return total


def first_kernel(counts, scales, dest, hour_t, tensor, flipped, message, buffer, arrived):
    hours, rows, cols = counts.shape
    rank = dest.shape[0]
    dest_low = dest[...].astype(BF16)

    def fetch(hour, slot):
        return pltpu.make_async_copy(counts.at[hour], buffer.at[slot], arrived.at[slot])

    fetch(0, 0).start()
    fetch(1, 1).start()
    message[:rank, :] = jnp.zeros((rank, rows), F32)
    for hour in range(hours):
        slot = hour % 2
        fetch(hour, slot).wait()
        for row_block in range(rows // SCALE_BLOCK):
            row = pl.ds(row_block * SCALE_BLOCK, SCALE_BLOCK)
            for col_block in range(cols // SCALE_BLOCK):
                col = pl.ds(col_block * SCALE_BLOCK, SCALE_BLOCK)
                scale = scales[hour, row_block, col_block]
                block = (buffer[slot, row, col].astype(F32) * scale).astype(BF16)
                tensor[hour, row, col] = block
                flipped[hour, col, row] = block.T
        if hour + 2 < hours:
            fetch(hour + 2, slot).start()
        part = jnp.dot(dest_low, flipped[hour], preferred_element_type=F32)
        message[:rank, :] += part * hour_t[:, hour : hour + 1]
    put_gram(message, own_gram(dest[...]))


def anchor_kernel(core, tensor, anchor, near, far, hour_gram, hour_t, anchor_out, low_out, sent):
    rank, width = anchor.shape
    message = near[...] + far[...]
    gram_part = get_gram(message, rank) * hour_gram[...]
    low = jnp.dot(gram_part, anchor[...], precision=HIGHEST, preferred_element_type=F32)
    updated = anchor[...] * message[:rank, :] / low
    anchor_out[...] = updated
    anchor_low = updated.astype(BF16)
    low_out[...] = anchor_low
    size = tensor.shape[2] // 2
    cols = half(tensor, core[0], True, size)
    sent[:rank, :] = hour_sum(
        [jnp.dot(anchor_low, tensor[h, :, cols], preferred_element_type=F32) for h in range(tensor.shape[0])], hour_t
    )
    put_gram(sent, own_gram(updated))


def anchor_kept_kernel(core, tensor, anchor_low, hour_t, sent, kept):
    rank = anchor_low.shape[0]
    size = tensor.shape[2] // 2
    cols = half(tensor, core[0], False, size)
    low = anchor_low[...]
    kept[:rank, :] = hour_sum(
        [jnp.dot(low, tensor[h, :, cols], preferred_element_type=F32) for h in range(tensor.shape[0])], hour_t
    )
    kept[rank:, :] = sent[rank:, :]


def dest_kernel(dest, near, far, hour_gram, dest_out):
    rank = dest.shape[0]
    message = near[...] + far[...]
    gram_part = get_gram(message, rank) * hour_gram[...]
    low = jnp.dot(gram_part, dest[...], precision=HIGHEST, preferred_element_type=F32)
    dest_out[...] = dest[...] * message[:rank, :] / low


def dest_own_kernel(core, flipped, dest, hour_t, message):
    rank = dest.shape[0]
    size = flipped.shape[1] // 2
    rows = half(flipped, core[0], False, size)
    low = dest[...].astype(BF16)
    message[:rank, :] = hour_sum(
        [jnp.dot(low, flipped[h, rows, :], preferred_element_type=F32) for h in range(flipped.shape[0])], hour_t
    )
    put_gram(message, own_gram(dest[...]))


def dest_other_kernel(core, flipped, dest, hour_t, before, message):
    rank = dest.shape[0]
    size = flipped.shape[1] // 2
    rows = half(flipped, core[0], True, size)
    low = dest[...].astype(BF16)
    message[:rank, :] = before[:rank, :] + hour_sum(
        [jnp.dot(low, flipped[h, rows, :], preferred_element_type=F32) for h in range(flipped.shape[0])], hour_t
    )
    put_gram(message, own_gram(dest[...]))
    message[rank:, :] += before[rank:, :]


def call(kernel, outs, name, flops, *args):
    specs = []
    operands = []
    for arg in args:
        if arg.ndim == 1:
            specs.append(SCALAR)
            operands.append(arg)
        else:
            specs.append(WHOLE)
            operands.append(in_vmem(arg))
    result = pl.pallas_call(
        kernel,
        in_specs=specs,
        out_specs=tuple(WHOLE for _ in outs),
        out_shape=tuple(pltpu.VMEM(shape, dtype) for shape, dtype in outs),
        compiler_params=PARAMS,
        cost_estimate=pl.CostEstimate(flops=flops, bytes_accessed=0, transcendentals=0),
        name=name,
    )(*operands)
    return result if len(outs) > 1 else result[0]


def swap(array, axis, mask):
    size = lax.axis_size(axis)
    return lax.ppermute(array, axis, [(index, index ^ mask) for index in range(size)])


def sum_dest(message):
    size = lax.axis_size("dst")
    mask = 1
    while 2 * mask < size:
        message = message + swap(message, "dst", 2 * mask - 1)
        mask *= 2
    return message, swap(message, "dst", 2 * mask - 1)


def sum_anchor(message):
    size = lax.axis_size("org")
    if size == 8:
        return message + swap(message, "org", 2), swap(message, "org", 4) + swap(message, "org", 6)
    mask = 2
    while 2 * mask < size:
        message = message + swap(message, "org", mask)
        mask *= 2
    return message, swap(message, "org", mask)


def body(counts, block_scales, anchor_factor, dest_factor, hour_factor):
    hours, rows, cols = counts.shape
    rank = anchor_factor.shape[0]
    size = cols // 2
    core = lax.axis_index("org") % 2
    core_arg = core.astype(jnp.int32).reshape(1)
    hour_t = hour_factor.T
    hour_gram = jnp.dot(hour_factor.T, hour_factor, precision=HIGHEST)
    dest_rows = rank + gram_rows(rank, rows)
    anchor_rows = rank + gram_rows(rank, size)
    half_flops = 2 * 4 * hours * rank * rows * size

    tensor, flipped, message = pl.pallas_call(
        first_kernel,
        in_specs=[pl.BlockSpec(memory_space=pl.ANY), SCALAR, WHOLE, WHOLE],
        out_specs=(WHOLE, WHOLE, WHOLE),
        out_shape=(
            pltpu.VMEM((hours, rows, cols), BF16),
            pltpu.VMEM((hours, cols, rows), BF16),
            pltpu.VMEM((dest_rows, rows), F32),
        ),
        scratch_shapes=[pltpu.VMEM((2, rows, cols), jnp.int32), pltpu.SemaphoreType.DMA((2,))],
        compiler_params=PARAMS,
        name="first",
    )(
        pltpu.with_memory_space_constraint(counts, pltpu.HBM),
        block_scales,
        in_vmem(dest_factor),
        in_vmem(hour_t),
    )

    anchor_now = anchor_factor
    dest_own = lax.dynamic_slice_in_dim(dest_factor, core * size, size, 1)
    for sweep in range(SWEEPS):
        near, far = sum_dest(message)
        anchor_now, anchor_low, sent = call(
            anchor_kernel,
            [((rank, rows), F32), ((rank, rows), BF16), ((anchor_rows, size), F32)],
            "anchor", half_flops, core_arg, tensor, anchor_now, near, far, hour_gram, hour_t,
        )
        received = swap(sent, "org", 1)
        kept = call(
            anchor_kept_kernel, [((anchor_rows, size), F32)], "anchor_kept", half_flops,
            core_arg, tensor, anchor_low, hour_t, sent,
        )
        near, far = sum_anchor(kept + received)
        dest_own = call(dest_kernel, [((rank, size), F32)], "dest", 0, dest_own, near, far, hour_gram)
        dest_other = swap(dest_own, "org", 1)
        if sweep + 1 < SWEEPS:
            partial = call(
                dest_own_kernel, [((dest_rows, rows), F32)], "dest_own", half_flops,
                core_arg, flipped, dest_own, hour_t,
            )
            message = call(
                dest_other_kernel, [((dest_rows, rows), F32)], "dest_other", half_flops,
                core_arg, flipped, dest_other, hour_t, partial,
            )
    first = jnp.where(core == 0, dest_own, dest_other)
    second = jnp.where(core == 0, dest_other, dest_own)
    return anchor_now, jnp.concatenate([first, second], axis=1)


def solution(mesh):
    return jax.shard_map(
        body,
        mesh=mesh,
        in_specs=(
            P(None, "org", "dst"),
            P(None, "org", "dst"),
            P(None, "org"),
            P(None, "dst"),
            P(),
        ),
        out_specs=(P(None, "org"), P(None, "dst")),
        check_vma=False,
    )
```

time: 709 us -> 216 us (0.30); the launches traced: 699 us -> 215 us
  blocking collectives: 252 us -> 0 us
  waiting for transfers between devices: 271 us -> 103 us
  matrix products: 111 us -> 0.23 us
  starting transfers between devices: 0.71 us -> 58 us
  Pallas kernels: 0 us -> 34.8 us
  local copies, waits for them, and re-layouts: 37.4 us -> 16.5 us
  between operations: 15 us -> 1.12 us
  other arithmetic: 12 us -> 1.31 us
    psum x12 -> x0, waiting for transfers between devices: 271 us -> none  [the longest x6 183 us: dest_step(): summed = lax.psum(totals, 'org')]
    psum x12 -> x0, blocking collectives: 252 us -> none  [the longest x6 136 us: dest_step(): gram_part = lax.psum(own_gram, 'org') * hour_gram]
    dot_general x49 -> x1, matrix products: 111 us -> 0.23 us  [body(): hour_gram = jnp.dot(hour_factor.T, hour_factor, precision=HIGHEST)]
    ppermute x0 -> x42, waiting for transfers between devices: none -> 103 us  [swap(): lax.ppermute(array, axis, [(index, index ^ mask) for index in range(size)])]
    ppermute x0 -> x42, starting transfers between devices: none -> 58 us  [swap(): lax.ppermute(array, axis, [(index, index ^ mask) for index in range(size)])]
    pallas_call x0 -> x29, Pallas kernels: none -> 34.8 us  [the longest x28 24.3 us: call(): pl.pallas_call(kernel, in_specs=specs, out_specs=tuple((WHOLE for _ in ou...]
    mul x2 -> x0, local copies, waits for them, and re-layouts: 25.6 us -> none  [dequantize(): values = blocks * scales[:, :, None, :, None]]
    unnamed x11 -> x28, local copies, waits for them, and re-layouts: 3.32 us -> 16.5 us
  transfers between devices with their start and end apart: 12 -> 42, of which waited for: 12 -> 38; matrix products, arithmetic and copies ran while one was open for 1% -> 0% of each run, Pallas kernels for 0% -> 5%
where the time goes in v1:
time: 216 us; the launch traced here: 215 us
  waiting for transfers between devices  103 us (48%)
  starting transfers between devices  58 us (27%)
  Pallas kernels  34.8 us (16%)
  local copies, waits for them, and re-layouts  16.5 us (8%)
    ppermute x42, waiting for transfers between devices, swap(): lax.ppermute(array, axis, [(index, index ^ mask) for index in range(size)])  103 us
    ppermute x42, starting transfers between devices, swap(): lax.ppermute(array, axis, [(index, index ^ mask) for index in range(size)])  58 us
    pallas_call x28, Pallas kernels, call(): pl.pallas_call(kernel, in_specs=specs, out_specs=tuple((WHOLE for _ in ou...  24.3 us
    unnamed x28, local copies, waits for them, and re-layouts  16.5 us
    pallas_call x1, Pallas kernels, body(): pl.pallas_call(first_kernel, in_specs=[pl.BlockSpec(memory_space=pl.ANY),...  10.5 us
  transfers between devices with their start and end apart: 42, of which 38 were waited for; matrix products, arithmetic and copies ran while one was open for 0% of the time, Pallas kernels for 5%

profile of v1, /device:TPU:0, one launch (start us, length us, event | category | flops | bytes accessed | tf_op | source)
XLA Modules:
  0.0 215.5 jit_solution(14693002315284647712)
XLA Ops:
  3.1 10.5 %first.1 = (bf16[8,512,1024]{2,1,0:T(8,128)(2,1)S(1)}, bf16[8,1024,512]{2,1,0:T(8,128)(2,1)S(1)}, f32[80,512]{1,0:T(8,128)S(1)}) custom-call(s32[8,512,1024]{2,1,0:T(8,128)} %counts.1, f32[8,4,8]{2,1,0:T(4,128)S(1)} %copy-done.7, f32[64,1024]{1,0:T(8,128)S(1)} %copy-done.4, f32[64,8]{1,0:T(8,128)S(1)} %bitcast.8), custom_call_target="tpu_custom_call" | custom-call | tf_op jit(solution)/shard_map/first/pallas_call | solution.py:215
  13.6 3.3 %copy-done = bf16[8,512,1024]{2,1,0:T(8,128)(2,1)} copy-done((bf16[8,512,1024]{2,1,0:T(8,128)(2,1)}, bf16[8,512,1024]{2,1,0:T(8,128)(2,1)S(1)}, u32[]{:S(2)}) %copy-start) | copy-done | bytes 8388632
  16.9 3.3 %copy-done.2 = bf16[8,1024,512]{2,1,0:T(8,128)(2,1)} copy-done((bf16[8,1024,512]{2,1,0:T(8,128)(2,1)}, bf16[8,1024,512]{2,1,0:T(8,128)(2,1)S(1)}, u32[]{:S(2)}) %copy-start.2) | copy-done | bytes 8388632
  23.2 4.2 %collective-permute-done = f32[80,512]{1,0:T(8,128)S(1)} collective-permute-done((f32[80,512]{1,0:T(8,128)S(1)}, f32[80,512]{1,0:T(8,128)S(1)}, u32[]{:S(2)}, u32[]{:S(2)}) %collective-permute-start) | collective-permute-done | bytes 163872 | tf_op jit(solution)/shard_map/ppermute | solution.py:180
  27.4 3.8 %collective-permute-start.1 = (f32[80,512]{1,0:T(8,128)S(1)}, f32[80,512]{1,0:T(8,128)S(1)}, u32[]{:S(2)}, u32[]{:S(2)}) collective-permute-start(f32[80,512]{1,0:T(8,128)S(1)} %add.80.near), channel_id=1, source_target_pairs={{0,3},{1,2},{2,1},{3,0},{4,7},{5,6},{6,5},{7,4},{8,11},{9,10},{10,... | collective-permute-start | bytes 491528 | tf_op jit(solution)/shard_map/ppermute | solution.py:180
  31.5 3.3 %collective-permute-done.1.far = f32[80,512]{1,0:T(8,128)S(1)} collective-permute-done((f32[80,512]{1,0:T(8,128)S(1)}, f32[80,512]{1,0:T(8,128)S(1)}, u32[]{:S(2)}, u32[]{:S(2)}) %collective-permute-start.1) | collective-permute-done | bytes 163872 | tf_op jit(solution)/shard_map/ppermute | solution.py:180
  34.8 3.4 %copy-done.1 = bf16[8,512,1024]{2,1,0:T(8,128)(2,1)S(1)} copy-done((bf16[8,512,1024]{2,1,0:T(8,128)(2,1)S(1)}, bf16[8,512,1024]{2,1,0:T(8,128)(2,1)}, u32[]{:S(2)}) %copy-start.1) | copy-done | bytes 8388632
  44.4 3.5 %collective-permute-done.3 = f32[80,512]{1,0:T(8,128)S(1)} collective-permute-done((f32[80,512]{1,0:T(8,128)S(1)}, f32[80,512]{1,0:T(8,128)S(1)}, u32[]{:S(2)}, u32[]{:S(2)}) %collective-permute-start.3) | collective-permute-done | bytes 163872 | tf_op jit(solution)/shard_map/ppermute | solution.py:180
  48.0 3.9 %collective-permute-done.4 = f32[80,512]{1,0:T(8,128)S(1)} collective-permute-done((f32[80,512]{1,0:T(8,128)S(1)}, f32[80,512]{1,0:T(8,128)S(1)}, u32[]{:S(2)}, u32[]{:S(2)}) %collective-permute-start.4) | collective-permute-done | bytes 163872 | tf_op jit(solution)/shard_map/ppermute | solution.py:180
  52.4 3.4 %copy-done.3 = bf16[8,1024,512]{2,1,0:T(8,128)(2,1)S(1)} copy-done((bf16[8,1024,512]{2,1,0:T(8,128)(2,1)S(1)}, bf16[8,1024,512]{2,1,0:T(8,128)(2,1)}, u32[]{:S(2)}) %copy-start.3) | copy-done | bytes 8388632
  57.7 3.0 %collective-permute-start.7 = (f32[80,512]{1,0:T(8,128)S(1)}, f32[80,512]{1,0:T(8,128)S(1)}, u32[]{:S(2)}, u32[]{:S(2)}) collective-permute-start(f32[80,512]{1,0:T(8,128)S(1)} %dest_other.5), channel_id=1, source_target_pairs={{0,1},{1,0},{2,3},{3,2},{4,5},{5,4},{6,7},{7,6},{8,9},{9,8},{10,11... | collective-permute-start | bytes 491528 | tf_op jit(solution)/shard_map/ppermute | solution.py:180
  60.7 4.9 %collective-permute-done.7 = f32[80,512]{1,0:T(8,128)S(1)} collective-permute-done((f32[80,512]{1,0:T(8,128)S(1)}, f32[80,512]{1,0:T(8,128)S(1)}, u32[]{:S(2)}, u32[]{:S(2)}) %collective-permute-start.7) | collective-permute-done | bytes 163872 | tf_op jit(solution)/shard_map/ppermute | solution.py:180
  68.3 5.3 %collective-permute-done.8.far = f32[80,512]{1,0:T(8,128)S(1)} collective-permute-done((f32[80,512]{1,0:T(8,128)S(1)}, f32[80,512]{1,0:T(8,128)S(1)}, u32[]{:S(2)}, u32[]{:S(2)}) %collective-permute-start.8) | collective-permute-done | bytes 163872 | tf_op jit(solution)/shard_map/ppermute | solution.py:180
  79.9 3.6 %collective-permute-done.10 = f32[80,512]{1,0:T(8,128)S(1)} collective-permute-done((f32[80,512]{1,0:T(8,128)S(1)}, f32[80,512]{1,0:T(8,128)S(1)}, u32[]{:S(2)}, u32[]{:S(2)}) %collective-permute-start.10) | collective-permute-done | bytes 163872 | tf_op jit(solution)/shard_map/ppermute | solution.py:180
  89.9 3.2 %collective-permute-start.14 = (f32[80,512]{1,0:T(8,128)S(1)}, f32[80,512]{1,0:T(8,128)S(1)}, u32[]{:S(2)}, u32[]{:S(2)}) collective-permute-start(f32[80,512]{1,0:T(8,128)S(1)} %dest_other.6), channel_id=1, source_target_pairs={{0,1},{1,0},{2,3},{3,2},{4,5},{5,4},{6,7},{7,6},{8,9},{9,8},{10,11... | collective-permute-start | bytes 491528 | tf_op jit(solution)/shard_map/ppermute | solution.py:180
  93.1 4.5 %collective-permute-done.14 = f32[80,512]{1,0:T(8,128)S(1)} collective-permute-done((f32[80,512]{1,0:T(8,128)S(1)}, f32[80,512]{1,0:T(8,128)S(1)}, u32[]{:S(2)}, u32[]{:S(2)}) %collective-permute-start.14) | collective-permute-done | bytes 163872 | tf_op jit(solution)/shard_map/ppermute | solution.py:180
  100.3 5.1 %collective-permute-done.15.far = f32[80,512]{1,0:T(8,128)S(1)} collective-permute-done((f32[80,512]{1,0:T(8,128)S(1)}, f32[80,512]{1,0:T(8,128)S(1)}, u32[]{:S(2)}, u32[]{:S(2)}) %collective-permute-start.15) | collective-permute-done | bytes 163872 | tf_op jit(solution)/shard_map/ppermute | solution.py:180
  111.8 3.6 %collective-permute-done.17 = f32[80,512]{1,0:T(8,128)S(1)} collective-permute-done((f32[80,512]{1,0:T(8,128)S(1)}, f32[80,512]{1,0:T(8,128)S(1)}, u32[]{:S(2)}, u32[]{:S(2)}) %collective-permute-start.17) | collective-permute-done | bytes 163872 | tf_op jit(solution)/shard_map/ppermute | solution.py:180
  115.4 3.2 %collective-permute-done.18 = f32[80,512]{1,0:T(8,128)S(1)} collective-permute-done((f32[80,512]{1,0:T(8,128)S(1)}, f32[80,512]{1,0:T(8,128)S(1)}, u32[]{:S(2)}, u32[]{:S(2)}) %collective-permute-start.18) | collective-permute-done | bytes 163872 | tf_op jit(solution)/shard_map/ppermute | solution.py:180
  121.4 3.1 %collective-permute-start.21 = (f32[80,512]{1,0:T(8,128)S(1)}, f32[80,512]{1,0:T(8,128)S(1)}, u32[]{:S(2)}, u32[]{:S(2)}) collective-permute-start(f32[80,512]{1,0:T(8,128)S(1)} %dest_other.7), channel_id=1, source_target_pairs={{0,1},{1,0},{2,3},{3,2},{4,5},{5,4},{6,7},{7,6},{8,9},{9,8},{10,11... | collective-permute-start | bytes 491528 | tf_op jit(solution)/shard_map/ppermute | solution.py:180
  124.5 4.5 %collective-permute-done.21 = f32[80,512]{1,0:T(8,128)S(1)} collective-permute-done((f32[80,512]{1,0:T(8,128)S(1)}, f32[80,512]{1,0:T(8,128)S(1)}, u32[]{:S(2)}, u32[]{:S(2)}) %collective-permute-start.21) | collective-permute-done | bytes 163872 | tf_op jit(solution)/shard_map/ppermute | solution.py:180
  131.7 5.0 %collective-permute-done.22.far = f32[80,512]{1,0:T(8,128)S(1)} collective-permute-done((f32[80,512]{1,0:T(8,128)S(1)}, f32[80,512]{1,0:T(8,128)S(1)}, u32[]{:S(2)}, u32[]{:S(2)}) %collective-permute-start.22) | collective-permute-done | bytes 163872 | tf_op jit(solution)/shard_map/ppermute | solution.py:180
  143.0 3.6 %collective-permute-done.24 = f32[80,512]{1,0:T(8,128)S(1)} collective-permute-done((f32[80,512]{1,0:T(8,128)S(1)}, f32[80,512]{1,0:T(8,128)S(1)}, u32[]{:S(2)}, u32[]{:S(2)}) %collective-permute-start.24) | collective-permute-done | bytes 163872 | tf_op jit(solution)/shard_map/ppermute | solution.py:180
  153.0 3.1 %collective-permute-start.28 = (f32[80,512]{1,0:T(8,128)S(1)}, f32[80,512]{1,0:T(8,128)S(1)}, u32[]{:S(2)}, u32[]{:S(2)}) collective-permute-start(f32[80,512]{1,0:T(8,128)S(1)} %dest_other.8), channel_id=1, source_target_pairs={{0,1},{1,0},{2,3},{3,2},{4,5},{5,4},{6,7},{7,6},{8,9},{9,8},{10,11... | collective-permute-start | bytes 491528 | tf_op jit(solution)/shard_map/ppermute | solution.py:180
  156.1 4.5 %collective-permute-done.28 = f32[80,512]{1,0:T(8,128)S(1)} collective-permute-done((f32[80,512]{1,0:T(8,128)S(1)}, f32[80,512]{1,0:T(8,128)S(1)}, u32[]{:S(2)}, u32[]{:S(2)}) %collective-permute-start.28) | collective-permute-done | bytes 163872 | tf_op jit(solution)/shard_map/ppermute | solution.py:180
  163.3 5.0 %collective-permute-done.29.far = f32[80,512]{1,0:T(8,128)S(1)} collective-permute-done((f32[80,512]{1,0:T(8,128)S(1)}, f32[80,512]{1,0:T(8,128)S(1)}, u32[]{:S(2)}, u32[]{:S(2)}) %collective-permute-start.29) | collective-permute-done | bytes 163872 | tf_op jit(solution)/shard_map/ppermute | solution.py:180
  174.6 3.6 %collective-permute-done.31 = f32[80,512]{1,0:T(8,128)S(1)} collective-permute-done((f32[80,512]{1,0:T(8,128)S(1)}, f32[80,512]{1,0:T(8,128)S(1)}, u32[]{:S(2)}, u32[]{:S(2)}) %collective-permute-start.31) | collective-permute-done | bytes 163872 | tf_op jit(solution)/shard_map/ppermute | solution.py:180
  178.2 3.2 %collective-permute-done.32 = f32[80,512]{1,0:T(8,128)S(1)} collective-permute-done((f32[80,512]{1,0:T(8,128)S(1)}, f32[80,512]{1,0:T(8,128)S(1)}, u32[]{:S(2)}, u32[]{:S(2)}) %collective-permute-start.32) | collective-permute-done | bytes 163872 | tf_op jit(solution)/shard_map/ppermute | solution.py:180
  184.1 3.1 %collective-permute-start.35 = (f32[80,512]{1,0:T(8,128)S(1)}, f32[80,512]{1,0:T(8,128)S(1)}, u32[]{:S(2)}, u32[]{:S(2)}) collective-permute-start(f32[80,512]{1,0:T(8,128)S(1)} %dest_other.9), channel_id=1, source_target_pairs={{0,1},{1,0},{2,3},{3,2},{4,5},{5,4},{6,7},{7,6},{8,9},{9,8},{10,11... | collective-permute-start | bytes 491528 | tf_op jit(solution)/shard_map/ppermute | solution.py:180
  187.2 4.5 %collective-permute-done.35 = f32[80,512]{1,0:T(8,128)S(1)} collective-permute-done((f32[80,512]{1,0:T(8,128)S(1)}, f32[80,512]{1,0:T(8,128)S(1)}, u32[]{:S(2)}, u32[]{:S(2)}) %collective-permute-start.35) | collective-permute-done | bytes 163872 | tf_op jit(solution)/shard_map/ppermute | solution.py:180
  194.5 5.0 %collective-permute-done.36.far = f32[80,512]{1,0:T(8,128)S(1)} collective-permute-done((f32[80,512]{1,0:T(8,128)S(1)}, f32[80,512]{1,0:T(8,128)S(1)}, u32[]{:S(2)}, u32[]{:S(2)}) %collective-permute-start.36) | collective-permute-done | bytes 163872 | tf_op jit(solution)/shard_map/ppermute | solution.py:180
  205.8 3.6 %collective-permute-done.38 = f32[80,512]{1,0:T(8,128)S(1)} collective-permute-done((f32[80,512]{1,0:T(8,128)S(1)}, f32[80,512]{1,0:T(8,128)S(1)}, u32[]{:S(2)}, u32[]{:S(2)}) %collective-permute-start.38) | collective-permute-done | bytes 163872 | tf_op jit(solution)/shard_map/ppermute | solution.py:180
  (139 shorter events, 83.6 us)
Async XLA Ops:
  20.2 7.2 %collective-permute-start = (f32[80,512]{1,0:T(8,128)S(1)}, f32[80,512]{1,0:T(8,128)S(1)}, u32[]{:S(2)}, u32[]{:S(2)}) collective-permute-start(f32[80,512]{1,0:T(8,128)S(1)} %get-tuple-element.24), channel_id=1, source_target_pairs={{0,1},{1,0},{2,3},{3,2},{4,5},{5,4},{6,7},{7,6},{8,9},{9,8},{10,11... | collective-permute-start | bytes 491528 | tf_op jit(solution)/shard_map/ppermute | solution.py:180
  27.4 7.4 %collective-permute-start.1 = (f32[80,512]{1,0:T(8,128)S(1)}, f32[80,512]{1,0:T(8,128)S(1)}, u32[]{:S(2)}, u32[]{:S(2)}) collective-permute-start(f32[80,512]{1,0:T(8,128)S(1)} %add.80.near), channel_id=1, source_target_pairs={{0,3},{1,2},{2,1},{3,0},{4,7},{5,6},{6,5},{7,4},{8,11},{9,10},{10,... | collective-permute-start | bytes 491528 | tf_op jit(solution)/shard_map/ppermute | solution.py:180
  40.9 7.1 %collective-permute-start.3 = (f32[80,512]{1,0:T(8,128)S(1)}, f32[80,512]{1,0:T(8,128)S(1)}, u32[]{:S(2)}, u32[]{:S(2)}) collective-permute-start(f32[80,512]{1,0:T(8,128)S(1)} %add.82), channel_id=1, source_target_pairs={{0,8},{4,12},{8,0},{12,4},{16,24},{20,28},{24,16},{28,20},{1,9},{5... | collective-permute-start | bytes 491528 | tf_op jit(solution)/shard_map/ppermute | solution.py:180
  42.5 9.5 %collective-permute-start.4 = (f32[80,512]{1,0:T(8,128)S(1)}, f32[80,512]{1,0:T(8,128)S(1)}, u32[]{:S(2)}, u32[]{:S(2)}) collective-permute-start(f32[80,512]{1,0:T(8,128)S(1)} %add.82), channel_id=1, source_target_pairs={{0,16},{4,20},{8,24},{12,28},{16,0},{20,4},{24,8},{28,12},{1,17},{... | collective-permute-start | bytes 491528 | tf_op jit(solution)/shard_map/ppermute | solution.py:180
  44.0 8.0 %collective-permute-start.5 = (f32[80,512]{1,0:T(8,128)S(1)}, f32[80,512]{1,0:T(8,128)S(1)}, u32[]{:S(2)}, u32[]{:S(2)}) collective-permute-start(f32[80,512]{1,0:T(8,128)S(1)} %add.82), channel_id=1, source_target_pairs={{0,24},{4,28},{8,16},{12,20},{16,8},{20,12},{24,0},{28,4},{1,25},{... | collective-permute-start | bytes 491528 | tf_op jit(solution)/shard_map/ppermute | solution.py:180
  52.3 4.4 %collective-permute-start.6 = (f32[64,512]{1,0:T(8,128)S(1)}, f32[64,512]{1,0:T(8,128)S(1)}, u32[]{:S(2)}, u32[]{:S(2)}) collective-permute-start(f32[64,512]{1,0:T(8,128)S(1)} %dest.8), channel_id=1, source_target_pairs={{0,4},{4,0},{8,12},{12,8},{16,20},{20,16},{24,28},{28,24},{1,5},{5... | collective-permute-start | bytes 393224 | tf_op jit(solution)/shard_map/ppermute | solution.py:180
  57.7 7.9 %collective-permute-start.7 = (f32[80,512]{1,0:T(8,128)S(1)}, f32[80,512]{1,0:T(8,128)S(1)}, u32[]{:S(2)}, u32[]{:S(2)}) collective-permute-start(f32[80,512]{1,0:T(8,128)S(1)} %dest_other.5), channel_id=1, source_target_pairs={{0,1},{1,0},{2,3},{3,2},{4,5},{5,4},{6,7},{7,6},{8,9},{9,8},{10,11... | collective-permute-start | bytes 491528 | tf_op jit(solution)/shard_map/ppermute | solution.py:180
  65.6 8.0 %collective-permute-start.8 = (f32[80,512]{1,0:T(8,128)S(1)}, f32[80,512]{1,0:T(8,128)S(1)}, u32[]{:S(2)}, u32[]{:S(2)}) collective-permute-start(f32[80,512]{1,0:T(8,128)S(1)} %add.85.near), channel_id=1, source_target_pairs={{0,3},{1,2},{2,1},{3,0},{4,7},{5,6},{6,5},{7,4},{8,11},{9,10},{10,... | collective-permute-start | bytes 491528 | tf_op jit(solution)/shard_map/ppermute | solution.py:180
  76.4 7.1 %collective-permute-start.10 = (f32[80,512]{1,0:T(8,128)S(1)}, f32[80,512]{1,0:T(8,128)S(1)}, u32[]{:S(2)}, u32[]{:S(2)}) collective-permute-start(f32[80,512]{1,0:T(8,128)S(1)} %add.86), channel_id=1, source_target_pairs={{0,8},{4,12},{8,0},{12,4},{16,24},{20,28},{24,16},{28,20},{1,9},{5... | collective-permute-start | bytes 491528 | tf_op jit(solution)/shard_map/ppermute | solution.py:180
  77.7 7.8 %collective-permute-start.11 = (f32[80,512]{1,0:T(8,128)S(1)}, f32[80,512]{1,0:T(8,128)S(1)}, u32[]{:S(2)}, u32[]{:S(2)}) collective-permute-start(f32[80,512]{1,0:T(8,128)S(1)} %add.86), channel_id=1, source_target_pairs={{0,16},{4,20},{8,24},{12,28},{16,0},{20,4},{24,8},{28,12},{1,17},{... | collective-permute-start | bytes 491528 | tf_op jit(solution)/shard_map/ppermute | solution.py:180
  78.5 8.7 %collective-permute-start.12 = (f32[80,512]{1,0:T(8,128)S(1)}, f32[80,512]{1,0:T(8,128)S(1)}, u32[]{:S(2)}, u32[]{:S(2)}) collective-permute-start(f32[80,512]{1,0:T(8,128)S(1)} %add.86), channel_id=1, source_target_pairs={{0,24},{4,28},{8,16},{12,20},{16,8},{20,12},{24,0},{28,4},{1,25},{... | collective-permute-start | bytes 491528 | tf_op jit(solution)/shard_map/ppermute | solution.py:180
  89.9 7.7 %collective-permute-start.14 = (f32[80,512]{1,0:T(8,128)S(1)}, f32[80,512]{1,0:T(8,128)S(1)}, u32[]{:S(2)}, u32[]{:S(2)}) collective-permute-start(f32[80,512]{1,0:T(8,128)S(1)} %dest_other.6), channel_id=1, source_target_pairs={{0,1},{1,0},{2,3},{3,2},{4,5},{5,4},{6,7},{7,6},{8,9},{9,8},{10,11... | collective-permute-start | bytes 491528 | tf_op jit(solution)/shard_map/ppermute | solution.py:180
  97.6 7.7 %collective-permute-start.15 = (f32[80,512]{1,0:T(8,128)S(1)}, f32[80,512]{1,0:T(8,128)S(1)}, u32[]{:S(2)}, u32[]{:S(2)}) collective-permute-start(f32[80,512]{1,0:T(8,128)S(1)} %add.89.near), channel_id=1, source_target_pairs={{0,3},{1,2},{2,1},{3,0},{4,7},{5,6},{6,5},{7,4},{8,11},{9,10},{10,... | collective-permute-start | bytes 491528 | tf_op jit(solution)/shard_map/ppermute | solution.py:180
  108.3 7.1 %collective-permute-start.17 = (f32[80,512]{1,0:T(8,128)S(1)}, f32[80,512]{1,0:T(8,128)S(1)}, u32[]{:S(2)}, u32[]{:S(2)}) collective-permute-start(f32[80,512]{1,0:T(8,128)S(1)} %add.90), channel_id=1, source_target_pairs={{0,8},{4,12},{8,0},{12,4},{16,24},{20,28},{24,16},{28,20},{1,9},{5... | collective-permute-start | bytes 491528 | tf_op jit(solution)/shard_map/ppermute | solution.py:180
  109.1 9.5 %collective-permute-start.18 = (f32[80,512]{1,0:T(8,128)S(1)}, f32[80,512]{1,0:T(8,128)S(1)}, u32[]{:S(2)}, u32[]{:S(2)}) collective-permute-start(f32[80,512]{1,0:T(8,128)S(1)} %add.90), channel_id=1, source_target_pairs={{0,16},{4,20},{8,24},{12,28},{16,0},{20,4},{24,8},{28,12},{1,17},{... | collective-permute-start | bytes 491528 | tf_op jit(solution)/shard_map/ppermute | solution.py:180
  110.6 8.0 %collective-permute-start.19 = (f32[80,512]{1,0:T(8,128)S(1)}, f32[80,512]{1,0:T(8,128)S(1)}, u32[]{:S(2)}, u32[]{:S(2)}) collective-permute-start(f32[80,512]{1,0:T(8,128)S(1)} %add.90), channel_id=1, source_target_pairs={{0,24},{4,28},{8,16},{12,20},{16,8},{20,12},{24,0},{28,4},{1,25},{... | collective-permute-start | bytes 491528 | tf_op jit(solution)/shard_map/ppermute | solution.py:180
  121.4 7.6 %collective-permute-start.21 = (f32[80,512]{1,0:T(8,128)S(1)}, f32[80,512]{1,0:T(8,128)S(1)}, u32[]{:S(2)}, u32[]{:S(2)}) collective-permute-start(f32[80,512]{1,0:T(8,128)S(1)} %dest_other.7), channel_id=1, source_target_pairs={{0,1},{1,0},{2,3},{3,2},{4,5},{5,4},{6,7},{7,6},{8,9},{9,8},{10,11... | collective-permute-start | bytes 491528 | tf_op jit(solution)/shard_map/ppermute | solution.py:180
  129.0 7.7 %collective-permute-start.22 = (f32[80,512]{1,0:T(8,128)S(1)}, f32[80,512]{1,0:T(8,128)S(1)}, u32[]{:S(2)}, u32[]{:S(2)}) collective-permute-start(f32[80,512]{1,0:T(8,128)S(1)} %add.93.near), channel_id=1, source_target_pairs={{0,3},{1,2},{2,1},{3,0},{4,7},{5,6},{6,5},{7,4},{8,11},{9,10},{10,... | collective-permute-start | bytes 491528 | tf_op jit(solution)/shard_map/ppermute | solution.py:180
  138.0 1.5 collective-permute-start.23
  139.5 7.1 %collective-permute-start.24 = (f32[80,512]{1,0:T(8,128)S(1)}, f32[80,512]{1,0:T(8,128)S(1)}, u32[]{:S(2)}, u32[]{:S(2)}) collective-permute-start(f32[80,512]{1,0:T(8,128)S(1)} %add.94), channel_id=1, source_target_pairs={{0,8},{4,12},{8,0},{12,4},{16,24},{20,28},{24,16},{28,20},{1,9},{5... | collective-permute-start | bytes 491528 | tf_op jit(solution)/shard_map/ppermute | solution.py:180
  140.7 7.8 %collective-permute-start.25 = (f32[80,512]{1,0:T(8,128)S(1)}, f32[80,512]{1,0:T(8,128)S(1)}, u32[]{:S(2)}, u32[]{:S(2)}) collective-permute-start(f32[80,512]{1,0:T(8,128)S(1)} %add.94), channel_id=1, source_target_pairs={{0,16},{4,20},{8,24},{12,28},{16,0},{20,4},{24,8},{28,12},{1,17},{... | collective-permute-start | bytes 491528 | tf_op jit(solution)/shard_map/ppermute | solution.py:180
  141.6 8.7 %collective-permute-start.26 = (f32[80,512]{1,0:T(8,128)S(1)}, f32[80,512]{1,0:T(8,128)S(1)}, u32[]{:S(2)}, u32[]{:S(2)}) collective-permute-start(f32[80,512]{1,0:T(8,128)S(1)} %add.94), channel_id=1, source_target_pairs={{0,24},{4,28},{8,16},{12,20},{16,8},{20,12},{24,0},{28,4},{1,25},{... | collective-permute-start | bytes 491528 | tf_op jit(solution)/shard_map/ppermute | solution.py:180
  153.0 7.6 %collective-permute-start.28 = (f32[80,512]{1,0:T(8,128)S(1)}, f32[80,512]{1,0:T(8,128)S(1)}, u32[]{:S(2)}, u32[]{:S(2)}) collective-permute-start(f32[80,512]{1,0:T(8,128)S(1)} %dest_other.8), channel_id=1, source_target_pairs={{0,1},{1,0},{2,3},{3,2},{4,5},{5,4},{6,7},{7,6},{8,9},{9,8},{10,11... | collective-permute-start | bytes 491528 | tf_op jit(solution)/shard_map/ppermute | solution.py:180
  160.6 7.7 %collective-permute-start.29 = (f32[80,512]{1,0:T(8,128)S(1)}, f32[80,512]{1,0:T(8,128)S(1)}, u32[]{:S(2)}, u32[]{:S(2)}) collective-permute-start(f32[80,512]{1,0:T(8,128)S(1)} %add.97.near), channel_id=1, source_target_pairs={{0,3},{1,2},{2,1},{3,0},{4,7},{5,6},{6,5},{7,4},{8,11},{9,10},{10,... | collective-permute-start | bytes 491528 | tf_op jit(solution)/shard_map/ppermute | solution.py:180
  171.1 7.1 %collective-permute-start.31 = (f32[80,512]{1,0:T(8,128)S(1)}, f32[80,512]{1,0:T(8,128)S(1)}, u32[]{:S(2)}, u32[]{:S(2)}) collective-permute-start(f32[80,512]{1,0:T(8,128)S(1)} %add.98), channel_id=1, source_target_pairs={{0,8},{4,12},{8,0},{12,4},{16,24},{20,28},{24,16},{28,20},{1,9},{5... | collective-permute-start | bytes 491528 | tf_op jit(solution)/shard_map/ppermute | solution.py:180
  171.9 9.5 %collective-permute-start.32 = (f32[80,512]{1,0:T(8,128)S(1)}, f32[80,512]{1,0:T(8,128)S(1)}, u32[]{:S(2)}, u32[]{:S(2)}) collective-permute-start(f32[80,512]{1,0:T(8,128)S(1)} %add.98), channel_id=1, source_target_pairs={{0,16},{4,20},{8,24},{12,28},{16,0},{20,4},{24,8},{28,12},{1,17},{... | collective-permute-start | bytes 491528 | tf_op jit(solution)/shard_map/ppermute | solution.py:180
  173.4 8.0 %collective-permute-start.33 = (f32[80,512]{1,0:T(8,128)S(1)}, f32[80,512]{1,0:T(8,128)S(1)}, u32[]{:S(2)}, u32[]{:S(2)}) collective-permute-start(f32[80,512]{1,0:T(8,128)S(1)} %add.98), channel_id=1, source_target_pairs={{0,24},{4,28},{8,16},{12,20},{16,8},{20,12},{24,0},{28,4},{1,25},{... | collective-permute-start | bytes 491528 | tf_op jit(solution)/shard_map/ppermute | solution.py:180
  184.1 7.6 %collective-permute-start.35 = (f32[80,512]{1,0:T(8,128)S(1)}, f32[80,512]{1,0:T(8,128)S(1)}, u32[]{:S(2)}, u32[]{:S(2)}) collective-permute-start(f32[80,512]{1,0:T(8,128)S(1)} %dest_other.9), channel_id=1, source_target_pairs={{0,1},{1,0},{2,3},{3,2},{4,5},{5,4},{6,7},{7,6},{8,9},{9,8},{10,11... | collective-permute-start | bytes 491528 | tf_op jit(solution)/shard_map/ppermute | solution.py:180
  191.8 7.7 %collective-permute-start.36 = (f32[80,512]{1,0:T(8,128)S(1)}, f32[80,512]{1,0:T(8,128)S(1)}, u32[]{:S(2)}, u32[]{:S(2)}) collective-permute-start(f32[80,512]{1,0:T(8,128)S(1)} %add.101.near), channel_id=1, source_target_pairs={{0,3},{1,2},{2,1},{3,0},{4,7},{5,6},{6,5},{7,4},{8,11},{9,10},{10,... | collective-permute-start | bytes 491528 | tf_op jit(solution)/shard_map/ppermute | solution.py:180
  202.2 7.1 %collective-permute-start.38 = (f32[80,512]{1,0:T(8,128)S(1)}, f32[80,512]{1,0:T(8,128)S(1)}, u32[]{:S(2)}, u32[]{:S(2)}) collective-permute-start(f32[80,512]{1,0:T(8,128)S(1)} %add.102), channel_id=1, source_target_pairs={{0,8},{4,12},{8,0},{12,4},{16,24},{20,28},{24,16},{28,20},{1,9},{5... | collective-permute-start | bytes 491528 | tf_op jit(solution)/shard_map/ppermute | solution.py:180
  203.5 7.9 %collective-permute-start.39 = (f32[80,512]{1,0:T(8,128)S(1)}, f32[80,512]{1,0:T(8,128)S(1)}, u32[]{:S(2)}, u32[]{:S(2)}) collective-permute-start(f32[80,512]{1,0:T(8,128)S(1)} %add.102), channel_id=1, source_target_pairs={{0,16},{4,20},{8,24},{12,28},{16,0},{20,4},{24,8},{28,12},{1,17},{... | collective-permute-start | bytes 491528 | tf_op jit(solution)/shard_map/ppermute | solution.py:180
  204.3 8.7 %collective-permute-start.40 = (f32[80,512]{1,0:T(8,128)S(1)}, f32[80,512]{1,0:T(8,128)S(1)}, u32[]{:S(2)}, u32[]{:S(2)}) collective-permute-start(f32[80,512]{1,0:T(8,128)S(1)} %add.102), channel_id=1, source_target_pairs={{0,24},{4,28},{8,16},{12,20},{16,8},{20,12},{24,0},{28,4},{1,25},{... | collective-permute-start | bytes 491528 | tf_op jit(solution)/shard_map/ppermute | solution.py:180
  (23 other events, 156.9 us)

commit v2 on v1

v2 whole, which is shorter than its diff:
```python
import functools

import jax
import jax.numpy as jnp
from jax import lax
from jax.experimental import pallas as pl
from jax.experimental.pallas import tpu as pltpu
from jax.sharding import PartitionSpec as P

SCALE_BLOCK = 128
SWEEPS = 6
F32 = jnp.float32
BF16 = jnp.bfloat16
HIGHEST = lax.Precision.HIGHEST

WHOLE = pl.BlockSpec(memory_space=pltpu.VMEM)
PARAMS = pltpu.CompilerParams(vmem_limit_bytes=8 * 2**20)


def in_vmem(array):
    return pltpu.with_memory_space_constraint(array, pltpu.VMEM)


def gram_rows(rank, width):
    return 8 * -(-(rank // 8) // (width // rank))


def gram_cells(rank, width):
    per_row = width // rank
    for block in range(rank // 8):
        yield block, rank + 8 * (block // per_row), rank * (block % per_row)


def put_gram(message, gram):
    rank = gram.shape[0]
    width = message.shape[1]
    message[rank:, :] = jnp.zeros((message.shape[0] - rank, width), F32)
    for block, row, lane in gram_cells(rank, width):
        message[row : row + 8, lane : lane + rank] = gram[8 * block : 8 * block + 8, :]


def get_gram(message, rank):
    width = message.shape[1]
    return jnp.concatenate(
        [message[row : row + 8, lane : lane + rank] for _, row, lane in gram_cells(rank, width)], axis=0
    )


def own_gram(factor):
    return lax.dot_general(factor, factor, (((1,), (1,)), ((), ())), precision=HIGHEST, preferred_element_type=F32)


def half(flip, size):
    core = lax.axis_index("org") % 2
    start = (1 - core if flip else core) * size
    return pl.ds(pl.multiple_of(start, size), size)


def hour_sum(parts, hour_t):
    total = None
    for hour, part in enumerate(parts):
        term = part * hour_t[:, hour : hour + 1]
        total = term if total is None else total + term
    return total


def first_kernel(
    counts, scales, dest, hour, tensor, message, dest_own, hour_gram, hour_t,
    buffer, scale_now, dest_now, hour_now, arrived, small_arrived,
):
    hours, rows, cols = counts.shape
    small = [
        pltpu.make_async_copy(source, target, small_arrived.at[index])
        for index, (source, target) in enumerate(((scales, scale_now), (dest, dest_now), (hour, hour_now)))
    ]
    for copy in small:
        copy.start()
    large = [pltpu.make_async_copy(counts.at[h], buffer.at[h], arrived.at[h]) for h in range(hours)]
    for copy in large:
        copy.start()
    for copy in small:
        copy.wait()
    hour_t[...] = hour_now[...].T
    hour_gram[...] = own_gram(hour_t[...])
    dest_own[...] = dest_now[:, half(False, cols // 2)]
    dest_low = dest_now[...].astype(BF16)
    put_gram(message, own_gram(dest_now[...]))
    total = None
    for h in range(hours):
        large[h].wait()
        for row_block in range(rows // SCALE_BLOCK):
            row = pl.ds(row_block * SCALE_BLOCK, SCALE_BLOCK)
            for col_block in range(cols // SCALE_BLOCK):
                col = pl.ds(col_block * SCALE_BLOCK, SCALE_BLOCK)
                scale = scale_now[h, row_block, col_block]
                tensor[h, row, col] = (buffer[h, row, col].astype(F32) * scale).astype(BF16)
        part = lax.dot_general(dest_low, tensor[h], (((1,), (1,)), ((), ())), preferred_element_type=F32)
        part = part * hour_t[:, h : h + 1]
        total = part if total is None else total + part
    message[: total.shape[0], :] = total


def flip_kernel(tensor, after, flipped):
    for h in range(tensor.shape[0]):
        flipped[h] = tensor[h].T


def join_kernel(own, other, joined):
    size = own.shape[1]
    joined[:, half(False, size)] = own[...]
    joined[:, half(True, size)] = other[...]


def anchor_kernel(tensor, anchor, near, far, hour_gram, hour_t, _, anchor_out, low_out, sent):
    rank, width = anchor.shape
    message = near[...] + far[...]
    gram_part = get_gram(message, rank) * hour_gram[...]
    low = jnp.dot(gram_part, anchor[...], precision=HIGHEST, preferred_element_type=F32)
    updated = anchor[...] * message[:rank, :] / low
    anchor_out[...] = updated
    anchor_low = updated.astype(BF16)
    low_out[...] = anchor_low
    size = tensor.shape[2] // 2
    cols = half(True, size)
    sent[:rank, :] = hour_sum(
        [jnp.dot(anchor_low, tensor[h, :, cols], preferred_element_type=F32) for h in range(tensor.shape[0])], hour_t
    )
    put_gram(sent, own_gram(updated))


def anchor_kept_kernel(tensor, anchor_low, hour_t, sent, kept):
    rank = anchor_low.shape[0]
    size = tensor.shape[2] // 2
    cols = half(False, size)
    low = anchor_low[...]
    kept[:rank, :] = hour_sum(
        [jnp.dot(low, tensor[h, :, cols], preferred_element_type=F32) for h in range(tensor.shape[0])], hour_t
    )
    kept[rank:, :] = sent[rank:, :]


def dest_kernel(dest, near, far, hour_gram, dest_out):
    rank = dest.shape[0]
    message = near[...] + far[...]
    gram_part = get_gram(message, rank) * hour_gram[...]
    low = jnp.dot(gram_part, dest[...], precision=HIGHEST, preferred_element_type=F32)
    dest_out[...] = dest[...] * message[:rank, :] / low


def dest_own_kernel(flipped, dest, hour_t, message):
    rank = dest.shape[0]
    size = flipped.shape[1] // 2
    rows = half(False, size)
    low = dest[...].astype(BF16)
    message[:rank, :] = hour_sum(
        [jnp.dot(low, flipped[h, rows, :], preferred_element_type=F32) for h in range(flipped.shape[0])], hour_t
    )
    put_gram(message, own_gram(dest[...]))


def dest_other_kernel(flipped, dest, hour_t, before, message):
    rank = dest.shape[0]
    size = flipped.shape[1] // 2
    rows = half(True, size)
    low = dest[...].astype(BF16)
    message[:rank, :] = before[:rank, :] + hour_sum(
        [jnp.dot(low, flipped[h, rows, :], preferred_element_type=F32) for h in range(flipped.shape[0])], hour_t
    )
    put_gram(message, own_gram(dest[...]))
    message[rank:, :] += before[rank:, :]


def call(kernel, outs, name, flops, *args):
    result = pl.pallas_call(
        kernel,
        in_specs=[WHOLE] * len(args),
        out_specs=tuple(WHOLE for _ in outs),
        out_shape=tuple(pltpu.VMEM(shape, dtype) for shape, dtype in outs),
        compiler_params=PARAMS,
        cost_estimate=pl.CostEstimate(flops=flops, bytes_accessed=0, transcendentals=0),
        name=name,
    )(*[in_vmem(arg) for arg in args])
    return result if len(outs) > 1 else result[0]


def swap(array, axis, mask):
    size = lax.axis_size(axis)
    return lax.ppermute(array, axis, [(index, index ^ mask) for index in range(size)])


def sum_dest(message):
    size = lax.axis_size("dst")
    mask = 1
    while 2 * mask < size:
        message = message + swap(message, "dst", 2 * mask - 1)
        mask *= 2
    return message, swap(message, "dst", 2 * mask - 1)


def sum_anchor(message):
    size = lax.axis_size("org")
    if size == 8:
        return message + swap(message, "org", 2), swap(message, "org", 4) + swap(message, "org", 6)
    mask = 2
    while 2 * mask < size:
        message = message + swap(message, "org", mask)
        mask *= 2
    return message, swap(message, "org", mask)


def body(counts, block_scales, anchor_factor, dest_factor, hour_factor):
    hours, rows, cols = counts.shape
    rank = anchor_factor.shape[0]
    size = cols // 2
    dest_rows = rank + gram_rows(rank, rows)
    anchor_rows = rank + gram_rows(rank, size)
    half_flops = 2 * 4 * hours * rank * rows * size

    tensor, message, dest_own, hour_gram, hour_t = pl.pallas_call(
        first_kernel,
        in_specs=[pl.BlockSpec(memory_space=pl.ANY)] * 4,
        out_specs=(WHOLE,) * 5,
        out_shape=(
            pltpu.VMEM((hours, rows, cols), BF16),
            pltpu.VMEM((dest_rows, rows), F32),
            pltpu.VMEM((rank, size), F32),
            pltpu.VMEM((rank, rank), F32),
            pltpu.VMEM((rank, hours), F32),
        ),
        scratch_shapes=[
            pltpu.VMEM(counts.shape, jnp.int32),
            pltpu.SMEM(block_scales.shape, F32),
            pltpu.VMEM(dest_factor.shape, F32),
            pltpu.VMEM(hour_factor.shape, F32),
            pltpu.SemaphoreType.DMA((hours,)),
            pltpu.SemaphoreType.DMA((3,)),
        ],
        compiler_params=pltpu.CompilerParams(vmem_limit_bytes=28 * 2**20),
        name="first",
    )(*[pltpu.with_memory_space_constraint(x, pltpu.HBM) for x in (counts, block_scales, dest_factor, hour_factor)])

    anchor_now = anchor_factor
    for sweep in range(SWEEPS):
        near, far = sum_dest(message)
        if sweep == 0:
            flipped = call(flip_kernel, [((hours, cols, rows), BF16)], "flip", 4 * half_flops, tensor, near)
        anchor_now, anchor_low, sent = call(
            anchor_kernel,
            [((rank, rows), F32), ((rank, rows), BF16), ((anchor_rows, size), F32)],
            "anchor", half_flops, tensor, anchor_now, near, far, hour_gram, hour_t, flipped,
        )
        received = swap(sent, "org", 1)
        kept = call(
            anchor_kept_kernel, [((anchor_rows, size), F32)], "anchor_kept", half_flops,
            tensor, anchor_low, hour_t, sent,
        )
        near, far = sum_anchor(kept + received)
        dest_own = call(dest_kernel, [((rank, size), F32)], "dest", 0, dest_own, near, far, hour_gram)
        dest_other = swap(dest_own, "org", 1)
        if sweep + 1 < SWEEPS:
            partial = call(
                dest_own_kernel, [((dest_rows, rows), F32)], "dest_own", half_flops,
                flipped, dest_own, hour_t,
            )
            message = call(
                dest_other_kernel, [((dest_rows, rows), F32)], "dest_other", half_flops,
                flipped, dest_other, hour_t, partial,
            )
    return anchor_now, call(join_kernel, [((rank, cols), F32)], "join", 0, dest_own, dest_other)


def solution(mesh):
    return jax.shard_map(
        body,
        mesh=mesh,
        in_specs=(
            P(None, "org", "dst"),
            P(None, "org", "dst"),
            P(None, "org"),
            P(None, "dst"),
            P(),
        ),
        out_specs=(P(None, "org"), P(None, "dst")),
        check_vma=False,
    )
```

time: 216 us -> 196 us (0.907)
  local copies, waits for them, and re-layouts: 16.5 us -> 1.37 us
  waiting for transfers between devices: 103 us -> 99.2 us
  Pallas kernels: 34.8 us -> 37.4 us
    unnamed x28 -> x4, local copies, waits for them, and re-layouts: 16.5 us -> 1.37 us
    ppermute x42, waiting for transfers between devices: 103 us -> 99.2 us  [swap(): lax.ppermute(array, axis, [(index, index ^ mask) for index in range(size)])]
    pallas_call x29 -> x31, Pallas kernels: 34.8 us -> 37.4 us  [the longest x30 27.8 us: call(): pl.pallas_call(kernel, in_specs=[WHOLE] * len(args), out_specs=tuple((WHO...]
  transfers between devices with their start and end apart: 42 -> 42, of which waited for: 38 -> 42; matrix products, arithmetic and copies ran while one was open for 0% -> 0% of each run, Pallas kernels for 5% -> 6%
where the time goes in v2:
time: 196 us
  waiting for transfers between devices  99.2 us (51%)
  starting transfers between devices  56.2 us (29%)
  Pallas kernels  37.4 us (19%)
    ppermute x42, waiting for transfers between devices, swap(): lax.ppermute(array, axis, [(index, index ^ mask) for index in range(size)])  99.2 us
    ppermute x42, starting transfers between devices, swap(): lax.ppermute(array, axis, [(index, index ^ mask) for index in range(size)])  56.2 us
    pallas_call x30, Pallas kernels, call(): pl.pallas_call(kernel, in_specs=[WHOLE] * len(args), out_specs=tuple((WHO...  27.8 us
    pallas_call x1, Pallas kernels, body(): pl.pallas_call(first_kernel, in_specs=[pl.BlockSpec(memory_space=pl.ANY)]...  9.66 us
  transfers between devices with their start and end apart: 42, of which 42 were waited for; matrix products, arithmetic and copies ran while one was open for 0% of the time, Pallas kernels for 6%

profile of v2, /device:TPU:0, one launch (start us, length us, event | category | flops | bytes accessed | tf_op | source)
XLA Modules:
  0.0 195.6 jit_solution(7784119431979262055)
XLA Ops:
  0.6 9.7 %first.1 = (bf16[8,512,1024]{2,1,0:T(8,128)(2,1)S(1)}, f32[72,512]{1,0:T(8,128)S(1)}, f32[64,512]{1,0:T(8,128)S(1)}, f32[64,64]{1,0:T(8,128)S(1)}, f32[64,8]{1,0:T(8,128)S(1)}) custom-call(s32[8,512,1024]{2,1,0:T(8,128)} %counts.1, f32[8,4,8]{2,1,0:T(4,128)} %scales.1, f32[64,1024]{1,0:T(8,128)} %dest.7, f32[8,64]{1,0:T(8,128)} %hour.1), custom_call_target="tpu_custom_call" | custom-call | tf_op jit(solution)/shard_map/first/pallas_call | solution.py:219
  10.3 3.1 %collective-permute-start = (f32[72,512]{1,0:T(8,128)S(1)}, f32[72,512]{1,0:T(8,128)S(1)}, u32[]{:S(2)}, u32[]{:S(2)}) collective-permute-start(f32[72,512]{1,0:T(8,128)S(1)} %get-tuple-element.26), channel_id=1, source_target_pairs={{0,1},{1,0},{2,3},{3,2},{4,5},{5,4},{6,7},{7,6},{8,9},{9,8},{10,11... | collective-permute-start | bytes 442376 | tf_op jit(solution)/shard_map/ppermute | solution.py:188
  13.4 3.8 %collective-permute-done = f32[72,512]{1,0:T(8,128)S(1)} collective-permute-done((f32[72,512]{1,0:T(8,128)S(1)}, f32[72,512]{1,0:T(8,128)S(1)}, u32[]{:S(2)}, u32[]{:S(2)}) %collective-permute-start) | collective-permute-done | bytes 147488 | tf_op jit(solution)/shard_map/ppermute | solution.py:188
  17.3 3.8 %collective-permute-start.1 = (f32[72,512]{1,0:T(8,128)S(1)}, f32[72,512]{1,0:T(8,128)S(1)}, u32[]{:S(2)}, u32[]{:S(2)}) collective-permute-start(f32[72,512]{1,0:T(8,128)S(1)} %add.72.after.near), channel_id=1, source_target_pairs={{0,3},{1,2},{2,1},{3,0},{4,7},{5,6},{6,5},{7,4},{8,11},{9,10},{10,... | collective-permute-start | bytes 442376 | tf_op jit(solution)/shard_map/ppermute | solution.py:188
  30.6 3.2 %collective-permute-done.3 = f32[72,512]{1,0:T(8,128)S(1)} collective-permute-done((f32[72,512]{1,0:T(8,128)S(1)}, f32[72,512]{1,0:T(8,128)S(1)}, u32[]{:S(2)}, u32[]{:S(2)}) %collective-permute-start.3) | collective-permute-done | bytes 147488 | tf_op jit(solution)/shard_map/ppermute | solution.py:188
  33.8 3.6 %collective-permute-done.5 = f32[72,512]{1,0:T(8,128)S(1)} collective-permute-done((f32[72,512]{1,0:T(8,128)S(1)}, f32[72,512]{1,0:T(8,128)S(1)}, u32[]{:S(2)}, u32[]{:S(2)}) %collective-permute-start.5) | collective-permute-done | bytes 147488 | tf_op jit(solution)/shard_map/ppermute | solution.py:188
  44.1 4.2 %collective-permute-done.7 = f32[72,512]{1,0:T(8,128)S(1)} collective-permute-done((f32[72,512]{1,0:T(8,128)S(1)}, f32[72,512]{1,0:T(8,128)S(1)}, u32[]{:S(2)}, u32[]{:S(2)}) %collective-permute-start.7) | collective-permute-done | bytes 147488 | tf_op jit(solution)/shard_map/ppermute | solution.py:188
  48.3 3.0 %collective-permute-start.8 = (f32[72,512]{1,0:T(8,128)S(1)}, f32[72,512]{1,0:T(8,128)S(1)}, u32[]{:S(2)}, u32[]{:S(2)}) collective-permute-start(f32[72,512]{1,0:T(8,128)S(1)} %add.76.near), channel_id=1, source_target_pairs={{0,3},{1,2},{2,1},{3,0},{4,7},{5,6},{6,5},{7,4},{8,11},{9,10},{10,... | collective-permute-start | bytes 442376 | tf_op jit(solution)/shard_map/ppermute | solution.py:188
  51.3 4.4 %collective-permute-done.8.far = f32[72,512]{1,0:T(8,128)S(1)} collective-permute-done((f32[72,512]{1,0:T(8,128)S(1)}, f32[72,512]{1,0:T(8,128)S(1)}, u32[]{:S(2)}, u32[]{:S(2)}) %collective-permute-start.8) | collective-permute-done | bytes 147488 | tf_op jit(solution)/shard_map/ppermute | solution.py:188
  62.0 3.2 %collective-permute-done.10 = f32[72,512]{1,0:T(8,128)S(1)} collective-permute-done((f32[72,512]{1,0:T(8,128)S(1)}, f32[72,512]{1,0:T(8,128)S(1)}, u32[]{:S(2)}, u32[]{:S(2)}) %collective-permute-start.10) | collective-permute-done | bytes 147488 | tf_op jit(solution)/shard_map/ppermute | solution.py:188
  71.9 2.9 %collective-permute-start.14 = (f32[72,512]{1,0:T(8,128)S(1)}, f32[72,512]{1,0:T(8,128)S(1)}, u32[]{:S(2)}, u32[]{:S(2)}) collective-permute-start(f32[72,512]{1,0:T(8,128)S(1)} %dest_other.6), channel_id=1, source_target_pairs={{0,1},{1,0},{2,3},{3,2},{4,5},{5,4},{6,7},{7,6},{8,9},{9,8},{10,11... | collective-permute-start | bytes 442376 | tf_op jit(solution)/shard_map/ppermute | solution.py:188
  74.9 4.2 %collective-permute-done.14 = f32[72,512]{1,0:T(8,128)S(1)} collective-permute-done((f32[72,512]{1,0:T(8,128)S(1)}, f32[72,512]{1,0:T(8,128)S(1)}, u32[]{:S(2)}, u32[]{:S(2)}) %collective-permute-start.14) | collective-permute-done | bytes 147488 | tf_op jit(solution)/shard_map/ppermute | solution.py:188
  79.1 2.7 %collective-permute-start.15 = (f32[72,512]{1,0:T(8,128)S(1)}, f32[72,512]{1,0:T(8,128)S(1)}, u32[]{:S(2)}, u32[]{:S(2)}) collective-permute-start(f32[72,512]{1,0:T(8,128)S(1)} %add.80.near), channel_id=1, source_target_pairs={{0,3},{1,2},{2,1},{3,0},{4,7},{5,6},{6,5},{7,4},{8,11},{9,10},{10,... | collective-permute-start | bytes 442376 | tf_op jit(solution)/shard_map/ppermute | solution.py:188
  81.8 4.7 %collective-permute-done.15.far = f32[72,512]{1,0:T(8,128)S(1)} collective-permute-done((f32[72,512]{1,0:T(8,128)S(1)}, f32[72,512]{1,0:T(8,128)S(1)}, u32[]{:S(2)}, u32[]{:S(2)}) %collective-permute-start.15) | collective-permute-done | bytes 147488 | tf_op jit(solution)/shard_map/ppermute | solution.py:188
  92.8 3.2 %collective-permute-done.17 = f32[72,512]{1,0:T(8,128)S(1)} collective-permute-done((f32[72,512]{1,0:T(8,128)S(1)}, f32[72,512]{1,0:T(8,128)S(1)}, u32[]{:S(2)}, u32[]{:S(2)}) %collective-permute-start.17) | collective-permute-done | bytes 147488 | tf_op jit(solution)/shard_map/ppermute | solution.py:188
  96.0 3.4 %collective-permute-done.19 = f32[72,512]{1,0:T(8,128)S(1)} collective-permute-done((f32[72,512]{1,0:T(8,128)S(1)}, f32[72,512]{1,0:T(8,128)S(1)}, u32[]{:S(2)}, u32[]{:S(2)}) %collective-permute-start.19) | collective-permute-done | bytes 147488 | tf_op jit(solution)/shard_map/ppermute | solution.py:188
  103.6 2.7 %collective-permute-start.21 = (f32[72,512]{1,0:T(8,128)S(1)}, f32[72,512]{1,0:T(8,128)S(1)}, u32[]{:S(2)}, u32[]{:S(2)}) collective-permute-start(f32[72,512]{1,0:T(8,128)S(1)} %dest_other.7), channel_id=1, source_target_pairs={{0,1},{1,0},{2,3},{3,2},{4,5},{5,4},{6,7},{7,6},{8,9},{9,8},{10,11... | collective-permute-start | bytes 442376 | tf_op jit(solution)/shard_map/ppermute | solution.py:188
  106.3 4.2 %collective-permute-done.21 = f32[72,512]{1,0:T(8,128)S(1)} collective-permute-done((f32[72,512]{1,0:T(8,128)S(1)}, f32[72,512]{1,0:T(8,128)S(1)}, u32[]{:S(2)}, u32[]{:S(2)}) %collective-permute-start.21) | collective-permute-done | bytes 147488 | tf_op jit(solution)/shard_map/ppermute | solution.py:188
  110.5 2.7 %collective-permute-start.22 = (f32[72,512]{1,0:T(8,128)S(1)}, f32[72,512]{1,0:T(8,128)S(1)}, u32[]{:S(2)}, u32[]{:S(2)}) collective-permute-start(f32[72,512]{1,0:T(8,128)S(1)} %add.84.near), channel_id=1, source_target_pairs={{0,3},{1,2},{2,1},{3,0},{4,7},{5,6},{6,5},{7,4},{8,11},{9,10},{10,... | collective-permute-start | bytes 442376 | tf_op jit(solution)/shard_map/ppermute | solution.py:188
  113.3 4.7 %collective-permute-done.22.far = f32[72,512]{1,0:T(8,128)S(1)} collective-permute-done((f32[72,512]{1,0:T(8,128)S(1)}, f32[72,512]{1,0:T(8,128)S(1)}, u32[]{:S(2)}, u32[]{:S(2)}) %collective-permute-start.22) | collective-permute-done | bytes 147488 | tf_op jit(solution)/shard_map/ppermute | solution.py:188
  124.2 3.2 %collective-permute-done.24 = f32[72,512]{1,0:T(8,128)S(1)} collective-permute-done((f32[72,512]{1,0:T(8,128)S(1)}, f32[72,512]{1,0:T(8,128)S(1)}, u32[]{:S(2)}, u32[]{:S(2)}) %collective-permute-start.24) | collective-permute-done | bytes 147488 | tf_op jit(solution)/shard_map/ppermute | solution.py:188
  134.0 2.7 %collective-permute-start.28 = (f32[72,512]{1,0:T(8,128)S(1)}, f32[72,512]{1,0:T(8,128)S(1)}, u32[]{:S(2)}, u32[]{:S(2)}) collective-permute-start(f32[72,512]{1,0:T(8,128)S(1)} %dest_other.8), channel_id=1, source_target_pairs={{0,1},{1,0},{2,3},{3,2},{4,5},{5,4},{6,7},{7,6},{8,9},{9,8},{10,11... | collective-permute-start | bytes 442376 | tf_op jit(solution)/shard_map/ppermute | solution.py:188
  136.8 4.2 %collective-permute-done.28 = f32[72,512]{1,0:T(8,128)S(1)} collective-permute-done((f32[72,512]{1,0:T(8,128)S(1)}, f32[72,512]{1,0:T(8,128)S(1)}, u32[]{:S(2)}, u32[]{:S(2)}) %collective-permute-start.28) | collective-permute-done | bytes 147488 | tf_op jit(solution)/shard_map/ppermute | solution.py:188
  141.0 2.7 %collective-permute-start.29 = (f32[72,512]{1,0:T(8,128)S(1)}, f32[72,512]{1,0:T(8,128)S(1)}, u32[]{:S(2)}, u32[]{:S(2)}) collective-permute-start(f32[72,512]{1,0:T(8,128)S(1)} %add.88.near), channel_id=1, source_target_pairs={{0,3},{1,2},{2,1},{3,0},{4,7},{5,6},{6,5},{7,4},{8,11},{9,10},{10,... | collective-permute-start | bytes 442376 | tf_op jit(solution)/shard_map/ppermute | solution.py:188
  143.7 4.7 %collective-permute-done.29.far = f32[72,512]{1,0:T(8,128)S(1)} collective-permute-done((f32[72,512]{1,0:T(8,128)S(1)}, f32[72,512]{1,0:T(8,128)S(1)}, u32[]{:S(2)}, u32[]{:S(2)}) %collective-permute-start.29) | collective-permute-done | bytes 147488 | tf_op jit(solution)/shard_map/ppermute | solution.py:188
  154.7 3.2 %collective-permute-done.31 = f32[72,512]{1,0:T(8,128)S(1)} collective-permute-done((f32[72,512]{1,0:T(8,128)S(1)}, f32[72,512]{1,0:T(8,128)S(1)}, u32[]{:S(2)}, u32[]{:S(2)}) %collective-permute-start.31) | collective-permute-done | bytes 147488 | tf_op jit(solution)/shard_map/ppermute | solution.py:188
  157.9 3.4 %collective-permute-done.33 = f32[72,512]{1,0:T(8,128)S(1)} collective-permute-done((f32[72,512]{1,0:T(8,128)S(1)}, f32[72,512]{1,0:T(8,128)S(1)}, u32[]{:S(2)}, u32[]{:S(2)}) %collective-permute-start.33) | collective-permute-done | bytes 147488 | tf_op jit(solution)/shard_map/ppermute | solution.py:188
  165.5 2.7 %collective-permute-start.35 = (f32[72,512]{1,0:T(8,128)S(1)}, f32[72,512]{1,0:T(8,128)S(1)}, u32[]{:S(2)}, u32[]{:S(2)}) collective-permute-start(f32[72,512]{1,0:T(8,128)S(1)} %dest_other.9), channel_id=1, source_target_pairs={{0,1},{1,0},{2,3},{3,2},{4,5},{5,4},{6,7},{7,6},{8,9},{9,8},{10,11... | collective-permute-start | bytes 442376 | tf_op jit(solution)/shard_map/ppermute | solution.py:188
  168.2 4.2 %collective-permute-done.35 = f32[72,512]{1,0:T(8,128)S(1)} collective-permute-done((f32[72,512]{1,0:T(8,128)S(1)}, f32[72,512]{1,0:T(8,128)S(1)}, u32[]{:S(2)}, u32[]{:S(2)}) %collective-permute-start.35) | collective-permute-done | bytes 147488 | tf_op jit(solution)/shard_map/ppermute | solution.py:188
  172.5 2.7 %collective-permute-start.36 = (f32[72,512]{1,0:T(8,128)S(1)}, f32[72,512]{1,0:T(8,128)S(1)}, u32[]{:S(2)}, u32[]{:S(2)}) collective-permute-start(f32[72,512]{1,0:T(8,128)S(1)} %add.92.near), channel_id=1, source_target_pairs={{0,3},{1,2},{2,1},{3,0},{4,7},{5,6},{6,5},{7,4},{8,11},{9,10},{10,... | collective-permute-start | bytes 442376 | tf_op jit(solution)/shard_map/ppermute | solution.py:188
  175.1 4.7 %collective-permute-done.36.far = f32[72,512]{1,0:T(8,128)S(1)} collective-permute-done((f32[72,512]{1,0:T(8,128)S(1)}, f32[72,512]{1,0:T(8,128)S(1)}, u32[]{:S(2)}, u32[]{:S(2)}) %collective-permute-start.36) | collective-permute-done | bytes 147488 | tf_op jit(solution)/shard_map/ppermute | solution.py:188
  186.2 3.2 %collective-permute-done.38 = f32[72,512]{1,0:T(8,128)S(1)} collective-permute-done((f32[72,512]{1,0:T(8,128)S(1)}, f32[72,512]{1,0:T(8,128)S(1)}, u32[]{:S(2)}, u32[]{:S(2)}) %collective-permute-start.38) | collective-permute-done | bytes 147488 | tf_op jit(solution)/shard_map/ppermute | solution.py:188
  (111 shorter events, 75.4 us)
Async XLA Ops:
  10.3 6.9 %collective-permute-start = (f32[72,512]{1,0:T(8,128)S(1)}, f32[72,512]{1,0:T(8,128)S(1)}, u32[]{:S(2)}, u32[]{:S(2)}) collective-permute-start(f32[72,512]{1,0:T(8,128)S(1)} %get-tuple-element.26), channel_id=1, source_target_pairs={{0,1},{1,0},{2,3},{3,2},{4,5},{5,4},{6,7},{7,6},{8,9},{9,8},{10,11... | collective-permute-start | bytes 442376 | tf_op jit(solution)/shard_map/ppermute | solution.py:188
  17.3 7.1 %collective-permute-start.1 = (f32[72,512]{1,0:T(8,128)S(1)}, f32[72,512]{1,0:T(8,128)S(1)}, u32[]{:S(2)}, u32[]{:S(2)}) collective-permute-start(f32[72,512]{1,0:T(8,128)S(1)} %add.72.after.near), channel_id=1, source_target_pairs={{0,3},{1,2},{2,1},{3,0},{4,7},{5,6},{6,5},{7,4},{8,11},{9,10},{10,... | collective-permute-start | bytes 442376 | tf_op jit(solution)/shard_map/ppermute | solution.py:188
  27.1 6.8 %collective-permute-start.3 = (f32[72,512]{1,0:T(8,128)S(1)}, f32[72,512]{1,0:T(8,128)S(1)}, u32[]{:S(2)}, u32[]{:S(2)}) collective-permute-start(f32[72,512]{1,0:T(8,128)S(1)} %add.73), channel_id=1, source_target_pairs={{0,8},{4,12},{8,0},{12,4},{16,24},{20,28},{24,16},{28,20},{1,9},{5... | collective-permute-start | bytes 442376 | tf_op jit(solution)/shard_map/ppermute | solution.py:188
  28.8 8.6 %collective-permute-start.5 = (f32[72,512]{1,0:T(8,128)S(1)}, f32[72,512]{1,0:T(8,128)S(1)}, u32[]{:S(2)}, u32[]{:S(2)}) collective-permute-start(f32[72,512]{1,0:T(8,128)S(1)} %add.73), channel_id=1, source_target_pairs={{0,24},{4,28},{8,16},{12,20},{16,8},{20,12},{24,0},{28,4},{1,25},{... | collective-permute-start | bytes 442376 | tf_op jit(solution)/shard_map/ppermute | solution.py:188
  30.3 8.5 %collective-permute-start.4 = (f32[72,512]{1,0:T(8,128)S(1)}, f32[72,512]{1,0:T(8,128)S(1)}, u32[]{:S(2)}, u32[]{:S(2)}) collective-permute-start(f32[72,512]{1,0:T(8,128)S(1)} %add.73), channel_id=1, source_target_pairs={{0,16},{4,20},{8,24},{12,28},{16,0},{20,4},{24,8},{28,12},{1,17},{... | collective-permute-start | bytes 442376 | tf_op jit(solution)/shard_map/ppermute | solution.py:188
  39.1 1.4 collective-permute-start.6
  41.6 6.7 %collective-permute-start.7 = (f32[72,512]{1,0:T(8,128)S(1)}, f32[72,512]{1,0:T(8,128)S(1)}, u32[]{:S(2)}, u32[]{:S(2)}) collective-permute-start(f32[72,512]{1,0:T(8,128)S(1)} %dest_other.5), channel_id=1, source_target_pairs={{0,1},{1,0},{2,3},{3,2},{4,5},{5,4},{6,7},{7,6},{8,9},{9,8},{10,11... | collective-permute-start | bytes 442376 | tf_op jit(solution)/shard_map/ppermute | solution.py:188
  48.3 7.4 %collective-permute-start.8 = (f32[72,512]{1,0:T(8,128)S(1)}, f32[72,512]{1,0:T(8,128)S(1)}, u32[]{:S(2)}, u32[]{:S(2)}) collective-permute-start(f32[72,512]{1,0:T(8,128)S(1)} %add.76.near), channel_id=1, source_target_pairs={{0,3},{1,2},{2,1},{3,0},{4,7},{5,6},{6,5},{7,4},{8,11},{9,10},{10,... | collective-permute-start | bytes 442376 | tf_op jit(solution)/shard_map/ppermute | solution.py:188
  58.4 6.8 %collective-permute-start.10 = (f32[72,512]{1,0:T(8,128)S(1)}, f32[72,512]{1,0:T(8,128)S(1)}, u32[]{:S(2)}, u32[]{:S(2)}) collective-permute-start(f32[72,512]{1,0:T(8,128)S(1)} %add.77), channel_id=1, source_target_pairs={{0,8},{4,12},{8,0},{12,4},{16,24},{20,28},{24,16},{28,20},{1,9},{5... | collective-permute-start | bytes 442376 | tf_op jit(solution)/shard_map/ppermute | solution.py:188
  60.0 7.6 %collective-permute-start.12 = (f32[72,512]{1,0:T(8,128)S(1)}, f32[72,512]{1,0:T(8,128)S(1)}, u32[]{:S(2)}, u32[]{:S(2)}) collective-permute-start(f32[72,512]{1,0:T(8,128)S(1)} %add.77), channel_id=1, source_target_pairs={{0,24},{4,28},{8,16},{12,20},{16,8},{20,12},{24,0},{28,4},{1,25},{... | collective-permute-start | bytes 442376 | tf_op jit(solution)/shard_map/ppermute | solution.py:188
  60.5 8.5 %collective-permute-start.11 = (f32[72,512]{1,0:T(8,128)S(1)}, f32[72,512]{1,0:T(8,128)S(1)}, u32[]{:S(2)}, u32[]{:S(2)}) collective-permute-start(f32[72,512]{1,0:T(8,128)S(1)} %add.77), channel_id=1, source_target_pairs={{0,16},{4,20},{8,24},{12,28},{16,0},{20,4},{24,8},{28,12},{1,17},{... | collective-permute-start | bytes 442376 | tf_op jit(solution)/shard_map/ppermute | solution.py:188
  69.3 1.4 collective-permute-start.13
  71.9 7.1 %collective-permute-start.14 = (f32[72,512]{1,0:T(8,128)S(1)}, f32[72,512]{1,0:T(8,128)S(1)}, u32[]{:S(2)}, u32[]{:S(2)}) collective-permute-start(f32[72,512]{1,0:T(8,128)S(1)} %dest_other.6), channel_id=1, source_target_pairs={{0,1},{1,0},{2,3},{3,2},{4,5},{5,4},{6,7},{7,6},{8,9},{9,8},{10,11... | collective-permute-start | bytes 442376 | tf_op jit(solution)/shard_map/ppermute | solution.py:188
  79.1 7.4 %collective-permute-start.15 = (f32[72,512]{1,0:T(8,128)S(1)}, f32[72,512]{1,0:T(8,128)S(1)}, u32[]{:S(2)}, u32[]{:S(2)}) collective-permute-start(f32[72,512]{1,0:T(8,128)S(1)} %add.80.near), channel_id=1, source_target_pairs={{0,3},{1,2},{2,1},{3,0},{4,7},{5,6},{6,5},{7,4},{8,11},{9,10},{10,... | collective-permute-start | bytes 442376 | tf_op jit(solution)/shard_map/ppermute | solution.py:188
  89.2 6.8 %collective-permute-start.17 = (f32[72,512]{1,0:T(8,128)S(1)}, f32[72,512]{1,0:T(8,128)S(1)}, u32[]{:S(2)}, u32[]{:S(2)}) collective-permute-start(f32[72,512]{1,0:T(8,128)S(1)} %add.81), channel_id=1, source_target_pairs={{0,8},{4,12},{8,0},{12,4},{16,24},{20,28},{24,16},{28,20},{1,9},{5... | collective-permute-start | bytes 442376 | tf_op jit(solution)/shard_map/ppermute | solution.py:188
  90.8 8.6 %collective-permute-start.19 = (f32[72,512]{1,0:T(8,128)S(1)}, f32[72,512]{1,0:T(8,128)S(1)}, u32[]{:S(2)}, u32[]{:S(2)}) collective-permute-start(f32[72,512]{1,0:T(8,128)S(1)} %add.81), channel_id=1, source_target_pairs={{0,24},{4,28},{8,16},{12,20},{16,8},{20,12},{24,0},{28,4},{1,25},{... | collective-permute-start | bytes 442376 | tf_op jit(solution)/shard_map/ppermute | solution.py:188
  92.3 8.5 %collective-permute-start.18 = (f32[72,512]{1,0:T(8,128)S(1)}, f32[72,512]{1,0:T(8,128)S(1)}, u32[]{:S(2)}, u32[]{:S(2)}) collective-permute-start(f32[72,512]{1,0:T(8,128)S(1)} %add.81), channel_id=1, source_target_pairs={{0,16},{4,20},{8,24},{12,28},{16,0},{20,4},{24,8},{28,12},{1,17},{... | collective-permute-start | bytes 442376 | tf_op jit(solution)/shard_map/ppermute | solution.py:188
  103.6 6.9 %collective-permute-start.21 = (f32[72,512]{1,0:T(8,128)S(1)}, f32[72,512]{1,0:T(8,128)S(1)}, u32[]{:S(2)}, u32[]{:S(2)}) collective-permute-start(f32[72,512]{1,0:T(8,128)S(1)} %dest_other.7), channel_id=1, source_target_pairs={{0,1},{1,0},{2,3},{3,2},{4,5},{5,4},{6,7},{7,6},{8,9},{9,8},{10,11... | collective-permute-start | bytes 442376 | tf_op jit(solution)/shard_map/ppermute | solution.py:188
  110.5 7.4 %collective-permute-start.22 = (f32[72,512]{1,0:T(8,128)S(1)}, f32[72,512]{1,0:T(8,128)S(1)}, u32[]{:S(2)}, u32[]{:S(2)}) collective-permute-start(f32[72,512]{1,0:T(8,128)S(1)} %add.84.near), channel_id=1, source_target_pairs={{0,3},{1,2},{2,1},{3,0},{4,7},{5,6},{6,5},{7,4},{8,11},{9,10},{10,... | collective-permute-start | bytes 442376 | tf_op jit(solution)/shard_map/ppermute | solution.py:188
  120.7 6.8 %collective-permute-start.24 = (f32[72,512]{1,0:T(8,128)S(1)}, f32[72,512]{1,0:T(8,128)S(1)}, u32[]{:S(2)}, u32[]{:S(2)}) collective-permute-start(f32[72,512]{1,0:T(8,128)S(1)} %add.85), channel_id=1, source_target_pairs={{0,8},{4,12},{8,0},{12,4},{16,24},{20,28},{24,16},{28,20},{1,9},{5... | collective-permute-start | bytes 442376 | tf_op jit(solution)/shard_map/ppermute | solution.py:188
  122.2 7.6 %collective-permute-start.26 = (f32[72,512]{1,0:T(8,128)S(1)}, f32[72,512]{1,0:T(8,128)S(1)}, u32[]{:S(2)}, u32[]{:S(2)}) collective-permute-start(f32[72,512]{1,0:T(8,128)S(1)} %add.85), channel_id=1, source_target_pairs={{0,24},{4,28},{8,16},{12,20},{16,8},{20,12},{24,0},{28,4},{1,25},{... | collective-permute-start | bytes 442376 | tf_op jit(solution)/shard_map/ppermute | solution.py:188
  122.7 8.5 %collective-permute-start.25 = (f32[72,512]{1,0:T(8,128)S(1)}, f32[72,512]{1,0:T(8,128)S(1)}, u32[]{:S(2)}, u32[]{:S(2)}) collective-permute-start(f32[72,512]{1,0:T(8,128)S(1)} %add.85), channel_id=1, source_target_pairs={{0,16},{4,20},{8,24},{12,28},{16,0},{20,4},{24,8},{28,12},{1,17},{... | collective-permute-start | bytes 442376 | tf_op jit(solution)/shard_map/ppermute | solution.py:188
  134.0 7.0 %collective-permute-start.28 = (f32[72,512]{1,0:T(8,128)S(1)}, f32[72,512]{1,0:T(8,128)S(1)}, u32[]{:S(2)}, u32[]{:S(2)}) collective-permute-start(f32[72,512]{1,0:T(8,128)S(1)} %dest_other.8), channel_id=1, source_target_pairs={{0,1},{1,0},{2,3},{3,2},{4,5},{5,4},{6,7},{7,6},{8,9},{9,8},{10,11... | collective-permute-start | bytes 442376 | tf_op jit(solution)/shard_map/ppermute | solution.py:188
  141.0 7.4 %collective-permute-start.29 = (f32[72,512]{1,0:T(8,128)S(1)}, f32[72,512]{1,0:T(8,128)S(1)}, u32[]{:S(2)}, u32[]{:S(2)}) collective-permute-start(f32[72,512]{1,0:T(8,128)S(1)} %add.88.near), channel_id=1, source_target_pairs={{0,3},{1,2},{2,1},{3,0},{4,7},{5,6},{6,5},{7,4},{8,11},{9,10},{10,... | collective-permute-start | bytes 442376 | tf_op jit(solution)/shard_map/ppermute | solution.py:188
  151.1 6.8 %collective-permute-start.31 = (f32[72,512]{1,0:T(8,128)S(1)}, f32[72,512]{1,0:T(8,128)S(1)}, u32[]{:S(2)}, u32[]{:S(2)}) collective-permute-start(f32[72,512]{1,0:T(8,128)S(1)} %add.89), channel_id=1, source_target_pairs={{0,8},{4,12},{8,0},{12,4},{16,24},{20,28},{24,16},{28,20},{1,9},{5... | collective-permute-start | bytes 442376 | tf_op jit(solution)/shard_map/ppermute | solution.py:188
  152.7 8.6 %collective-permute-start.33 = (f32[72,512]{1,0:T(8,128)S(1)}, f32[72,512]{1,0:T(8,128)S(1)}, u32[]{:S(2)}, u32[]{:S(2)}) collective-permute-start(f32[72,512]{1,0:T(8,128)S(1)} %add.89), channel_id=1, source_target_pairs={{0,24},{4,28},{8,16},{12,20},{16,8},{20,12},{24,0},{28,4},{1,25},{... | collective-permute-start | bytes 442376 | tf_op jit(solution)/shard_map/ppermute | solution.py:188
  154.2 8.5 %collective-permute-start.32 = (f32[72,512]{1,0:T(8,128)S(1)}, f32[72,512]{1,0:T(8,128)S(1)}, u32[]{:S(2)}, u32[]{:S(2)}) collective-permute-start(f32[72,512]{1,0:T(8,128)S(1)} %add.89), channel_id=1, source_target_pairs={{0,16},{4,20},{8,24},{12,28},{16,0},{20,4},{24,8},{28,12},{1,17},{... | collective-permute-start | bytes 442376 | tf_op jit(solution)/shard_map/ppermute | solution.py:188
  165.5 7.0 %collective-permute-start.35 = (f32[72,512]{1,0:T(8,128)S(1)}, f32[72,512]{1,0:T(8,128)S(1)}, u32[]{:S(2)}, u32[]{:S(2)}) collective-permute-start(f32[72,512]{1,0:T(8,128)S(1)} %dest_other.9), channel_id=1, source_target_pairs={{0,1},{1,0},{2,3},{3,2},{4,5},{5,4},{6,7},{7,6},{8,9},{9,8},{10,11... | collective-permute-start | bytes 442376 | tf_op jit(solution)/shard_map/ppermute | solution.py:188
  172.5 7.4 %collective-permute-start.36 = (f32[72,512]{1,0:T(8,128)S(1)}, f32[72,512]{1,0:T(8,128)S(1)}, u32[]{:S(2)}, u32[]{:S(2)}) collective-permute-start(f32[72,512]{1,0:T(8,128)S(1)} %add.92.near), channel_id=1, source_target_pairs={{0,3},{1,2},{2,1},{3,0},{4,7},{5,6},{6,5},{7,4},{8,11},{9,10},{10,... | collective-permute-start | bytes 442376 | tf_op jit(solution)/shard_map/ppermute | solution.py:188
  182.6 6.8 %collective-permute-start.38 = (f32[72,512]{1,0:T(8,128)S(1)}, f32[72,512]{1,0:T(8,128)S(1)}, u32[]{:S(2)}, u32[]{:S(2)}) collective-permute-start(f32[72,512]{1,0:T(8,128)S(1)} %add.93), channel_id=1, source_target_pairs={{0,8},{4,12},{8,0},{12,4},{16,24},{20,28},{24,16},{28,20},{1,9},{5... | collective-permute-start | bytes 442376 | tf_op jit(solution)/shard_map/ppermute | solution.py:188
  184.2 7.6 %collective-permute-start.40 = (f32[72,512]{1,0:T(8,128)S(1)}, f32[72,512]{1,0:T(8,128)S(1)}, u32[]{:S(2)}, u32[]{:S(2)}) collective-permute-start(f32[72,512]{1,0:T(8,128)S(1)} %add.93), channel_id=1, source_target_pairs={{0,24},{4,28},{8,16},{12,20},{16,8},{20,12},{24,0},{28,4},{1,25},{... | collective-permute-start | bytes 442376 | tf_op jit(solution)/shard_map/ppermute | solution.py:188
  184.6 8.5 %collective-permute-start.39 = (f32[72,512]{1,0:T(8,128)S(1)}, f32[72,512]{1,0:T(8,128)S(1)}, u32[]{:S(2)}, u32[]{:S(2)}) collective-permute-start(f32[72,512]{1,0:T(8,128)S(1)} %add.93), channel_id=1, source_target_pairs={{0,16},{4,20},{8,24},{12,28},{16,0},{20,4},{24,8},{28,12},{1,17},{... | collective-permute-start | bytes 442376 | tf_op jit(solution)/shard_map/ppermute | solution.py:188
  (11 other events, 17.2 us)

commit v3 on v2

--- a/solution.py
+++ b/solution.py
@@ -9,6 +9,7 @@
 
 SCALE_BLOCK = 128
 SWEEPS = 6
+IN_FLIGHT = 4
 F32 = jnp.float32
 BF16 = jnp.bfloat16
 HIGHEST = lax.Precision.HIGHEST
@@ -76,7 +77,7 @@
     for copy in small:
         copy.start()
     large = [pltpu.make_async_copy(counts.at[h], buffer.at[h], arrived.at[h]) for h in range(hours)]
-    for copy in large:
+    for copy in large[:IN_FLIGHT]:
         copy.start()
     for copy in small:
         copy.wait()
@@ -88,12 +89,18 @@
     total = None
     for h in range(hours):
         large[h].wait()
+        if h + IN_FLIGHT < hours:
+            large[h + IN_FLIGHT].start()
         for row_block in range(rows // SCALE_BLOCK):
             row = pl.ds(row_block * SCALE_BLOCK, SCALE_BLOCK)
-            for col_block in range(cols // SCALE_BLOCK):
-                col = pl.ds(col_block * SCALE_BLOCK, SCALE_BLOCK)
-                scale = scale_now[h, row_block, col_block]
-                tensor[h, row, col] = (buffer[h, row, col].astype(F32) * scale).astype(BF16)
+            scale = jnp.concatenate(
+                [
+                    jnp.full((1, SCALE_BLOCK), scale_now[h, row_block, col_block], F32)
+                    for col_block in range(cols // SCALE_BLOCK)
+                ],
+                axis=1,
+            )
+            tensor[h, row, :] = (buffer[h, row, :].astype(F32) * scale).astype(BF16)
         part = lax.dot_general(dest_low, tensor[h], (((1,), (1,)), ((), ())), preferred_element_type=F32)
         part = part * hour_t[:, h : h + 1]
         total = part if total is None else total + part

time: 196 us -> 194 us (0.990)
  Pallas kernels: 37.4 us -> 35.2 us
    pallas_call x1, Pallas kernels: 9.66 us -> 7.46 us  [body(): pl.pallas_call(first_kernel, in_specs=[pl.BlockSpec(memory_space=pl.ANY)]...]
where the time goes in v3:
time: 194 us; the launch traced here: 193 us
  waiting for transfers between devices  99.2 us (51%)
  starting transfers between devices  56.1 us (29%)
  Pallas kernels  35.2 us (18%)
    ppermute x42, waiting for transfers between devices, swap(): lax.ppermute(array, axis, [(index, index ^ mask) for index in range(size)])  99.2 us
    ppermute x42, starting transfers between devices, swap(): lax.ppermute(array, axis, [(index, index ^ mask) for index in range(size)])  56.1 us
    pallas_call x30, Pallas kernels, call(): pl.pallas_call(kernel, in_specs=[WHOLE] * len(args), out_specs=tuple((WHO...  27.8 us
    pallas_call x1, Pallas kernels, body(): pl.pallas_call(first_kernel, in_specs=[pl.BlockSpec(memory_space=pl.ANY)]...  7.46 us
  transfers between devices with their start and end apart: 42, of which 42 were waited for; matrix products, arithmetic and copies ran while one was open for 0% of the time, Pallas kernels for 6%

profile of v3, /device:TPU:0, one launch (start us, length us, event | category | flops | bytes accessed | tf_op | source)
XLA Modules:
  0.0 193.4 jit_solution(9911141748679776823)
XLA Ops:
  0.6 7.5 %first.1 = (bf16[8,512,1024]{2,1,0:T(8,128)(2,1)S(1)}, f32[72,512]{1,0:T(8,128)S(1)}, f32[64,512]{1,0:T(8,128)S(1)}, f32[64,64]{1,0:T(8,128)S(1)}, f32[64,8]{1,0:T(8,128)S(1)}) custom-call(s32[8,512,1024]{2,1,0:T(8,128)} %counts.1, f32[8,4,8]{2,1,0:T(4,128)} %scales.1, f32[64,1024]{1,0:T(8,128)} %dest.7, f32[8,64]{1,0:T(8,128)} %hour.1), custom_call_target="tpu_custom_call" | custom-call | tf_op jit(solution)/shard_map/first/pallas_call | solution.py:226
  8.1 3.1 %collective-permute-start = (f32[72,512]{1,0:T(8,128)S(1)}, f32[72,512]{1,0:T(8,128)S(1)}, u32[]{:S(2)}, u32[]{:S(2)}) collective-permute-start(f32[72,512]{1,0:T(8,128)S(1)} %get-tuple-element.26), channel_id=1, source_target_pairs={{0,1},{1,0},{2,3},{3,2},{4,5},{5,4},{6,7},{7,6},{8,9},{9,8},{10,11... | collective-permute-start | bytes 442376 | tf_op jit(solution)/shard_map/ppermute | solution.py:195
  11.2 3.8 %collective-permute-done = f32[72,512]{1,0:T(8,128)S(1)} collective-permute-done((f32[72,512]{1,0:T(8,128)S(1)}, f32[72,512]{1,0:T(8,128)S(1)}, u32[]{:S(2)}, u32[]{:S(2)}) %collective-permute-start) | collective-permute-done | bytes 147488 | tf_op jit(solution)/shard_map/ppermute | solution.py:195
  15.1 3.8 %collective-permute-start.1 = (f32[72,512]{1,0:T(8,128)S(1)}, f32[72,512]{1,0:T(8,128)S(1)}, u32[]{:S(2)}, u32[]{:S(2)}) collective-permute-start(f32[72,512]{1,0:T(8,128)S(1)} %add.72.after.near), channel_id=1, source_target_pairs={{0,3},{1,2},{2,1},{3,0},{4,7},{5,6},{6,5},{7,4},{8,11},{9,10},{10,... | collective-permute-start | bytes 442376 | tf_op jit(solution)/shard_map/ppermute | solution.py:195
  28.4 3.2 %collective-permute-done.3 = f32[72,512]{1,0:T(8,128)S(1)} collective-permute-done((f32[72,512]{1,0:T(8,128)S(1)}, f32[72,512]{1,0:T(8,128)S(1)}, u32[]{:S(2)}, u32[]{:S(2)}) %collective-permute-start.3) | collective-permute-done | bytes 147488 | tf_op jit(solution)/shard_map/ppermute | solution.py:195
  31.6 3.6 %collective-permute-done.5 = f32[72,512]{1,0:T(8,128)S(1)} collective-permute-done((f32[72,512]{1,0:T(8,128)S(1)}, f32[72,512]{1,0:T(8,128)S(1)}, u32[]{:S(2)}, u32[]{:S(2)}) %collective-permute-start.5) | collective-permute-done | bytes 147488 | tf_op jit(solution)/shard_map/ppermute | solution.py:195
  41.9 4.2 %collective-permute-done.7 = f32[72,512]{1,0:T(8,128)S(1)} collective-permute-done((f32[72,512]{1,0:T(8,128)S(1)}, f32[72,512]{1,0:T(8,128)S(1)}, u32[]{:S(2)}, u32[]{:S(2)}) %collective-permute-start.7) | collective-permute-done | bytes 147488 | tf_op jit(solution)/shard_map/ppermute | solution.py:195
  46.1 2.9 %collective-permute-start.8 = (f32[72,512]{1,0:T(8,128)S(1)}, f32[72,512]{1,0:T(8,128)S(1)}, u32[]{:S(2)}, u32[]{:S(2)}) collective-permute-start(f32[72,512]{1,0:T(8,128)S(1)} %add.76.near), channel_id=1, source_target_pairs={{0,3},{1,2},{2,1},{3,0},{4,7},{5,6},{6,5},{7,4},{8,11},{9,10},{10,... | collective-permute-start | bytes 442376 | tf_op jit(solution)/shard_map/ppermute | solution.py:195
  49.1 4.5 %collective-permute-done.8.far = f32[72,512]{1,0:T(8,128)S(1)} collective-permute-done((f32[72,512]{1,0:T(8,128)S(1)}, f32[72,512]{1,0:T(8,128)S(1)}, u32[]{:S(2)}, u32[]{:S(2)}) %collective-permute-start.8) | collective-permute-done | bytes 147488 | tf_op jit(solution)/shard_map/ppermute | solution.py:195
  59.8 3.2 %collective-permute-done.10 = f32[72,512]{1,0:T(8,128)S(1)} collective-permute-done((f32[72,512]{1,0:T(8,128)S(1)}, f32[72,512]{1,0:T(8,128)S(1)}, u32[]{:S(2)}, u32[]{:S(2)}) %collective-permute-start.10) | collective-permute-done | bytes 147488 | tf_op jit(solution)/shard_map/ppermute | solution.py:195
  69.8 2.9 %collective-permute-start.14 = (f32[72,512]{1,0:T(8,128)S(1)}, f32[72,512]{1,0:T(8,128)S(1)}, u32[]{:S(2)}, u32[]{:S(2)}) collective-permute-start(f32[72,512]{1,0:T(8,128)S(1)} %dest_other.6), channel_id=1, source_target_pairs={{0,1},{1,0},{2,3},{3,2},{4,5},{5,4},{6,7},{7,6},{8,9},{9,8},{10,11... | collective-permute-start | bytes 442376 | tf_op jit(solution)/shard_map/ppermute | solution.py:195
  72.7 4.2 %collective-permute-done.14 = f32[72,512]{1,0:T(8,128)S(1)} collective-permute-done((f32[72,512]{1,0:T(8,128)S(1)}, f32[72,512]{1,0:T(8,128)S(1)}, u32[]{:S(2)}, u32[]{:S(2)}) %collective-permute-start.14) | collective-permute-done | bytes 147488 | tf_op jit(solution)/shard_map/ppermute | solution.py:195
  76.9 2.7 %collective-permute-start.15 = (f32[72,512]{1,0:T(8,128)S(1)}, f32[72,512]{1,0:T(8,128)S(1)}, u32[]{:S(2)}, u32[]{:S(2)}) collective-permute-start(f32[72,512]{1,0:T(8,128)S(1)} %add.80.near), channel_id=1, source_target_pairs={{0,3},{1,2},{2,1},{3,0},{4,7},{5,6},{6,5},{7,4},{8,11},{9,10},{10,... | collective-permute-start | bytes 442376 | tf_op jit(solution)/shard_map/ppermute | solution.py:195
  79.6 4.7 %collective-permute-done.15.far = f32[72,512]{1,0:T(8,128)S(1)} collective-permute-done((f32[72,512]{1,0:T(8,128)S(1)}, f32[72,512]{1,0:T(8,128)S(1)}, u32[]{:S(2)}, u32[]{:S(2)}) %collective-permute-start.15) | collective-permute-done | bytes 147488 | tf_op jit(solution)/shard_map/ppermute | solution.py:195
  90.6 3.2 %collective-permute-done.17 = f32[72,512]{1,0:T(8,128)S(1)} collective-permute-done((f32[72,512]{1,0:T(8,128)S(1)}, f32[72,512]{1,0:T(8,128)S(1)}, u32[]{:S(2)}, u32[]{:S(2)}) %collective-permute-start.17) | collective-permute-done | bytes 147488 | tf_op jit(solution)/shard_map/ppermute | solution.py:195
  93.8 3.4 %collective-permute-done.19 = f32[72,512]{1,0:T(8,128)S(1)} collective-permute-done((f32[72,512]{1,0:T(8,128)S(1)}, f32[72,512]{1,0:T(8,128)S(1)}, u32[]{:S(2)}, u32[]{:S(2)}) %collective-permute-start.19) | collective-permute-done | bytes 147488 | tf_op jit(solution)/shard_map/ppermute | solution.py:195
  101.4 2.7 %collective-permute-start.21 = (f32[72,512]{1,0:T(8,128)S(1)}, f32[72,512]{1,0:T(8,128)S(1)}, u32[]{:S(2)}, u32[]{:S(2)}) collective-permute-start(f32[72,512]{1,0:T(8,128)S(1)} %dest_other.7), channel_id=1, source_target_pairs={{0,1},{1,0},{2,3},{3,2},{4,5},{5,4},{6,7},{7,6},{8,9},{9,8},{10,11... | collective-permute-start | bytes 442376 | tf_op jit(solution)/shard_map/ppermute | solution.py:195
  104.1 4.2 %collective-permute-done.21 = f32[72,512]{1,0:T(8,128)S(1)} collective-permute-done((f32[72,512]{1,0:T(8,128)S(1)}, f32[72,512]{1,0:T(8,128)S(1)}, u32[]{:S(2)}, u32[]{:S(2)}) %collective-permute-start.21) | collective-permute-done | bytes 147488 | tf_op jit(solution)/shard_map/ppermute | solution.py:195
  108.4 2.7 %collective-permute-start.22 = (f32[72,512]{1,0:T(8,128)S(1)}, f32[72,512]{1,0:T(8,128)S(1)}, u32[]{:S(2)}, u32[]{:S(2)}) collective-permute-start(f32[72,512]{1,0:T(8,128)S(1)} %add.84.near), channel_id=1, source_target_pairs={{0,3},{1,2},{2,1},{3,0},{4,7},{5,6},{6,5},{7,4},{8,11},{9,10},{10,... | collective-permute-start | bytes 442376 | tf_op jit(solution)/shard_map/ppermute | solution.py:195
  111.1 4.7 %collective-permute-done.22.far = f32[72,512]{1,0:T(8,128)S(1)} collective-permute-done((f32[72,512]{1,0:T(8,128)S(1)}, f32[72,512]{1,0:T(8,128)S(1)}, u32[]{:S(2)}, u32[]{:S(2)}) %collective-permute-start.22) | collective-permute-done | bytes 147488 | tf_op jit(solution)/shard_map/ppermute | solution.py:195
  122.1 3.2 %collective-permute-done.24 = f32[72,512]{1,0:T(8,128)S(1)} collective-permute-done((f32[72,512]{1,0:T(8,128)S(1)}, f32[72,512]{1,0:T(8,128)S(1)}, u32[]{:S(2)}, u32[]{:S(2)}) %collective-permute-start.24) | collective-permute-done | bytes 147488 | tf_op jit(solution)/shard_map/ppermute | solution.py:195
  131.8 2.7 %collective-permute-start.28 = (f32[72,512]{1,0:T(8,128)S(1)}, f32[72,512]{1,0:T(8,128)S(1)}, u32[]{:S(2)}, u32[]{:S(2)}) collective-permute-start(f32[72,512]{1,0:T(8,128)S(1)} %dest_other.8), channel_id=1, source_target_pairs={{0,1},{1,0},{2,3},{3,2},{4,5},{5,4},{6,7},{7,6},{8,9},{9,8},{10,11... | collective-permute-start | bytes 442376 | tf_op jit(solution)/shard_map/ppermute | solution.py:195
  134.6 4.2 %collective-permute-done.28 = f32[72,512]{1,0:T(8,128)S(1)} collective-permute-done((f32[72,512]{1,0:T(8,128)S(1)}, f32[72,512]{1,0:T(8,128)S(1)}, u32[]{:S(2)}, u32[]{:S(2)}) %collective-permute-start.28) | collective-permute-done | bytes 147488 | tf_op jit(solution)/shard_map/ppermute | solution.py:195
  138.8 2.7 %collective-permute-start.29 = (f32[72,512]{1,0:T(8,128)S(1)}, f32[72,512]{1,0:T(8,128)S(1)}, u32[]{:S(2)}, u32[]{:S(2)}) collective-permute-start(f32[72,512]{1,0:T(8,128)S(1)} %add.88.near), channel_id=1, source_target_pairs={{0,3},{1,2},{2,1},{3,0},{4,7},{5,6},{6,5},{7,4},{8,11},{9,10},{10,... | collective-permute-start | bytes 442376 | tf_op jit(solution)/shard_map/ppermute | solution.py:195
  141.5 4.7 %collective-permute-done.29.far = f32[72,512]{1,0:T(8,128)S(1)} collective-permute-done((f32[72,512]{1,0:T(8,128)S(1)}, f32[72,512]{1,0:T(8,128)S(1)}, u32[]{:S(2)}, u32[]{:S(2)}) %collective-permute-start.29) | collective-permute-done | bytes 147488 | tf_op jit(solution)/shard_map/ppermute | solution.py:195
  152.5 3.2 %collective-permute-done.31 = f32[72,512]{1,0:T(8,128)S(1)} collective-permute-done((f32[72,512]{1,0:T(8,128)S(1)}, f32[72,512]{1,0:T(8,128)S(1)}, u32[]{:S(2)}, u32[]{:S(2)}) %collective-permute-start.31) | collective-permute-done | bytes 147488 | tf_op jit(solution)/shard_map/ppermute | solution.py:195
  155.7 3.4 %collective-permute-done.33 = f32[72,512]{1,0:T(8,128)S(1)} collective-permute-done((f32[72,512]{1,0:T(8,128)S(1)}, f32[72,512]{1,0:T(8,128)S(1)}, u32[]{:S(2)}, u32[]{:S(2)}) %collective-permute-start.33) | collective-permute-done | bytes 147488 | tf_op jit(solution)/shard_map/ppermute | solution.py:195
  163.3 2.7 %collective-permute-start.35 = (f32[72,512]{1,0:T(8,128)S(1)}, f32[72,512]{1,0:T(8,128)S(1)}, u32[]{:S(2)}, u32[]{:S(2)}) collective-permute-start(f32[72,512]{1,0:T(8,128)S(1)} %dest_other.9), channel_id=1, source_target_pairs={{0,1},{1,0},{2,3},{3,2},{4,5},{5,4},{6,7},{7,6},{8,9},{9,8},{10,11... | collective-permute-start | bytes 442376 | tf_op jit(solution)/shard_map/ppermute | solution.py:195
  166.0 4.2 %collective-permute-done.35 = f32[72,512]{1,0:T(8,128)S(1)} collective-permute-done((f32[72,512]{1,0:T(8,128)S(1)}, f32[72,512]{1,0:T(8,128)S(1)}, u32[]{:S(2)}, u32[]{:S(2)}) %collective-permute-start.35) | collective-permute-done | bytes 147488 | tf_op jit(solution)/shard_map/ppermute | solution.py:195
  170.3 2.7 %collective-permute-start.36 = (f32[72,512]{1,0:T(8,128)S(1)}, f32[72,512]{1,0:T(8,128)S(1)}, u32[]{:S(2)}, u32[]{:S(2)}) collective-permute-start(f32[72,512]{1,0:T(8,128)S(1)} %add.92.near), channel_id=1, source_target_pairs={{0,3},{1,2},{2,1},{3,0},{4,7},{5,6},{6,5},{7,4},{8,11},{9,10},{10,... | collective-permute-start | bytes 442376 | tf_op jit(solution)/shard_map/ppermute | solution.py:195
  172.9 4.7 %collective-permute-done.36.far = f32[72,512]{1,0:T(8,128)S(1)} collective-permute-done((f32[72,512]{1,0:T(8,128)S(1)}, f32[72,512]{1,0:T(8,128)S(1)}, u32[]{:S(2)}, u32[]{:S(2)}) %collective-permute-start.36) | collective-permute-done | bytes 147488 | tf_op jit(solution)/shard_map/ppermute | solution.py:195
  184.0 3.2 %collective-permute-done.38 = f32[72,512]{1,0:T(8,128)S(1)} collective-permute-done((f32[72,512]{1,0:T(8,128)S(1)}, f32[72,512]{1,0:T(8,128)S(1)}, u32[]{:S(2)}, u32[]{:S(2)}) %collective-permute-start.38) | collective-permute-done | bytes 147488 | tf_op jit(solution)/shard_map/ppermute | solution.py:195
  (111 shorter events, 75.5 us)
Async XLA Ops:
  8.1 6.9 %collective-permute-start = (f32[72,512]{1,0:T(8,128)S(1)}, f32[72,512]{1,0:T(8,128)S(1)}, u32[]{:S(2)}, u32[]{:S(2)}) collective-permute-start(f32[72,512]{1,0:T(8,128)S(1)} %get-tuple-element.26), channel_id=1, source_target_pairs={{0,1},{1,0},{2,3},{3,2},{4,5},{5,4},{6,7},{7,6},{8,9},{9,8},{10,11... | collective-permute-start | bytes 442376 | tf_op jit(solution)/shard_map/ppermute | solution.py:195
  15.1 7.1 %collective-permute-start.1 = (f32[72,512]{1,0:T(8,128)S(1)}, f32[72,512]{1,0:T(8,128)S(1)}, u32[]{:S(2)}, u32[]{:S(2)}) collective-permute-start(f32[72,512]{1,0:T(8,128)S(1)} %add.72.after.near), channel_id=1, source_target_pairs={{0,3},{1,2},{2,1},{3,0},{4,7},{5,6},{6,5},{7,4},{8,11},{9,10},{10,... | collective-permute-start | bytes 442376 | tf_op jit(solution)/shard_map/ppermute | solution.py:195
  24.9 6.8 %collective-permute-start.3 = (f32[72,512]{1,0:T(8,128)S(1)}, f32[72,512]{1,0:T(8,128)S(1)}, u32[]{:S(2)}, u32[]{:S(2)}) collective-permute-start(f32[72,512]{1,0:T(8,128)S(1)} %add.73), channel_id=1, source_target_pairs={{0,8},{4,12},{8,0},{12,4},{16,24},{20,28},{24,16},{28,20},{1,9},{5... | collective-permute-start | bytes 442376 | tf_op jit(solution)/shard_map/ppermute | solution.py:195
  26.6 8.6 %collective-permute-start.5 = (f32[72,512]{1,0:T(8,128)S(1)}, f32[72,512]{1,0:T(8,128)S(1)}, u32[]{:S(2)}, u32[]{:S(2)}) collective-permute-start(f32[72,512]{1,0:T(8,128)S(1)} %add.73), channel_id=1, source_target_pairs={{0,24},{4,28},{8,16},{12,20},{16,8},{20,12},{24,0},{28,4},{1,25},{... | collective-permute-start | bytes 442376 | tf_op jit(solution)/shard_map/ppermute | solution.py:195
  28.1 8.5 %collective-permute-start.4 = (f32[72,512]{1,0:T(8,128)S(1)}, f32[72,512]{1,0:T(8,128)S(1)}, u32[]{:S(2)}, u32[]{:S(2)}) collective-permute-start(f32[72,512]{1,0:T(8,128)S(1)} %add.73), channel_id=1, source_target_pairs={{0,16},{4,20},{8,24},{12,28},{16,0},{20,4},{24,8},{28,12},{1,17},{... | collective-permute-start | bytes 442376 | tf_op jit(solution)/shard_map/ppermute | solution.py:195
  39.4 6.7 %collective-permute-start.7 = (f32[72,512]{1,0:T(8,128)S(1)}, f32[72,512]{1,0:T(8,128)S(1)}, u32[]{:S(2)}, u32[]{:S(2)}) collective-permute-start(f32[72,512]{1,0:T(8,128)S(1)} %dest_other.5), channel_id=1, source_target_pairs={{0,1},{1,0},{2,3},{3,2},{4,5},{5,4},{6,7},{7,6},{8,9},{9,8},{10,11... | collective-permute-start | bytes 442376 | tf_op jit(solution)/shard_map/ppermute | solution.py:195
  46.1 7.4 %collective-permute-start.8 = (f32[72,512]{1,0:T(8,128)S(1)}, f32[72,512]{1,0:T(8,128)S(1)}, u32[]{:S(2)}, u32[]{:S(2)}) collective-permute-start(f32[72,512]{1,0:T(8,128)S(1)} %add.76.near), channel_id=1, source_target_pairs={{0,3},{1,2},{2,1},{3,0},{4,7},{5,6},{6,5},{7,4},{8,11},{9,10},{10,... | collective-permute-start | bytes 442376 | tf_op jit(solution)/shard_map/ppermute | solution.py:195
  56.3 6.8 %collective-permute-start.10 = (f32[72,512]{1,0:T(8,128)S(1)}, f32[72,512]{1,0:T(8,128)S(1)}, u32[]{:S(2)}, u32[]{:S(2)}) collective-permute-start(f32[72,512]{1,0:T(8,128)S(1)} %add.77), channel_id=1, source_target_pairs={{0,8},{4,12},{8,0},{12,4},{16,24},{20,28},{24,16},{28,20},{1,9},{5... | collective-permute-start | bytes 442376 | tf_op jit(solution)/shard_map/ppermute | solution.py:195
  57.8 7.6 %collective-permute-start.12 = (f32[72,512]{1,0:T(8,128)S(1)}, f32[72,512]{1,0:T(8,128)S(1)}, u32[]{:S(2)}, u32[]{:S(2)}) collective-permute-start(f32[72,512]{1,0:T(8,128)S(1)} %add.77), channel_id=1, source_target_pairs={{0,24},{4,28},{8,16},{12,20},{16,8},{20,12},{24,0},{28,4},{1,25},{... | collective-permute-start | bytes 442376 | tf_op jit(solution)/shard_map/ppermute | solution.py:195
  58.3 8.5 %collective-permute-start.11 = (f32[72,512]{1,0:T(8,128)S(1)}, f32[72,512]{1,0:T(8,128)S(1)}, u32[]{:S(2)}, u32[]{:S(2)}) collective-permute-start(f32[72,512]{1,0:T(8,128)S(1)} %add.77), channel_id=1, source_target_pairs={{0,16},{4,20},{8,24},{12,28},{16,0},{20,4},{24,8},{28,12},{1,17},{... | collective-permute-start | bytes 442376 | tf_op jit(solution)/shard_map/ppermute | solution.py:195
  69.8 7.1 %collective-permute-start.14 = (f32[72,512]{1,0:T(8,128)S(1)}, f32[72,512]{1,0:T(8,128)S(1)}, u32[]{:S(2)}, u32[]{:S(2)}) collective-permute-start(f32[72,512]{1,0:T(8,128)S(1)} %dest_other.6), channel_id=1, source_target_pairs={{0,1},{1,0},{2,3},{3,2},{4,5},{5,4},{6,7},{7,6},{8,9},{9,8},{10,11... | collective-permute-start | bytes 442376 | tf_op jit(solution)/shard_map/ppermute | solution.py:195
  76.9 7.4 %collective-permute-start.15 = (f32[72,512]{1,0:T(8,128)S(1)}, f32[72,512]{1,0:T(8,128)S(1)}, u32[]{:S(2)}, u32[]{:S(2)}) collective-permute-start(f32[72,512]{1,0:T(8,128)S(1)} %add.80.near), channel_id=1, source_target_pairs={{0,3},{1,2},{2,1},{3,0},{4,7},{5,6},{6,5},{7,4},{8,11},{9,10},{10,... | collective-permute-start | bytes 442376 | tf_op jit(solution)/shard_map/ppermute | solution.py:195
  87.1 6.8 %collective-permute-start.17 = (f32[72,512]{1,0:T(8,128)S(1)}, f32[72,512]{1,0:T(8,128)S(1)}, u32[]{:S(2)}, u32[]{:S(2)}) collective-permute-start(f32[72,512]{1,0:T(8,128)S(1)} %add.81), channel_id=1, source_target_pairs={{0,8},{4,12},{8,0},{12,4},{16,24},{20,28},{24,16},{28,20},{1,9},{5... | collective-permute-start | bytes 442376 | tf_op jit(solution)/shard_map/ppermute | solution.py:195
  88.6 8.6 %collective-permute-start.19 = (f32[72,512]{1,0:T(8,128)S(1)}, f32[72,512]{1,0:T(8,128)S(1)}, u32[]{:S(2)}, u32[]{:S(2)}) collective-permute-start(f32[72,512]{1,0:T(8,128)S(1)} %add.81), channel_id=1, source_target_pairs={{0,24},{4,28},{8,16},{12,20},{16,8},{20,12},{24,0},{28,4},{1,25},{... | collective-permute-start | bytes 442376 | tf_op jit(solution)/shard_map/ppermute | solution.py:195
  90.1 8.5 %collective-permute-start.18 = (f32[72,512]{1,0:T(8,128)S(1)}, f32[72,512]{1,0:T(8,128)S(1)}, u32[]{:S(2)}, u32[]{:S(2)}) collective-permute-start(f32[72,512]{1,0:T(8,128)S(1)} %add.81), channel_id=1, source_target_pairs={{0,16},{4,20},{8,24},{12,28},{16,0},{20,4},{24,8},{28,12},{1,17},{... | collective-permute-start | bytes 442376 | tf_op jit(solution)/shard_map/ppermute | solution.py:195
  98.9 1.4 collective-permute-start.20
  101.4 7.0 %collective-permute-start.21 = (f32[72,512]{1,0:T(8,128)S(1)}, f32[72,512]{1,0:T(8,128)S(1)}, u32[]{:S(2)}, u32[]{:S(2)}) collective-permute-start(f32[72,512]{1,0:T(8,128)S(1)} %dest_other.7), channel_id=1, source_target_pairs={{0,1},{1,0},{2,3},{3,2},{4,5},{5,4},{6,7},{7,6},{8,9},{9,8},{10,11... | collective-permute-start | bytes 442376 | tf_op jit(solution)/shard_map/ppermute | solution.py:195
  108.4 7.4 %collective-permute-start.22 = (f32[72,512]{1,0:T(8,128)S(1)}, f32[72,512]{1,0:T(8,128)S(1)}, u32[]{:S(2)}, u32[]{:S(2)}) collective-permute-start(f32[72,512]{1,0:T(8,128)S(1)} %add.84.near), channel_id=1, source_target_pairs={{0,3},{1,2},{2,1},{3,0},{4,7},{5,6},{6,5},{7,4},{8,11},{9,10},{10,... | collective-permute-start | bytes 442376 | tf_op jit(solution)/shard_map/ppermute | solution.py:195
  118.5 6.8 %collective-permute-start.24 = (f32[72,512]{1,0:T(8,128)S(1)}, f32[72,512]{1,0:T(8,128)S(1)}, u32[]{:S(2)}, u32[]{:S(2)}) collective-permute-start(f32[72,512]{1,0:T(8,128)S(1)} %add.85), channel_id=1, source_target_pairs={{0,8},{4,12},{8,0},{12,4},{16,24},{20,28},{24,16},{28,20},{1,9},{5... | collective-permute-start | bytes 442376 | tf_op jit(solution)/shard_map/ppermute | solution.py:195
  120.1 7.6 %collective-permute-start.26 = (f32[72,512]{1,0:T(8,128)S(1)}, f32[72,512]{1,0:T(8,128)S(1)}, u32[]{:S(2)}, u32[]{:S(2)}) collective-permute-start(f32[72,512]{1,0:T(8,128)S(1)} %add.85), channel_id=1, source_target_pairs={{0,24},{4,28},{8,16},{12,20},{16,8},{20,12},{24,0},{28,4},{1,25},{... | collective-permute-start | bytes 442376 | tf_op jit(solution)/shard_map/ppermute | solution.py:195
  120.5 8.5 %collective-permute-start.25 = (f32[72,512]{1,0:T(8,128)S(1)}, f32[72,512]{1,0:T(8,128)S(1)}, u32[]{:S(2)}, u32[]{:S(2)}) collective-permute-start(f32[72,512]{1,0:T(8,128)S(1)} %add.85), channel_id=1, source_target_pairs={{0,16},{4,20},{8,24},{12,28},{16,0},{20,4},{24,8},{28,12},{1,17},{... | collective-permute-start | bytes 442376 | tf_op jit(solution)/shard_map/ppermute | solution.py:195
  129.4 1.4 collective-permute-start.27
  131.8 6.9 %collective-permute-start.28 = (f32[72,512]{1,0:T(8,128)S(1)}, f32[72,512]{1,0:T(8,128)S(1)}, u32[]{:S(2)}, u32[]{:S(2)}) collective-permute-start(f32[72,512]{1,0:T(8,128)S(1)} %dest_other.8), channel_id=1, source_target_pairs={{0,1},{1,0},{2,3},{3,2},{4,5},{5,4},{6,7},{7,6},{8,9},{9,8},{10,11... | collective-permute-start | bytes 442376 | tf_op jit(solution)/shard_map/ppermute | solution.py:195
  138.8 7.4 %collective-permute-start.29 = (f32[72,512]{1,0:T(8,128)S(1)}, f32[72,512]{1,0:T(8,128)S(1)}, u32[]{:S(2)}, u32[]{:S(2)}) collective-permute-start(f32[72,512]{1,0:T(8,128)S(1)} %add.88.near), channel_id=1, source_target_pairs={{0,3},{1,2},{2,1},{3,0},{4,7},{5,6},{6,5},{7,4},{8,11},{9,10},{10,... | collective-permute-start | bytes 442376 | tf_op jit(solution)/shard_map/ppermute | solution.py:195
  148.9 6.8 %collective-permute-start.31 = (f32[72,512]{1,0:T(8,128)S(1)}, f32[72,512]{1,0:T(8,128)S(1)}, u32[]{:S(2)}, u32[]{:S(2)}) collective-permute-start(f32[72,512]{1,0:T(8,128)S(1)} %add.89), channel_id=1, source_target_pairs={{0,8},{4,12},{8,0},{12,4},{16,24},{20,28},{24,16},{28,20},{1,9},{5... | collective-permute-start | bytes 442376 | tf_op jit(solution)/shard_map/ppermute | solution.py:195
  150.5 8.6 %collective-permute-start.33 = (f32[72,512]{1,0:T(8,128)S(1)}, f32[72,512]{1,0:T(8,128)S(1)}, u32[]{:S(2)}, u32[]{:S(2)}) collective-permute-start(f32[72,512]{1,0:T(8,128)S(1)} %add.89), channel_id=1, source_target_pairs={{0,24},{4,28},{8,16},{12,20},{16,8},{20,12},{24,0},{28,4},{1,25},{... | collective-permute-start | bytes 442376 | tf_op jit(solution)/shard_map/ppermute | solution.py:195
  152.0 8.5 %collective-permute-start.32 = (f32[72,512]{1,0:T(8,128)S(1)}, f32[72,512]{1,0:T(8,128)S(1)}, u32[]{:S(2)}, u32[]{:S(2)}) collective-permute-start(f32[72,512]{1,0:T(8,128)S(1)} %add.89), channel_id=1, source_target_pairs={{0,16},{4,20},{8,24},{12,28},{16,0},{20,4},{24,8},{28,12},{1,17},{... | collective-permute-start | bytes 442376 | tf_op jit(solution)/shard_map/ppermute | solution.py:195
  163.3 6.9 %collective-permute-start.35 = (f32[72,512]{1,0:T(8,128)S(1)}, f32[72,512]{1,0:T(8,128)S(1)}, u32[]{:S(2)}, u32[]{:S(2)}) collective-permute-start(f32[72,512]{1,0:T(8,128)S(1)} %dest_other.9), channel_id=1, source_target_pairs={{0,1},{1,0},{2,3},{3,2},{4,5},{5,4},{6,7},{7,6},{8,9},{9,8},{10,11... | collective-permute-start | bytes 442376 | tf_op jit(solution)/shard_map/ppermute | solution.py:195
  170.3 7.4 %collective-permute-start.36 = (f32[72,512]{1,0:T(8,128)S(1)}, f32[72,512]{1,0:T(8,128)S(1)}, u32[]{:S(2)}, u32[]{:S(2)}) collective-permute-start(f32[72,512]{1,0:T(8,128)S(1)} %add.92.near), channel_id=1, source_target_pairs={{0,3},{1,2},{2,1},{3,0},{4,7},{5,6},{6,5},{7,4},{8,11},{9,10},{10,... | collective-permute-start | bytes 442376 | tf_op jit(solution)/shard_map/ppermute | solution.py:195
  180.4 6.8 %collective-permute-start.38 = (f32[72,512]{1,0:T(8,128)S(1)}, f32[72,512]{1,0:T(8,128)S(1)}, u32[]{:S(2)}, u32[]{:S(2)}) collective-permute-start(f32[72,512]{1,0:T(8,128)S(1)} %add.93), channel_id=1, source_target_pairs={{0,8},{4,12},{8,0},{12,4},{16,24},{20,28},{24,16},{28,20},{1,9},{5... | collective-permute-start | bytes 442376 | tf_op jit(solution)/shard_map/ppermute | solution.py:195
  182.0 7.6 %collective-permute-start.40 = (f32[72,512]{1,0:T(8,128)S(1)}, f32[72,512]{1,0:T(8,128)S(1)}, u32[]{:S(2)}, u32[]{:S(2)}) collective-permute-start(f32[72,512]{1,0:T(8,128)S(1)} %add.93), channel_id=1, source_target_pairs={{0,24},{4,28},{8,16},{12,20},{16,8},{20,12},{24,0},{28,4},{1,25},{... | collective-permute-start | bytes 442376 | tf_op jit(solution)/shard_map/ppermute | solution.py:195
  182.4 8.5 %collective-permute-start.39 = (f32[72,512]{1,0:T(8,128)S(1)}, f32[72,512]{1,0:T(8,128)S(1)}, u32[]{:S(2)}, u32[]{:S(2)}) collective-permute-start(f32[72,512]{1,0:T(8,128)S(1)} %add.93), channel_id=1, source_target_pairs={{0,16},{4,20},{8,24},{12,28},{16,0},{20,4},{24,8},{28,12},{1,17},{... | collective-permute-start | bytes 442376 | tf_op jit(solution)/shard_map/ppermute | solution.py:195
  (11 other events, 17.2 us)

commit v4 on v3

--- a/solution.py
+++ b/solution.py
@@ -10,6 +10,7 @@
 SCALE_BLOCK = 128
 SWEEPS = 6
 IN_FLIGHT = 4
+HINT = 10**10
 F32 = jnp.float32
 BF16 = jnp.bfloat16
 HIGHEST = lax.Precision.HIGHEST
@@ -66,7 +67,7 @@
 
 
 def first_kernel(
-    counts, scales, dest, hour, tensor, message, dest_own, hour_gram, hour_t,
+    counts, scales, dest, hour, tensor, message, message_low, dest_own, hour_gram, hour_t,
     buffer, scale_now, dest_now, hour_now, arrived, small_arrived,
 ):
     hours, rows, cols = counts.shape
@@ -104,7 +105,8 @@
         part = lax.dot_general(dest_low, tensor[h], (((1,), (1,)), ((), ())), preferred_element_type=F32)
         part = part * hour_t[:, h : h + 1]
         total = part if total is None else total + part
-    message[: total.shape[0], :] = total
+    message[: total.shape[0], :] = total[:, : rows // 2]
+    message_low[...] = total[:, rows // 2 :]
 
 
 def flip_kernel(tensor, after, flipped):
@@ -112,37 +114,56 @@
         flipped[h] = tensor[h].T
 
 
-def join_kernel(own, other, joined):
+def join_kernel(own, other, upper, lower, joined, stacked):
     size = own.shape[1]
     joined[:, half(False, size)] = own[...]
     joined[:, half(True, size)] = other[...]
-
-
-def anchor_kernel(tensor, anchor, near, far, hour_gram, hour_t, _, anchor_out, low_out, sent):
+    size = upper.shape[1]
+    stacked[:, :size] = upper[...]
+    stacked[:, size:] = lower[...]
+
+
+def add_kernel(left, right, *rest):
+    total = rest[-1]
+    total[...] = left[...] + right[...]
+
+
+def products(low, tensor, rows, cols, hour_t):
+    return hour_sum(
+        [jnp.dot(low, tensor[h, rows, cols], preferred_element_type=F32) for h in range(tensor.shape[0])], hour_t
+    )
+
+
+def updated(factor, totals, gram_part):
+    return factor * totals / jnp.dot(gram_part, factor, precision=HIGHEST, preferred_element_type=F32)
+
+
+def upper_kernel(tensor, anchor, near, far, hour_gram, hour_t, anchor_out, gram_part, gram, sent, kept):
     rank, width = anchor.shape
     message = near[...] + far[...]
-    gram_part = get_gram(message, rank) * hour_gram[...]
-    low = jnp.dot(gram_part, anchor[...], precision=HIGHEST, preferred_element_type=F32)
-    updated = anchor[...] * message[:rank, :] / low
-    anchor_out[...] = updated
-    anchor_low = updated.astype(BF16)
-    low_out[...] = anchor_low
+    gram_part[...] = get_gram(message, rank) * hour_gram[...]
+    anchor_out[...] = updated(anchor[...], message[:rank, :], gram_part[...])
+    low = anchor_out[...].astype(BF16)
     size = tensor.shape[2] // 2
-    cols = half(True, size)
-    sent[:rank, :] = hour_sum(
-        [jnp.dot(anchor_low, tensor[h, :, cols], preferred_element_type=F32) for h in range(tensor.shape[0])], hour_t
-    )
-    put_gram(sent, own_gram(updated))
-
-
-def anchor_kept_kernel(tensor, anchor_low, hour_t, sent, kept):
-    rank = anchor_low.shape[0]
+    sent[...] = products(low, tensor, pl.ds(0, width), half(True, size), hour_t)
+    kept[...] = products(low, tensor, pl.ds(0, width), half(False, size), hour_t)
+    gram[...] = own_gram(anchor_out[...])
+
+
+def lower_kernel(tensor, anchor, near, far, gram_part, hour_t, gram, before, _, anchor_out, sent):
+    rank, width = anchor.shape
+    anchor_out[...] = updated(anchor[...], near[...] + far[...], gram_part[...])
+    low = anchor_out[...].astype(BF16)
     size = tensor.shape[2] // 2
-    cols = half(False, size)
-    low = anchor_low[...]
-    kept[:rank, :] = hour_sum(
-        [jnp.dot(low, tensor[h, :, cols], preferred_element_type=F32) for h in range(tensor.shape[0])], hour_t
-    )
+    sent[:rank, :] = before[...] + products(low, tensor, pl.ds(width, width), half(True, size), hour_t)
+    put_gram(sent, gram[...] + own_gram(anchor_out[...]))
+
+
+def lower_kept_kernel(tensor, anchor, hour_t, before, sent, kept):
+    rank, width = anchor.shape
+    low = anchor[...].astype(BF16)
+    size = tensor.shape[2] // 2
+    kept[:rank, :] = before[...] + products(low, tensor, pl.ds(width, width), half(False, size), hour_t)
     kept[rank:, :] = sent[rank:, :]
 
 
@@ -150,31 +171,31 @@
     rank = dest.shape[0]
     message = near[...] + far[...]
     gram_part = get_gram(message, rank) * hour_gram[...]
-    low = jnp.dot(gram_part, dest[...], precision=HIGHEST, preferred_element_type=F32)
-    dest_out[...] = dest[...] * message[:rank, :] / low
-
-
-def dest_own_kernel(flipped, dest, hour_t, message):
-    rank = dest.shape[0]
-    size = flipped.shape[1] // 2
-    rows = half(False, size)
+    dest_out[...] = updated(dest[...], message[:rank, :], gram_part)
+
+
+def dest_own_kernel(flipped, dest, hour_t, upper, lower, gram):
     low = dest[...].astype(BF16)
-    message[:rank, :] = hour_sum(
-        [jnp.dot(low, flipped[h, rows, :], preferred_element_type=F32) for h in range(flipped.shape[0])], hour_t
-    )
-    put_gram(message, own_gram(dest[...]))
-
-
-def dest_other_kernel(flipped, dest, hour_t, before, message):
-    rank = dest.shape[0]
-    size = flipped.shape[1] // 2
-    rows = half(True, size)
+    rows = half(False, flipped.shape[1] // 2)
+    width = flipped.shape[2] // 2
+    upper[...] = products(low, flipped, rows, pl.ds(0, width), hour_t)
+    lower[...] = products(low, flipped, rows, pl.ds(width, width), hour_t)
+    gram[...] = own_gram(dest[...])
+
+
+def dest_upper_kernel(flipped, dest, hour_t, before, gram, message):
     low = dest[...].astype(BF16)
-    message[:rank, :] = before[:rank, :] + hour_sum(
-        [jnp.dot(low, flipped[h, rows, :], preferred_element_type=F32) for h in range(flipped.shape[0])], hour_t
-    )
-    put_gram(message, own_gram(dest[...]))
-    message[rank:, :] += before[rank:, :]
+    rows = half(True, flipped.shape[1] // 2)
+    width = flipped.shape[2] // 2
+    message[: low.shape[0], :] = before[...] + products(low, flipped, rows, pl.ds(0, width), hour_t)
+    put_gram(message, gram[...] + own_gram(dest[...]))
+
+
+def dest_lower_kernel(flipped, dest, hour_t, before, message):
+    low = dest[...].astype(BF16)
+    rows = half(True, flipped.shape[1] // 2)
+    width = flipped.shape[2] // 2
+    message[...] = before[...] + products(low, flipped, rows, pl.ds(width, width), hour_t)
 
 
 def call(kernel, outs, name, flops, *args):
@@ -195,13 +216,13 @@
     return lax.ppermute(array, axis, [(index, index ^ mask) for index in range(size)])
 
 
-def sum_dest(message):
+def sum_dest(message, *before):
     size = lax.axis_size("dst")
     mask = 1
     while 2 * mask < size:
-        message = message + swap(message, "dst", 2 * mask - 1)
+        message = call(add_kernel, [(message.shape, F32)], "add", HINT, message, swap(message, "dst", mask), *before)
         mask *= 2
-    return message, swap(message, "dst", 2 * mask - 1)
+    return message, swap(message, "dst", mask)
 
 
 def sum_anchor(message):
@@ -219,17 +240,19 @@
     hours, rows, cols = counts.shape
     rank = anchor_factor.shape[0]
     size = cols // 2
-    dest_rows = rank + gram_rows(rank, rows)
+    width = rows // 2
+    dest_rows = rank + gram_rows(rank, width)
     anchor_rows = rank + gram_rows(rank, size)
     half_flops = 2 * 4 * hours * rank * rows * size
 
-    tensor, message, dest_own, hour_gram, hour_t = pl.pallas_call(
+    tensor, message, message_low, dest_own, hour_gram, hour_t = pl.pallas_call(
         first_kernel,
         in_specs=[pl.BlockSpec(memory_space=pl.ANY)] * 4,
-        out_specs=(WHOLE,) * 5,
+        out_specs=(WHOLE,) * 6,
         out_shape=(
             pltpu.VMEM((hours, rows, cols), BF16),
-            pltpu.VMEM((dest_rows, rows), F32),
+            pltpu.VMEM((dest_rows, width), F32),
+            pltpu.VMEM((rank, width), F32),
             pltpu.VMEM((rank, size), F32),
             pltpu.VMEM((rank, rank), F32),
             pltpu.VMEM((rank, hours), F32),
@@ -246,34 +269,46 @@
         name="first",
     )(*[pltpu.with_memory_space_constraint(x, pltpu.HBM) for x in (counts, block_scales, dest_factor, hour_factor)])
 
-    anchor_now = anchor_factor
+    upper, lower = anchor_factor[:, :width], anchor_factor[:, width:]
     for sweep in range(SWEEPS):
         near, far = sum_dest(message)
+        near_low, far_low = sum_dest(message_low)
         if sweep == 0:
             flipped = call(flip_kernel, [((hours, cols, rows), BF16)], "flip", 4 * half_flops, tensor, near)
-        anchor_now, anchor_low, sent = call(
-            anchor_kernel,
-            [((rank, rows), F32), ((rank, rows), BF16), ((anchor_rows, size), F32)],
-            "anchor", half_flops, tensor, anchor_now, near, far, hour_gram, hour_t, flipped,
+        upper, gram_part, gram, sent, kept = call(
+            upper_kernel,
+            [((rank, width), F32), ((rank, rank), F32), ((rank, rank), F32), ((rank, size), F32), ((rank, size), F32)],
+            "upper", half_flops, tensor, upper, near, far, hour_gram, hour_t,
+        )
+        lower, sent = call(
+            lower_kernel, [((rank, width), F32), ((anchor_rows, size), F32)], "lower", half_flops // 2,
+            tensor, lower, near_low, far_low, gram_part, hour_t, gram, sent, flipped,
         )
         received = swap(sent, "org", 1)
         kept = call(
-            anchor_kept_kernel, [((anchor_rows, size), F32)], "anchor_kept", half_flops,
-            tensor, anchor_low, hour_t, sent,
+            lower_kept_kernel, [((anchor_rows, size), F32)], "lower_kept", half_flops // 2,
+            tensor, lower, hour_t, kept, sent,
         )
         near, far = sum_anchor(kept + received)
         dest_own = call(dest_kernel, [((rank, size), F32)], "dest", 0, dest_own, near, far, hour_gram)
         dest_other = swap(dest_own, "org", 1)
         if sweep + 1 < SWEEPS:
-            partial = call(
-                dest_own_kernel, [((dest_rows, rows), F32)], "dest_own", half_flops,
-                flipped, dest_own, hour_t,
+            part, part_low, gram = call(
+                dest_own_kernel, [((rank, width), F32), ((rank, width), F32), ((rank, rank), F32)], "dest_own",
+                half_flops, flipped, dest_own, hour_t,
             )
             message = call(
-                dest_other_kernel, [((dest_rows, rows), F32)], "dest_other", half_flops,
-                flipped, dest_other, hour_t, partial,
+                dest_upper_kernel, [((dest_rows, width), F32)], "dest_upper", half_flops // 2,
+                flipped, dest_other, hour_t, part, gram,
             )
-    return anchor_now, call(join_kernel, [((rank, cols), F32)], "join", 0, dest_own, dest_other)
+            message_low = call(
+                dest_lower_kernel, [((rank, width), F32)], "dest_lower", half_flops // 2,
+                flipped, dest_other, hour_t, part_low,
+            )
+    dest_now, anchor_now = call(
+        join_kernel, [((rank, cols), F32), ((rank, rows), F32)], "join", 0, dest_own, dest_other, upper, lower
+    )
+    return anchor_now, dest_now
 
 
 def solution(mesh):

time: 194 us -> 188 us (0.969)
  waiting for transfers between devices: 99.2 us -> 80.6 us
  starting transfers between devices: 56.1 us -> 66.5 us
  Pallas kernels: 35.2 us -> 38.1 us
    ppermute x42 -> x54, waiting for transfers between devices: 99.2 us -> 80.6 us  [swap(): lax.ppermute(array, axis, [(index, index ^ mask) for index in range(size)])]
    ppermute x42 -> x54, starting transfers between devices: 56.1 us -> 66.5 us  [swap(): lax.ppermute(array, axis, [(index, index ^ mask) for index in range(size)])]
    pallas_call x30 -> x53, Pallas kernels: 27.8 us -> 30.6 us  [call(): pl.pallas_call(kernel, in_specs=[WHOLE] * len(args), out_specs=tuple((WHO...]
  transfers between devices with their start and end apart: 42 -> 54, of which waited for: 42 -> 47; matrix products, arithmetic and copies ran while one was open for 0% -> 0% of each run, Pallas kernels for 6% -> 11%
where the time goes in v4:
time: 188 us
  waiting for transfers between devices  80.6 us (43%)
  starting transfers between devices  66.5 us (35%)
  Pallas kernels  38.1 us (20%)
    ppermute x54, waiting for transfers between devices, swap(): lax.ppermute(array, axis, [(index, index ^ mask) for index in range(size)])  80.6 us
    ppermute x54, starting transfers between devices, swap(): lax.ppermute(array, axis, [(index, index ^ mask) for index in range(size)])  66.5 us
    pallas_call x53, Pallas kernels, call(): pl.pallas_call(kernel, in_specs=[WHOLE] * len(args), out_specs=tuple((WHO...  30.6 us
    pallas_call x1, Pallas kernels, body(): pl.pallas_call(first_kernel, in_specs=[pl.BlockSpec(memory_space=pl.ANY)]...  7.5 us
  transfers between devices with their start and end apart: 54, of which 47 were waited for; matrix products, arithmetic and copies ran while one was open for 0% of the time, Pallas kernels for 11%

profile of v4, /device:TPU:0, one launch (start us, length us, event | category | flops | bytes accessed | tf_op | source)
XLA Modules:
  0.0 188.0 jit_solution(12915140444908978982)
XLA Ops:
  0.6 7.5 %first.1 = (bf16[8,512,1024]{2,1,0:T(8,128)(2,1)S(1)}, f32[80,256]{1,0:T(8,128)S(1)}, f32[64,256]{1,0:T(8,128)S(1)}, f32[64,512]{1,0:T(8,128)S(1)}, f32[64,64]{1,0:T(8,128)S(1)}, /*index=5*/f32[64,8]{1,0:T(8,128)S(1)}) custom-call(s32[8,512,1024]{2,1,0:T(8,128)} %counts.1, f32[8,4,8]{2,1,0:T(4,128)} %scales.1, f32[64,1024]{1,0:T(8,128)} %dest.7, f32[8,64]{1,0:T(8,128)} %hour.1), custom_call_target="tpu_custom_call" | custom-call | tf_op jit(solution)/shard_map/first/pallas_call | solution.py:248
  8.1 3.1 %collective-permute-start = (f32[64,256]{1,0:T(8,128)S(1)}, f32[64,256]{1,0:T(8,128)S(1)}, u32[]{:S(2)}, u32[]{:S(2)}) collective-permute-start(f32[64,256]{1,0:T(8,128)S(1)} %get-tuple-element.69.left), channel_id=1, source_target_pairs={{0,1},{1,0},{2,3},{3,2},{4,5},{5,4},{6,7},{7,6},{8,9},{9,8},{10,11... | collective-permute-start | bytes 196616 | tf_op jit(solution)/shard_map/ppermute | solution.py:216
  11.3 2.3 %collective-permute-done.right = f32[64,256]{1,0:T(8,128)S(1)} collective-permute-done((f32[64,256]{1,0:T(8,128)S(1)}, f32[64,256]{1,0:T(8,128)S(1)}, u32[]{:S(2)}, u32[]{:S(2)}) %collective-permute-start) | collective-permute-done | bytes 65568 | tf_op jit(solution)/shard_map/ppermute | solution.py:216
  13.7 3.5 %collective-permute-start.1 = (f32[64,256]{1,0:T(8,128)S(1)}, f32[64,256]{1,0:T(8,128)S(1)}, u32[]{:S(2)}, u32[]{:S(2)}) collective-permute-start(f32[64,256]{1,0:T(8,128)S(1)} %add.84.near), channel_id=1, source_target_pairs={{0,2},{1,3},{2,0},{3,1},{4,6},{5,7},{6,4},{7,5},{8,10},{9,11},{10,... | collective-permute-start | bytes 196616 | tf_op jit(solution)/shard_map/ppermute | solution.py:216
  19.0 2.2 %flip.1._.flipped = bf16[8,1024,512]{2,1,0:T(8,128)(2,1)S(1)} custom-call(bf16[8,512,1024]{2,1,0:T(8,128)(2,1)S(1)} %get-tuple-element.68.tensor, f32[80,256]{1,0:T(8,128)S(1)} %add.85.near.after), custom_call_target="tpu_custom_call" | custom-call | flops 4294967296 | tf_op jit(solution)/shard_map/flip/pallas_call | solution.py:202
  29.7 3.2 %collective-permute-done.5 = f32[72,512]{1,0:T(8,128)S(1)} collective-permute-done((f32[72,512]{1,0:T(8,128)S(1)}, f32[72,512]{1,0:T(8,128)S(1)}, u32[]{:S(2)}, u32[]{:S(2)}) %collective-permute-start.5) | collective-permute-done | bytes 147488 | tf_op jit(solution)/shard_map/ppermute | solution.py:216
  32.9 3.4 %collective-permute-done.7 = f32[72,512]{1,0:T(8,128)S(1)} collective-permute-done((f32[72,512]{1,0:T(8,128)S(1)}, f32[72,512]{1,0:T(8,128)S(1)}, u32[]{:S(2)}, u32[]{:S(2)}) %collective-permute-start.7) | collective-permute-done | bytes 147488 | tf_op jit(solution)/shard_map/ppermute | solution.py:216
  42.7 2.0 %collective-permute-done.11.right = f32[80,256]{1,0:T(8,128)S(1)} collective-permute-done((f32[80,256]{1,0:T(8,128)S(1)}, f32[80,256]{1,0:T(8,128)S(1)}, u32[]{:S(2)}, u32[]{:S(2)}) %collective-permute-start.11) | collective-permute-done | bytes 81952 | tf_op jit(solution)/shard_map/ppermute | solution.py:216
  44.7 2.5 %collective-permute-start.12 = (f32[80,256]{1,0:T(8,128)S(1)}, f32[80,256]{1,0:T(8,128)S(1)}, u32[]{:S(2)}, u32[]{:S(2)}) collective-permute-start(f32[80,256]{1,0:T(8,128)S(1)} %add.87.near), channel_id=1, source_target_pairs={{0,2},{1,3},{2,0},{3,1},{4,6},{5,7},{6,4},{7,5},{8,10},{9,11},{10,... | collective-permute-start | bytes 245768 | tf_op jit(solution)/shard_map/ppermute | solution.py:216
  47.2 2.2 %collective-permute-start.10 = (f32[64,256]{1,0:T(8,128)S(1)}, f32[64,256]{1,0:T(8,128)S(1)}, u32[]{:S(2)}, u32[]{:S(2)}) collective-permute-start(f32[64,256]{1,0:T(8,128)S(1)} %add.86.near), channel_id=1, source_target_pairs={{0,2},{1,3},{2,0},{3,1},{4,6},{5,7},{6,4},{7,5},{8,10},{9,11},{10,... | collective-permute-start | bytes 196616 | tf_op jit(solution)/shard_map/ppermute | solution.py:216
  59.2 3.2 %collective-permute-done.14 = f32[72,512]{1,0:T(8,128)S(1)} collective-permute-done((f32[72,512]{1,0:T(8,128)S(1)}, f32[72,512]{1,0:T(8,128)S(1)}, u32[]{:S(2)}, u32[]{:S(2)}) %collective-permute-start.14) | collective-permute-done | bytes 147488 | tf_op jit(solution)/shard_map/ppermute | solution.py:216
  62.4 2.4 %collective-permute-done.16 = f32[72,512]{1,0:T(8,128)S(1)} collective-permute-done((f32[72,512]{1,0:T(8,128)S(1)}, f32[72,512]{1,0:T(8,128)S(1)}, u32[]{:S(2)}, u32[]{:S(2)}) %collective-permute-start.16) | collective-permute-done | bytes 147488 | tf_op jit(solution)/shard_map/ppermute | solution.py:216
  71.2 2.1 %collective-permute-done.20.right = f32[80,256]{1,0:T(8,128)S(1)} collective-permute-done((f32[80,256]{1,0:T(8,128)S(1)}, f32[80,256]{1,0:T(8,128)S(1)}, u32[]{:S(2)}, u32[]{:S(2)}) %collective-permute-start.20) | collective-permute-done | bytes 81952 | tf_op jit(solution)/shard_map/ppermute | solution.py:216
  73.3 3.2 %collective-permute-start.21 = (f32[80,256]{1,0:T(8,128)S(1)}, f32[80,256]{1,0:T(8,128)S(1)}, u32[]{:S(2)}, u32[]{:S(2)}) collective-permute-start(f32[80,256]{1,0:T(8,128)S(1)} %add.89.near), channel_id=1, source_target_pairs={{0,2},{1,3},{2,0},{3,1},{4,6},{5,7},{6,4},{7,5},{8,10},{9,11},{10,... | collective-permute-start | bytes 245768 | tf_op jit(solution)/shard_map/ppermute | solution.py:216
  78.4 3.1 %collective-permute-done.21.far = f32[80,256]{1,0:T(8,128)S(1)} collective-permute-done((f32[80,256]{1,0:T(8,128)S(1)}, f32[80,256]{1,0:T(8,128)S(1)}, u32[]{:S(2)}, u32[]{:S(2)}) %collective-permute-start.21) | collective-permute-done | bytes 81952 | tf_op jit(solution)/shard_map/ppermute | solution.py:216
  88.6 3.2 %collective-permute-done.23 = f32[72,512]{1,0:T(8,128)S(1)} collective-permute-done((f32[72,512]{1,0:T(8,128)S(1)}, f32[72,512]{1,0:T(8,128)S(1)}, u32[]{:S(2)}, u32[]{:S(2)}) %collective-permute-start.23) | collective-permute-done | bytes 147488 | tf_op jit(solution)/shard_map/ppermute | solution.py:216
  91.8 3.4 %collective-permute-done.25 = f32[72,512]{1,0:T(8,128)S(1)} collective-permute-done((f32[72,512]{1,0:T(8,128)S(1)}, f32[72,512]{1,0:T(8,128)S(1)}, u32[]{:S(2)}, u32[]{:S(2)}) %collective-permute-start.25) | collective-permute-done | bytes 147488 | tf_op jit(solution)/shard_map/ppermute | solution.py:216
  101.6 2.0 %collective-permute-done.29.right = f32[80,256]{1,0:T(8,128)S(1)} collective-permute-done((f32[80,256]{1,0:T(8,128)S(1)}, f32[80,256]{1,0:T(8,128)S(1)}, u32[]{:S(2)}, u32[]{:S(2)}) %collective-permute-start.29) | collective-permute-done | bytes 81952 | tf_op jit(solution)/shard_map/ppermute | solution.py:216
  103.7 2.9 %collective-permute-start.30 = (f32[80,256]{1,0:T(8,128)S(1)}, f32[80,256]{1,0:T(8,128)S(1)}, u32[]{:S(2)}, u32[]{:S(2)}) collective-permute-start(f32[80,256]{1,0:T(8,128)S(1)} %add.91.near), channel_id=1, source_target_pairs={{0,2},{1,3},{2,0},{3,1},{4,6},{5,7},{6,4},{7,5},{8,10},{9,11},{10,... | collective-permute-start | bytes 245768 | tf_op jit(solution)/shard_map/ppermute | solution.py:216
  106.6 2.2 %collective-permute-start.28 = (f32[64,256]{1,0:T(8,128)S(1)}, f32[64,256]{1,0:T(8,128)S(1)}, u32[]{:S(2)}, u32[]{:S(2)}) collective-permute-start(f32[64,256]{1,0:T(8,128)S(1)} %add.90.near), channel_id=1, source_target_pairs={{0,2},{1,3},{2,0},{3,1},{4,6},{5,7},{6,4},{7,5},{8,10},{9,11},{10,... | collective-permute-start | bytes 196616 | tf_op jit(solution)/shard_map/ppermute | solution.py:216
  118.6 3.2 %collective-permute-done.32 = f32[72,512]{1,0:T(8,128)S(1)} collective-permute-done((f32[72,512]{1,0:T(8,128)S(1)}, f32[72,512]{1,0:T(8,128)S(1)}, u32[]{:S(2)}, u32[]{:S(2)}) %collective-permute-start.32) | collective-permute-done | bytes 147488 | tf_op jit(solution)/shard_map/ppermute | solution.py:216
  121.8 2.4 %collective-permute-done.34 = f32[72,512]{1,0:T(8,128)S(1)} collective-permute-done((f32[72,512]{1,0:T(8,128)S(1)}, f32[72,512]{1,0:T(8,128)S(1)}, u32[]{:S(2)}, u32[]{:S(2)}) %collective-permute-start.34) | collective-permute-done | bytes 147488 | tf_op jit(solution)/shard_map/ppermute | solution.py:216
  130.6 1.9 %collective-permute-done.38.right = f32[80,256]{1,0:T(8,128)S(1)} collective-permute-done((f32[80,256]{1,0:T(8,128)S(1)}, f32[80,256]{1,0:T(8,128)S(1)}, u32[]{:S(2)}, u32[]{:S(2)}) %collective-permute-start.38) | collective-permute-done | bytes 81952 | tf_op jit(solution)/shard_map/ppermute | solution.py:216
  132.6 3.2 %collective-permute-start.39 = (f32[80,256]{1,0:T(8,128)S(1)}, f32[80,256]{1,0:T(8,128)S(1)}, u32[]{:S(2)}, u32[]{:S(2)}) collective-permute-start(f32[80,256]{1,0:T(8,128)S(1)} %add.93.near), channel_id=1, source_target_pairs={{0,2},{1,3},{2,0},{3,1},{4,6},{5,7},{6,4},{7,5},{8,10},{9,11},{10,... | collective-permute-start | bytes 245768 | tf_op jit(solution)/shard_map/ppermute | solution.py:216
  135.7 2.2 %collective-permute-start.37 = (f32[64,256]{1,0:T(8,128)S(1)}, f32[64,256]{1,0:T(8,128)S(1)}, u32[]{:S(2)}, u32[]{:S(2)}) collective-permute-start(f32[64,256]{1,0:T(8,128)S(1)} %add.92.near), channel_id=1, source_target_pairs={{0,2},{1,3},{2,0},{3,1},{4,6},{5,7},{6,4},{7,5},{8,10},{9,11},{10,... | collective-permute-start | bytes 196616 | tf_op jit(solution)/shard_map/ppermute | solution.py:216
  147.7 3.2 %collective-permute-done.41 = f32[72,512]{1,0:T(8,128)S(1)} collective-permute-done((f32[72,512]{1,0:T(8,128)S(1)}, f32[72,512]{1,0:T(8,128)S(1)}, u32[]{:S(2)}, u32[]{:S(2)}) %collective-permute-start.41) | collective-permute-done | bytes 147488 | tf_op jit(solution)/shard_map/ppermute | solution.py:216
  150.9 3.5 %collective-permute-done.43 = f32[72,512]{1,0:T(8,128)S(1)} collective-permute-done((f32[72,512]{1,0:T(8,128)S(1)}, f32[72,512]{1,0:T(8,128)S(1)}, u32[]{:S(2)}, u32[]{:S(2)}) %collective-permute-start.43) | collective-permute-done | bytes 147488 | tf_op jit(solution)/shard_map/ppermute | solution.py:216
  160.8 1.9 %collective-permute-done.47.right = f32[80,256]{1,0:T(8,128)S(1)} collective-permute-done((f32[80,256]{1,0:T(8,128)S(1)}, f32[80,256]{1,0:T(8,128)S(1)}, u32[]{:S(2)}, u32[]{:S(2)}) %collective-permute-start.47) | collective-permute-done | bytes 81952 | tf_op jit(solution)/shard_map/ppermute | solution.py:216
  162.7 3.2 %collective-permute-start.48 = (f32[80,256]{1,0:T(8,128)S(1)}, f32[80,256]{1,0:T(8,128)S(1)}, u32[]{:S(2)}, u32[]{:S(2)}) collective-permute-start(f32[80,256]{1,0:T(8,128)S(1)} %add.95.near), channel_id=1, source_target_pairs={{0,2},{1,3},{2,0},{3,1},{4,6},{5,7},{6,4},{7,5},{8,10},{9,11},{10,... | collective-permute-start | bytes 245768 | tf_op jit(solution)/shard_map/ppermute | solution.py:216
  165.9 2.2 %collective-permute-start.46 = (f32[64,256]{1,0:T(8,128)S(1)}, f32[64,256]{1,0:T(8,128)S(1)}, u32[]{:S(2)}, u32[]{:S(2)}) collective-permute-start(f32[64,256]{1,0:T(8,128)S(1)} %add.94.near), channel_id=1, source_target_pairs={{0,2},{1,3},{2,0},{3,1},{4,6},{5,7},{6,4},{7,5},{8,10},{9,11},{10,... | collective-permute-start | bytes 196616 | tf_op jit(solution)/shard_map/ppermute | solution.py:216
  177.9 3.2 %collective-permute-done.50 = f32[72,512]{1,0:T(8,128)S(1)} collective-permute-done((f32[72,512]{1,0:T(8,128)S(1)}, f32[72,512]{1,0:T(8,128)S(1)}, u32[]{:S(2)}, u32[]{:S(2)}) %collective-permute-start.50) | collective-permute-done | bytes 147488 | tf_op jit(solution)/shard_map/ppermute | solution.py:216
  181.1 2.4 %collective-permute-done.52 = f32[72,512]{1,0:T(8,128)S(1)} collective-permute-done((f32[72,512]{1,0:T(8,128)S(1)}, f32[72,512]{1,0:T(8,128)S(1)}, u32[]{:S(2)}, u32[]{:S(2)}) %collective-permute-start.52) | collective-permute-done | bytes 147488 | tf_op jit(solution)/shard_map/ppermute | solution.py:216
  (153 shorter events, 95.0 us)
Async XLA Ops:
  11.2 5.9 %collective-permute-start.2 = (f32[80,256]{1,0:T(8,128)S(1)}, f32[80,256]{1,0:T(8,128)S(1)}, u32[]{:S(2)}, u32[]{:S(2)}) collective-permute-start(f32[80,256]{1,0:T(8,128)S(1)} %get-tuple-element.70.left), channel_id=1, source_target_pairs={{0,1},{1,0},{2,3},{3,2},{4,5},{5,4},{6,7},{7,6},{8,9},{9,8},{10,11... | collective-permute-start | bytes 245768 | tf_op jit(solution)/shard_map/ppermute | solution.py:216
  13.7 10.2 %collective-permute-start.1 = (f32[64,256]{1,0:T(8,128)S(1)}, f32[64,256]{1,0:T(8,128)S(1)}, u32[]{:S(2)}, u32[]{:S(2)}) collective-permute-start(f32[64,256]{1,0:T(8,128)S(1)} %add.84.near), channel_id=1, source_target_pairs={{0,2},{1,3},{2,0},{3,1},{4,6},{5,7},{6,4},{7,5},{8,10},{9,11},{10,... | collective-permute-start | bytes 196616 | tf_op jit(solution)/shard_map/ppermute | solution.py:216
  26.1 6.8 %collective-permute-start.5 = (f32[72,512]{1,0:T(8,128)S(1)}, f32[72,512]{1,0:T(8,128)S(1)}, u32[]{:S(2)}, u32[]{:S(2)}) collective-permute-start(f32[72,512]{1,0:T(8,128)S(1)} %add.66), channel_id=1, source_target_pairs={{0,8},{4,12},{8,0},{12,4},{16,24},{20,28},{24,16},{28,20},{1,9},{5... | collective-permute-start | bytes 442376 | tf_op jit(solution)/shard_map/ppermute | solution.py:216
  27.7 8.6 %collective-permute-start.7 = (f32[72,512]{1,0:T(8,128)S(1)}, f32[72,512]{1,0:T(8,128)S(1)}, u32[]{:S(2)}, u32[]{:S(2)}) collective-permute-start(f32[72,512]{1,0:T(8,128)S(1)} %add.66), channel_id=1, source_target_pairs={{0,24},{4,28},{8,16},{12,20},{16,8},{20,12},{24,0},{28,4},{1,25},{... | collective-permute-start | bytes 442376 | tf_op jit(solution)/shard_map/ppermute | solution.py:216
  29.2 8.5 %collective-permute-start.6 = (f32[72,512]{1,0:T(8,128)S(1)}, f32[72,512]{1,0:T(8,128)S(1)}, u32[]{:S(2)}, u32[]{:S(2)}) collective-permute-start(f32[72,512]{1,0:T(8,128)S(1)} %add.66), channel_id=1, source_target_pairs={{0,16},{4,20},{8,24},{12,28},{16,0},{20,4},{24,8},{28,12},{1,17},{... | collective-permute-start | bytes 442376 | tf_op jit(solution)/shard_map/ppermute | solution.py:216
  44.7 5.9 %collective-permute-start.12 = (f32[80,256]{1,0:T(8,128)S(1)}, f32[80,256]{1,0:T(8,128)S(1)}, u32[]{:S(2)}, u32[]{:S(2)}) collective-permute-start(f32[80,256]{1,0:T(8,128)S(1)} %add.87.near), channel_id=1, source_target_pairs={{0,2},{1,3},{2,0},{3,1},{4,6},{5,7},{6,4},{7,5},{8,10},{9,11},{10,... | collective-permute-start | bytes 245768 | tf_op jit(solution)/shard_map/ppermute | solution.py:216
  47.2 6.1 %collective-permute-start.10 = (f32[64,256]{1,0:T(8,128)S(1)}, f32[64,256]{1,0:T(8,128)S(1)}, u32[]{:S(2)}, u32[]{:S(2)}) collective-permute-start(f32[64,256]{1,0:T(8,128)S(1)} %add.86.near), channel_id=1, source_target_pairs={{0,2},{1,3},{2,0},{3,1},{4,6},{5,7},{6,4},{7,5},{8,10},{9,11},{10,... | collective-permute-start | bytes 196616 | tf_op jit(solution)/shard_map/ppermute | solution.py:216
  55.6 6.8 %collective-permute-start.14 = (f32[72,512]{1,0:T(8,128)S(1)}, f32[72,512]{1,0:T(8,128)S(1)}, u32[]{:S(2)}, u32[]{:S(2)}) collective-permute-start(f32[72,512]{1,0:T(8,128)S(1)} %add.69), channel_id=1, source_target_pairs={{0,8},{4,12},{8,0},{12,4},{16,24},{20,28},{24,16},{28,20},{1,9},{5... | collective-permute-start | bytes 442376 | tf_op jit(solution)/shard_map/ppermute | solution.py:216
  57.2 7.6 %collective-permute-start.16 = (f32[72,512]{1,0:T(8,128)S(1)}, f32[72,512]{1,0:T(8,128)S(1)}, u32[]{:S(2)}, u32[]{:S(2)}) collective-permute-start(f32[72,512]{1,0:T(8,128)S(1)} %add.69), channel_id=1, source_target_pairs={{0,24},{4,28},{8,16},{12,20},{16,8},{20,12},{24,0},{28,4},{1,25},{... | collective-permute-start | bytes 442376 | tf_op jit(solution)/shard_map/ppermute | solution.py:216
  57.7 8.5 %collective-permute-start.15 = (f32[72,512]{1,0:T(8,128)S(1)}, f32[72,512]{1,0:T(8,128)S(1)}, u32[]{:S(2)}, u32[]{:S(2)}) collective-permute-start(f32[72,512]{1,0:T(8,128)S(1)} %add.69), channel_id=1, source_target_pairs={{0,16},{4,20},{8,24},{12,28},{16,0},{20,4},{24,8},{28,12},{1,17},{... | collective-permute-start | bytes 442376 | tf_op jit(solution)/shard_map/ppermute | solution.py:216
  70.6 5.8 %collective-permute-start.18 = (f32[64,256]{1,0:T(8,128)S(1)}, f32[64,256]{1,0:T(8,128)S(1)}, u32[]{:S(2)}, u32[]{:S(2)}) collective-permute-start(f32[64,256]{1,0:T(8,128)S(1)} %dest_lower.6.left), channel_id=1, source_target_pairs={{0,1},{1,0},{2,3},{3,2},{4,5},{5,4},{6,7},{7,6},{8,9},{9,8},{10,11... | collective-permute-start | bytes 196616 | tf_op jit(solution)/shard_map/ppermute | solution.py:216
  73.3 8.2 %collective-permute-start.21 = (f32[80,256]{1,0:T(8,128)S(1)}, f32[80,256]{1,0:T(8,128)S(1)}, u32[]{:S(2)}, u32[]{:S(2)}) collective-permute-start(f32[80,256]{1,0:T(8,128)S(1)} %add.89.near), channel_id=1, source_target_pairs={{0,2},{1,3},{2,0},{3,1},{4,6},{5,7},{6,4},{7,5},{8,10},{9,11},{10,... | collective-permute-start | bytes 245768 | tf_op jit(solution)/shard_map/ppermute | solution.py:216
  76.5 6.3 %collective-permute-start.19 = (f32[64,256]{1,0:T(8,128)S(1)}, f32[64,256]{1,0:T(8,128)S(1)}, u32[]{:S(2)}, u32[]{:S(2)}) collective-permute-start(f32[64,256]{1,0:T(8,128)S(1)} %add.88.near), channel_id=1, source_target_pairs={{0,2},{1,3},{2,0},{3,1},{4,6},{5,7},{6,4},{7,5},{8,10},{9,11},{10,... | collective-permute-start | bytes 196616 | tf_op jit(solution)/shard_map/ppermute | solution.py:216
  85.0 6.8 %collective-permute-start.23 = (f32[72,512]{1,0:T(8,128)S(1)}, f32[72,512]{1,0:T(8,128)S(1)}, u32[]{:S(2)}, u32[]{:S(2)}) collective-permute-start(f32[72,512]{1,0:T(8,128)S(1)} %add.72), channel_id=1, source_target_pairs={{0,8},{4,12},{8,0},{12,4},{16,24},{20,28},{24,16},{28,20},{1,9},{5... | collective-permute-start | bytes 442376 | tf_op jit(solution)/shard_map/ppermute | solution.py:216
  86.6 8.6 %collective-permute-start.25 = (f32[72,512]{1,0:T(8,128)S(1)}, f32[72,512]{1,0:T(8,128)S(1)}, u32[]{:S(2)}, u32[]{:S(2)}) collective-permute-start(f32[72,512]{1,0:T(8,128)S(1)} %add.72), channel_id=1, source_target_pairs={{0,24},{4,28},{8,16},{12,20},{16,8},{20,12},{24,0},{28,4},{1,25},{... | collective-permute-start | bytes 442376 | tf_op jit(solution)/shard_map/ppermute | solution.py:216
  88.1 8.5 %collective-permute-start.24 = (f32[72,512]{1,0:T(8,128)S(1)}, f32[72,512]{1,0:T(8,128)S(1)}, u32[]{:S(2)}, u32[]{:S(2)}) collective-permute-start(f32[72,512]{1,0:T(8,128)S(1)} %add.72), channel_id=1, source_target_pairs={{0,16},{4,20},{8,24},{12,28},{16,0},{20,4},{24,8},{28,12},{1,17},{... | collective-permute-start | bytes 442376 | tf_op jit(solution)/shard_map/ppermute | solution.py:216
  100.9 5.7 %collective-permute-start.27 = (f32[64,256]{1,0:T(8,128)S(1)}, f32[64,256]{1,0:T(8,128)S(1)}, u32[]{:S(2)}, u32[]{:S(2)}) collective-permute-start(f32[64,256]{1,0:T(8,128)S(1)} %dest_lower.7.left), channel_id=1, source_target_pairs={{0,1},{1,0},{2,3},{3,2},{4,5},{5,4},{6,7},{7,6},{8,9},{9,8},{10,11... | collective-permute-start | bytes 196616 | tf_op jit(solution)/shard_map/ppermute | solution.py:216
  103.7 6.3 %collective-permute-start.30 = (f32[80,256]{1,0:T(8,128)S(1)}, f32[80,256]{1,0:T(8,128)S(1)}, u32[]{:S(2)}, u32[]{:S(2)}) collective-permute-start(f32[80,256]{1,0:T(8,128)S(1)} %add.91.near), channel_id=1, source_target_pairs={{0,2},{1,3},{2,0},{3,1},{4,6},{5,7},{6,4},{7,5},{8,10},{9,11},{10,... | collective-permute-start | bytes 245768 | tf_op jit(solution)/shard_map/ppermute | solution.py:216
  106.6 6.1 %collective-permute-start.28 = (f32[64,256]{1,0:T(8,128)S(1)}, f32[64,256]{1,0:T(8,128)S(1)}, u32[]{:S(2)}, u32[]{:S(2)}) collective-permute-start(f32[64,256]{1,0:T(8,128)S(1)} %add.90.near), channel_id=1, source_target_pairs={{0,2},{1,3},{2,0},{3,1},{4,6},{5,7},{6,4},{7,5},{8,10},{9,11},{10,... | collective-permute-start | bytes 196616 | tf_op jit(solution)/shard_map/ppermute | solution.py:216
  115.0 6.8 %collective-permute-start.32 = (f32[72,512]{1,0:T(8,128)S(1)}, f32[72,512]{1,0:T(8,128)S(1)}, u32[]{:S(2)}, u32[]{:S(2)}) collective-permute-start(f32[72,512]{1,0:T(8,128)S(1)} %add.75), channel_id=1, source_target_pairs={{0,8},{4,12},{8,0},{12,4},{16,24},{20,28},{24,16},{28,20},{1,9},{5... | collective-permute-start | bytes 442376 | tf_op jit(solution)/shard_map/ppermute | solution.py:216
  116.6 7.6 %collective-permute-start.34 = (f32[72,512]{1,0:T(8,128)S(1)}, f32[72,512]{1,0:T(8,128)S(1)}, u32[]{:S(2)}, u32[]{:S(2)}) collective-permute-start(f32[72,512]{1,0:T(8,128)S(1)} %add.75), channel_id=1, source_target_pairs={{0,24},{4,28},{8,16},{12,20},{16,8},{20,12},{24,0},{28,4},{1,25},{... | collective-permute-start | bytes 442376 | tf_op jit(solution)/shard_map/ppermute | solution.py:216
  117.1 8.5 %collective-permute-start.33 = (f32[72,512]{1,0:T(8,128)S(1)}, f32[72,512]{1,0:T(8,128)S(1)}, u32[]{:S(2)}, u32[]{:S(2)}) collective-permute-start(f32[72,512]{1,0:T(8,128)S(1)} %add.75), channel_id=1, source_target_pairs={{0,16},{4,20},{8,24},{12,28},{16,0},{20,4},{24,8},{28,12},{1,17},{... | collective-permute-start | bytes 442376 | tf_op jit(solution)/shard_map/ppermute | solution.py:216
  132.6 6.5 %collective-permute-start.39 = (f32[80,256]{1,0:T(8,128)S(1)}, f32[80,256]{1,0:T(8,128)S(1)}, u32[]{:S(2)}, u32[]{:S(2)}) collective-permute-start(f32[80,256]{1,0:T(8,128)S(1)} %add.93.near), channel_id=1, source_target_pairs={{0,2},{1,3},{2,0},{3,1},{4,6},{5,7},{6,4},{7,5},{8,10},{9,11},{10,... | collective-permute-start | bytes 245768 | tf_op jit(solution)/shard_map/ppermute | solution.py:216
  135.7 6.1 %collective-permute-start.37 = (f32[64,256]{1,0:T(8,128)S(1)}, f32[64,256]{1,0:T(8,128)S(1)}, u32[]{:S(2)}, u32[]{:S(2)}) collective-permute-start(f32[64,256]{1,0:T(8,128)S(1)} %add.92.near), channel_id=1, source_target_pairs={{0,2},{1,3},{2,0},{3,1},{4,6},{5,7},{6,4},{7,5},{8,10},{9,11},{10,... | collective-permute-start | bytes 196616 | tf_op jit(solution)/shard_map/ppermute | solution.py:216
  144.1 6.7 %collective-permute-start.41 = (f32[72,512]{1,0:T(8,128)S(1)}, f32[72,512]{1,0:T(8,128)S(1)}, u32[]{:S(2)}, u32[]{:S(2)}) collective-permute-start(f32[72,512]{1,0:T(8,128)S(1)} %add.78), channel_id=1, source_target_pairs={{0,8},{4,12},{8,0},{12,4},{16,24},{20,28},{24,16},{28,20},{1,9},{5... | collective-permute-start | bytes 442376 | tf_op jit(solution)/shard_map/ppermute | solution.py:216
  145.7 8.7 %collective-permute-start.43 = (f32[72,512]{1,0:T(8,128)S(1)}, f32[72,512]{1,0:T(8,128)S(1)}, u32[]{:S(2)}, u32[]{:S(2)}) collective-permute-start(f32[72,512]{1,0:T(8,128)S(1)} %add.78), channel_id=1, source_target_pairs={{0,24},{4,28},{8,16},{12,20},{16,8},{20,12},{24,0},{28,4},{1,25},{... | collective-permute-start | bytes 442376 | tf_op jit(solution)/shard_map/ppermute | solution.py:216
  147.2 8.6 %collective-permute-start.42 = (f32[72,512]{1,0:T(8,128)S(1)}, f32[72,512]{1,0:T(8,128)S(1)}, u32[]{:S(2)}, u32[]{:S(2)}) collective-permute-start(f32[72,512]{1,0:T(8,128)S(1)} %add.78), channel_id=1, source_target_pairs={{0,16},{4,20},{8,24},{12,28},{16,0},{20,4},{24,8},{28,12},{1,17},{... | collective-permute-start | bytes 442376 | tf_op jit(solution)/shard_map/ppermute | solution.py:216
  162.7 6.5 %collective-permute-start.48 = (f32[80,256]{1,0:T(8,128)S(1)}, f32[80,256]{1,0:T(8,128)S(1)}, u32[]{:S(2)}, u32[]{:S(2)}) collective-permute-start(f32[80,256]{1,0:T(8,128)S(1)} %add.95.near), channel_id=1, source_target_pairs={{0,2},{1,3},{2,0},{3,1},{4,6},{5,7},{6,4},{7,5},{8,10},{9,11},{10,... | collective-permute-start | bytes 245768 | tf_op jit(solution)/shard_map/ppermute | solution.py:216
  165.9 6.1 %collective-permute-start.46 = (f32[64,256]{1,0:T(8,128)S(1)}, f32[64,256]{1,0:T(8,128)S(1)}, u32[]{:S(2)}, u32[]{:S(2)}) collective-permute-start(f32[64,256]{1,0:T(8,128)S(1)} %add.94.near), channel_id=1, source_target_pairs={{0,2},{1,3},{2,0},{3,1},{4,6},{5,7},{6,4},{7,5},{8,10},{9,11},{10,... | collective-permute-start | bytes 196616 | tf_op jit(solution)/shard_map/ppermute | solution.py:216
  174.3 6.8 %collective-permute-start.50 = (f32[72,512]{1,0:T(8,128)S(1)}, f32[72,512]{1,0:T(8,128)S(1)}, u32[]{:S(2)}, u32[]{:S(2)}) collective-permute-start(f32[72,512]{1,0:T(8,128)S(1)} %add.81), channel_id=1, source_target_pairs={{0,8},{4,12},{8,0},{12,4},{16,24},{20,28},{24,16},{28,20},{1,9},{5... | collective-permute-start | bytes 442376 | tf_op jit(solution)/shard_map/ppermute | solution.py:216
  175.9 7.6 %collective-permute-start.52 = (f32[72,512]{1,0:T(8,128)S(1)}, f32[72,512]{1,0:T(8,128)S(1)}, u32[]{:S(2)}, u32[]{:S(2)}) collective-permute-start(f32[72,512]{1,0:T(8,128)S(1)} %add.81), channel_id=1, source_target_pairs={{0,24},{4,28},{8,16},{12,20},{16,8},{20,12},{24,0},{28,4},{1,25},{... | collective-permute-start | bytes 442376 | tf_op jit(solution)/shard_map/ppermute | solution.py:216
  176.4 8.5 %collective-permute-start.51 = (f32[72,512]{1,0:T(8,128)S(1)}, f32[72,512]{1,0:T(8,128)S(1)}, u32[]{:S(2)}, u32[]{:S(2)}) collective-permute-start(f32[72,512]{1,0:T(8,128)S(1)} %add.81), channel_id=1, source_target_pairs={{0,16},{4,20},{8,24},{12,28},{16,0},{20,4},{24,8},{28,12},{1,17},{... | collective-permute-start | bytes 442376 | tf_op jit(solution)/shard_map/ppermute | solution.py:216
  (23 other events, 77.8 us)

commit v5 on v4

--- a/solution.py
+++ b/solution.py
@@ -13,9 +13,9 @@
 HINT = 10**10
 F32 = jnp.float32
 BF16 = jnp.bfloat16
-HIGHEST = lax.Precision.HIGHEST
 
 WHOLE = pl.BlockSpec(memory_space=pltpu.VMEM)
+ANYWHERE = pl.BlockSpec(memory_space=pl.ANY)
 PARAMS = pltpu.CompilerParams(vmem_limit_bytes=8 * 2**20)
 
 
@@ -48,8 +48,27 @@
     )
 
 
+def parts_of(array):
+    high = array.astype(BF16)
+    return high, (array - high.astype(F32)).astype(BF16)
+
+
 def own_gram(factor):
-    return lax.dot_general(factor, factor, (((1,), (1,)), ((), ())), precision=HIGHEST, preferred_element_type=F32)
+    def dot(left, right):
+        return lax.dot_general(left, right, (((1,), (1,)), ((), ())), preferred_element_type=F32)
+
+    high, low = parts_of(factor)
+    return dot(high, high) + (dot(high, low) + dot(low, high))
+
+
+def times(left, right):
+    left_high, left_low = parts_of(left)
+    right_high, right_low = parts_of(right)
+    return jnp.dot(
+        jnp.concatenate([left_high, left_low, left_high], axis=1),
+        jnp.concatenate([right_high, right_high, right_low], axis=0),
+        preferred_element_type=F32,
+    )
 
 
 def half(flip, size):
@@ -114,13 +133,30 @@
         flipped[h] = tensor[h].T
 
 
-def join_kernel(own, other, upper, lower, joined, stacked):
-    size = own.shape[1]
-    joined[:, half(False, size)] = own[...]
-    joined[:, half(True, size)] = other[...]
-    size = upper.shape[1]
-    stacked[:, :size] = upper[...]
-    stacked[:, size:] = lower[...]
+def store(copies, done):
+    started = [
+        pltpu.make_async_copy(source, target, done.at[index]) for index, (source, target) in enumerate(copies)
+    ]
+    for copy in started:
+        copy.start()
+    for copy in started:
+        copy.wait()
+
+
+def store_own_kernel(upper, lower, own, anchor_out, dest_out, done):
+    width = upper.shape[1]
+    store(
+        (
+            (upper, anchor_out.at[:, pl.ds(0, width)]),
+            (lower, anchor_out.at[:, pl.ds(width, width)]),
+            (own, dest_out.at[:, half(False, own.shape[1])]),
+        ),
+        done,
+    )
+
+
+def store_other_kernel(other, _, dest_out, done):
+    store(((other, dest_out.at[:, half(True, other.shape[1])]),), done)
 
 
 def add_kernel(left, right, *rest):
@@ -135,7 +171,7 @@
 
 
 def updated(factor, totals, gram_part):
-    return factor * totals / jnp.dot(gram_part, factor, precision=HIGHEST, preferred_element_type=F32)
+    return factor * totals / times(gram_part, factor)
 
 
 def upper_kernel(tensor, anchor, near, far, hour_gram, hour_t, anchor_out, gram_part, gram, sent, kept):
@@ -247,7 +283,7 @@
 
     tensor, message, message_low, dest_own, hour_gram, hour_t = pl.pallas_call(
         first_kernel,
-        in_specs=[pl.BlockSpec(memory_space=pl.ANY)] * 4,
+        in_specs=[ANYWHERE] * 4,
         out_specs=(WHOLE,) * 6,
         out_shape=(
             pltpu.VMEM((hours, rows, cols), BF16),
@@ -305,9 +341,25 @@
                 dest_lower_kernel, [((rank, width), F32)], "dest_lower", half_flops // 2,
                 flipped, dest_other, hour_t, part_low,
             )
-    dest_now, anchor_now = call(
-        join_kernel, [((rank, cols), F32), ((rank, rows), F32)], "join", 0, dest_own, dest_other, upper, lower
-    )
+    anchor_now, dest_now = pl.pallas_call(
+        store_own_kernel,
+        in_specs=[WHOLE] * 3,
+        out_specs=(ANYWHERE,) * 2,
+        out_shape=(pltpu.HBM((rank, rows), F32), pltpu.HBM((rank, cols), F32)),
+        scratch_shapes=[pltpu.SemaphoreType.DMA((3,))],
+        compiler_params=PARAMS,
+        name="store_own",
+    )(in_vmem(upper), in_vmem(lower), in_vmem(dest_own))
+    dest_now = pl.pallas_call(
+        store_other_kernel,
+        in_specs=[WHOLE, ANYWHERE],
+        out_specs=ANYWHERE,
+        out_shape=pltpu.HBM((rank, cols), F32),
+        scratch_shapes=[pltpu.SemaphoreType.DMA((1,))],
+        input_output_aliases={1: 0},
+        compiler_params=PARAMS,
+        name="store_other",
+    )(in_vmem(dest_other), pltpu.with_memory_space_constraint(dest_now, pltpu.HBM))
     return anchor_now, dest_now
 
 

time: 188 us -> 186 us (0.989)
    pallas_call x53 -> x52, Pallas kernels: 30.6 us -> 29 us  [call(): pl.pallas_call(kernel, in_specs=[WHOLE] * len(args), out_specs=tuple((WHO...]
    pallas_call x1 -> x3, Pallas kernels: 7.5 us -> 8.7 us  [the longest x1 7.31 us: body(): pl.pallas_call(first_kernel, in_specs=[ANYWHERE] * 4, out_specs=(WHOLE,)...]
where the time goes in v5:
time: 186 us
  waiting for transfers between devices  79.4 us (43%)
  starting transfers between devices  67 us (36%)
  Pallas kernels  37.7 us (20%)
    ppermute x54, waiting for transfers between devices, swap(): lax.ppermute(array, axis, [(index, index ^ mask) for index in range(size)])  79.4 us
    ppermute x54, starting transfers between devices, swap(): lax.ppermute(array, axis, [(index, index ^ mask) for index in range(size)])  67 us
    pallas_call x52, Pallas kernels, call(): pl.pallas_call(kernel, in_specs=[WHOLE] * len(args), out_specs=tuple((WHO...  29 us
    pallas_call x1, Pallas kernels, body(): pl.pallas_call(first_kernel, in_specs=[ANYWHERE] * 4, out_specs=(WHOLE,)...  7.31 us
  transfers between devices with their start and end apart: 54, of which 47 were waited for; matrix products, arithmetic and copies ran while one was open for 0% of the time, Pallas kernels for 11%

profile of v5, /device:TPU:0, one launch (start us, length us, event | category | flops | bytes accessed | tf_op | source)
XLA Modules:
  0.0 185.8 jit_solution(4098482057293189818)
XLA Ops:
  0.6 7.3 %first.1 = (bf16[8,512,1024]{2,1,0:T(8,128)(2,1)S(1)}, f32[80,256]{1,0:T(8,128)S(1)}, f32[64,256]{1,0:T(8,128)S(1)}, f32[64,512]{1,0:T(8,128)S(1)}, f32[64,64]{1,0:T(8,128)S(1)}, /*index=5*/f32[64,8]{1,0:T(8,128)S(1)}) custom-call(s32[8,512,1024]{2,1,0:T(8,128)} %counts.1, f32[8,4,8]{2,1,0:T(4,128)} %scales.1, f32[64,1024]{1,0:T(8,128)} %dest.7, f32[8,64]{1,0:T(8,128)} %hour.1), custom_call_target="tpu_custom_call" | custom-call | tf_op jit(solution)/shard_map/first/pallas_call | solution.py:284
  8.0 3.1 %collective-permute-start.2 = (f32[64,256]{1,0:T(8,128)S(1)}, f32[64,256]{1,0:T(8,128)S(1)}, u32[]{:S(2)}, u32[]{:S(2)}) collective-permute-start(f32[64,256]{1,0:T(8,128)S(1)} %get-tuple-element.73.left), channel_id=1, source_target_pairs={{0,1},{1,0},{2,3},{3,2},{4,5},{5,4},{6,7},{7,6},{8,9},{9,8},{10,11... | collective-permute-start | bytes 196616 | tf_op jit(solution)/shard_map/ppermute | solution.py:252
  11.1 2.3 %collective-permute-done.2.right = f32[64,256]{1,0:T(8,128)S(1)} collective-permute-done((f32[64,256]{1,0:T(8,128)S(1)}, f32[64,256]{1,0:T(8,128)S(1)}, u32[]{:S(2)}, u32[]{:S(2)}) %collective-permute-start.2) | collective-permute-done | bytes 65568 | tf_op jit(solution)/shard_map/ppermute | solution.py:252
  13.5 3.5 %collective-permute-start.3 = (f32[64,256]{1,0:T(8,128)S(1)}, f32[64,256]{1,0:T(8,128)S(1)}, u32[]{:S(2)}, u32[]{:S(2)}) collective-permute-start(f32[64,256]{1,0:T(8,128)S(1)} %add.85.near), channel_id=1, source_target_pairs={{0,2},{1,3},{2,0},{3,1},{4,6},{5,7},{6,4},{7,5},{8,10},{9,11},{10,... | collective-permute-start | bytes 196616 | tf_op jit(solution)/shard_map/ppermute | solution.py:252
  17.0 1.8 collective-permute-start.1
  18.8 2.2 %flip.1._.flipped = bf16[8,1024,512]{2,1,0:T(8,128)(2,1)S(1)} custom-call(bf16[8,512,1024]{2,1,0:T(8,128)(2,1)S(1)} %get-tuple-element.67.tensor, f32[80,256]{1,0:T(8,128)S(1)} %add.84.near.after), custom_call_target="tpu_custom_call" | custom-call | flops 4294967296 | tf_op jit(solution)/shard_map/flip/pallas_call | solution.py:238
  29.3 3.2 %collective-permute-done.5 = f32[72,512]{1,0:T(8,128)S(1)} collective-permute-done((f32[72,512]{1,0:T(8,128)S(1)}, f32[72,512]{1,0:T(8,128)S(1)}, u32[]{:S(2)}, u32[]{:S(2)}) %collective-permute-start.5) | collective-permute-done | bytes 147488 | tf_op jit(solution)/shard_map/ppermute | solution.py:252
  32.6 3.4 %collective-permute-done.7 = f32[72,512]{1,0:T(8,128)S(1)} collective-permute-done((f32[72,512]{1,0:T(8,128)S(1)}, f32[72,512]{1,0:T(8,128)S(1)}, u32[]{:S(2)}, u32[]{:S(2)}) %collective-permute-start.7) | collective-permute-done | bytes 147488 | tf_op jit(solution)/shard_map/ppermute | solution.py:252
  42.3 2.0 %collective-permute-done.9.right = f32[80,256]{1,0:T(8,128)S(1)} collective-permute-done((f32[80,256]{1,0:T(8,128)S(1)}, f32[80,256]{1,0:T(8,128)S(1)}, u32[]{:S(2)}, u32[]{:S(2)}) %collective-permute-start.9) | collective-permute-done | bytes 81952 | tf_op jit(solution)/shard_map/ppermute | solution.py:252
  44.3 2.5 %collective-permute-start.10 = (f32[80,256]{1,0:T(8,128)S(1)}, f32[80,256]{1,0:T(8,128)S(1)}, u32[]{:S(2)}, u32[]{:S(2)}) collective-permute-start(f32[80,256]{1,0:T(8,128)S(1)} %add.86.near), channel_id=1, source_target_pairs={{0,2},{1,3},{2,0},{3,1},{4,6},{5,7},{6,4},{7,5},{8,10},{9,11},{10,... | collective-permute-start | bytes 245768 | tf_op jit(solution)/shard_map/ppermute | solution.py:252
  46.8 2.2 %collective-permute-start.12 = (f32[64,256]{1,0:T(8,128)S(1)}, f32[64,256]{1,0:T(8,128)S(1)}, u32[]{:S(2)}, u32[]{:S(2)}) collective-permute-start(f32[64,256]{1,0:T(8,128)S(1)} %add.87.near), channel_id=1, source_target_pairs={{0,2},{1,3},{2,0},{3,1},{4,6},{5,7},{6,4},{7,5},{8,10},{9,11},{10,... | collective-permute-start | bytes 196616 | tf_op jit(solution)/shard_map/ppermute | solution.py:252
  58.7 3.2 %collective-permute-done.14 = f32[72,512]{1,0:T(8,128)S(1)} collective-permute-done((f32[72,512]{1,0:T(8,128)S(1)}, f32[72,512]{1,0:T(8,128)S(1)}, u32[]{:S(2)}, u32[]{:S(2)}) %collective-permute-start.14) | collective-permute-done | bytes 147488 | tf_op jit(solution)/shard_map/ppermute | solution.py:252
  61.9 2.4 %collective-permute-done.16 = f32[72,512]{1,0:T(8,128)S(1)} collective-permute-done((f32[72,512]{1,0:T(8,128)S(1)}, f32[72,512]{1,0:T(8,128)S(1)}, u32[]{:S(2)}, u32[]{:S(2)}) %collective-permute-start.16) | collective-permute-done | bytes 147488 | tf_op jit(solution)/shard_map/ppermute | solution.py:252
  70.8 1.9 %collective-permute-done.18.right = f32[80,256]{1,0:T(8,128)S(1)} collective-permute-done((f32[80,256]{1,0:T(8,128)S(1)}, f32[80,256]{1,0:T(8,128)S(1)}, u32[]{:S(2)}, u32[]{:S(2)}) %collective-permute-start.18) | collective-permute-done | bytes 81952 | tf_op jit(solution)/shard_map/ppermute | solution.py:252
  72.7 3.1 %collective-permute-start.19 = (f32[80,256]{1,0:T(8,128)S(1)}, f32[80,256]{1,0:T(8,128)S(1)}, u32[]{:S(2)}, u32[]{:S(2)}) collective-permute-start(f32[80,256]{1,0:T(8,128)S(1)} %add.88.near), channel_id=1, source_target_pairs={{0,2},{1,3},{2,0},{3,1},{4,6},{5,7},{6,4},{7,5},{8,10},{9,11},{10,... | collective-permute-start | bytes 245768 | tf_op jit(solution)/shard_map/ppermute | solution.py:252
  75.8 2.2 %collective-permute-start.21 = (f32[64,256]{1,0:T(8,128)S(1)}, f32[64,256]{1,0:T(8,128)S(1)}, u32[]{:S(2)}, u32[]{:S(2)}) collective-permute-start(f32[64,256]{1,0:T(8,128)S(1)} %add.89.near), channel_id=1, source_target_pairs={{0,2},{1,3},{2,0},{3,1},{4,6},{5,7},{6,4},{7,5},{8,10},{9,11},{10,... | collective-permute-start | bytes 196616 | tf_op jit(solution)/shard_map/ppermute | solution.py:252
  87.7 3.2 %collective-permute-done.23 = f32[72,512]{1,0:T(8,128)S(1)} collective-permute-done((f32[72,512]{1,0:T(8,128)S(1)}, f32[72,512]{1,0:T(8,128)S(1)}, u32[]{:S(2)}, u32[]{:S(2)}) %collective-permute-start.23) | collective-permute-done | bytes 147488 | tf_op jit(solution)/shard_map/ppermute | solution.py:252
  90.9 3.4 %collective-permute-done.25 = f32[72,512]{1,0:T(8,128)S(1)} collective-permute-done((f32[72,512]{1,0:T(8,128)S(1)}, f32[72,512]{1,0:T(8,128)S(1)}, u32[]{:S(2)}, u32[]{:S(2)}) %collective-permute-start.25) | collective-permute-done | bytes 147488 | tf_op jit(solution)/shard_map/ppermute | solution.py:252
  100.6 1.9 %collective-permute-done.27.right = f32[80,256]{1,0:T(8,128)S(1)} collective-permute-done((f32[80,256]{1,0:T(8,128)S(1)}, f32[80,256]{1,0:T(8,128)S(1)}, u32[]{:S(2)}, u32[]{:S(2)}) %collective-permute-start.27) | collective-permute-done | bytes 81952 | tf_op jit(solution)/shard_map/ppermute | solution.py:252
  102.5 3.1 %collective-permute-start.28 = (f32[80,256]{1,0:T(8,128)S(1)}, f32[80,256]{1,0:T(8,128)S(1)}, u32[]{:S(2)}, u32[]{:S(2)}) collective-permute-start(f32[80,256]{1,0:T(8,128)S(1)} %add.90.near), channel_id=1, source_target_pairs={{0,2},{1,3},{2,0},{3,1},{4,6},{5,7},{6,4},{7,5},{8,10},{9,11},{10,... | collective-permute-start | bytes 245768 | tf_op jit(solution)/shard_map/ppermute | solution.py:252
  105.7 2.2 %collective-permute-start.30 = (f32[64,256]{1,0:T(8,128)S(1)}, f32[64,256]{1,0:T(8,128)S(1)}, u32[]{:S(2)}, u32[]{:S(2)}) collective-permute-start(f32[64,256]{1,0:T(8,128)S(1)} %add.91.near), channel_id=1, source_target_pairs={{0,2},{1,3},{2,0},{3,1},{4,6},{5,7},{6,4},{7,5},{8,10},{9,11},{10,... | collective-permute-start | bytes 196616 | tf_op jit(solution)/shard_map/ppermute | solution.py:252
  117.6 3.2 %collective-permute-done.32 = f32[72,512]{1,0:T(8,128)S(1)} collective-permute-done((f32[72,512]{1,0:T(8,128)S(1)}, f32[72,512]{1,0:T(8,128)S(1)}, u32[]{:S(2)}, u32[]{:S(2)}) %collective-permute-start.32) | collective-permute-done | bytes 147488 | tf_op jit(solution)/shard_map/ppermute | solution.py:252
  120.8 2.4 %collective-permute-done.34 = f32[72,512]{1,0:T(8,128)S(1)} collective-permute-done((f32[72,512]{1,0:T(8,128)S(1)}, f32[72,512]{1,0:T(8,128)S(1)}, u32[]{:S(2)}, u32[]{:S(2)}) %collective-permute-start.34) | collective-permute-done | bytes 147488 | tf_op jit(solution)/shard_map/ppermute | solution.py:252
  129.5 1.9 %collective-permute-done.36.right = f32[80,256]{1,0:T(8,128)S(1)} collective-permute-done((f32[80,256]{1,0:T(8,128)S(1)}, f32[80,256]{1,0:T(8,128)S(1)}, u32[]{:S(2)}, u32[]{:S(2)}) %collective-permute-start.36) | collective-permute-done | bytes 81952 | tf_op jit(solution)/shard_map/ppermute | solution.py:252
  131.4 3.1 %collective-permute-start.37 = (f32[80,256]{1,0:T(8,128)S(1)}, f32[80,256]{1,0:T(8,128)S(1)}, u32[]{:S(2)}, u32[]{:S(2)}) collective-permute-start(f32[80,256]{1,0:T(8,128)S(1)} %add.92.near), channel_id=1, source_target_pairs={{0,2},{1,3},{2,0},{3,1},{4,6},{5,7},{6,4},{7,5},{8,10},{9,11},{10,... | collective-permute-start | bytes 245768 | tf_op jit(solution)/shard_map/ppermute | solution.py:252
  134.5 2.2 %collective-permute-start.39 = (f32[64,256]{1,0:T(8,128)S(1)}, f32[64,256]{1,0:T(8,128)S(1)}, u32[]{:S(2)}, u32[]{:S(2)}) collective-permute-start(f32[64,256]{1,0:T(8,128)S(1)} %add.93.near), channel_id=1, source_target_pairs={{0,2},{1,3},{2,0},{3,1},{4,6},{5,7},{6,4},{7,5},{8,10},{9,11},{10,... | collective-permute-start | bytes 196616 | tf_op jit(solution)/shard_map/ppermute | solution.py:252
  146.4 3.2 %collective-permute-done.41 = f32[72,512]{1,0:T(8,128)S(1)} collective-permute-done((f32[72,512]{1,0:T(8,128)S(1)}, f32[72,512]{1,0:T(8,128)S(1)}, u32[]{:S(2)}, u32[]{:S(2)}) %collective-permute-start.41) | collective-permute-done | bytes 147488 | tf_op jit(solution)/shard_map/ppermute | solution.py:252
  149.6 3.4 %collective-permute-done.43 = f32[72,512]{1,0:T(8,128)S(1)} collective-permute-done((f32[72,512]{1,0:T(8,128)S(1)}, f32[72,512]{1,0:T(8,128)S(1)}, u32[]{:S(2)}, u32[]{:S(2)}) %collective-permute-start.43) | collective-permute-done | bytes 147488 | tf_op jit(solution)/shard_map/ppermute | solution.py:252
  161.3 3.1 %collective-permute-start.46 = (f32[80,256]{1,0:T(8,128)S(1)}, f32[80,256]{1,0:T(8,128)S(1)}, u32[]{:S(2)}, u32[]{:S(2)}) collective-permute-start(f32[80,256]{1,0:T(8,128)S(1)} %add.94.near), channel_id=1, source_target_pairs={{0,2},{1,3},{2,0},{3,1},{4,6},{5,7},{6,4},{7,5},{8,10},{9,11},{10,... | collective-permute-start | bytes 245768 | tf_op jit(solution)/shard_map/ppermute | solution.py:252
  164.4 2.6 %collective-permute-start.48 = (f32[64,256]{1,0:T(8,128)S(1)}, f32[64,256]{1,0:T(8,128)S(1)}, u32[]{:S(2)}, u32[]{:S(2)}) collective-permute-start(f32[64,256]{1,0:T(8,128)S(1)} %add.95.near), channel_id=1, source_target_pairs={{0,2},{1,3},{2,0},{3,1},{4,6},{5,7},{6,4},{7,5},{8,10},{9,11},{10,... | collective-permute-start | bytes 196616 | tf_op jit(solution)/shard_map/ppermute | solution.py:252
  176.3 3.2 %collective-permute-done.50 = f32[72,512]{1,0:T(8,128)S(1)} collective-permute-done((f32[72,512]{1,0:T(8,128)S(1)}, f32[72,512]{1,0:T(8,128)S(1)}, u32[]{:S(2)}, u32[]{:S(2)}) %collective-permute-start.50) | collective-permute-done | bytes 147488 | tf_op jit(solution)/shard_map/ppermute | solution.py:252
  179.5 2.4 %collective-permute-done.52 = f32[72,512]{1,0:T(8,128)S(1)} collective-permute-done((f32[72,512]{1,0:T(8,128)S(1)}, f32[72,512]{1,0:T(8,128)S(1)}, u32[]{:S(2)}, u32[]{:S(2)}) %collective-permute-start.52) | collective-permute-done | bytes 147488 | tf_op jit(solution)/shard_map/ppermute | solution.py:252
  (152 shorter events, 93.8 us)
Async XLA Ops:
  11.1 5.9 %collective-permute-start = (f32[80,256]{1,0:T(8,128)S(1)}, f32[80,256]{1,0:T(8,128)S(1)}, u32[]{:S(2)}, u32[]{:S(2)}) collective-permute-start(f32[80,256]{1,0:T(8,128)S(1)} %get-tuple-element.68.left), channel_id=1, source_target_pairs={{0,1},{1,0},{2,3},{3,2},{4,5},{5,4},{6,7},{7,6},{8,9},{9,8},{10,11... | collective-permute-start | bytes 245768 | tf_op jit(solution)/shard_map/ppermute | solution.py:252
  13.5 10.1 %collective-permute-start.3 = (f32[64,256]{1,0:T(8,128)S(1)}, f32[64,256]{1,0:T(8,128)S(1)}, u32[]{:S(2)}, u32[]{:S(2)}) collective-permute-start(f32[64,256]{1,0:T(8,128)S(1)} %add.85.near), channel_id=1, source_target_pairs={{0,2},{1,3},{2,0},{3,1},{4,6},{5,7},{6,4},{7,5},{8,10},{9,11},{10,... | collective-permute-start | bytes 196616 | tf_op jit(solution)/shard_map/ppermute | solution.py:252
  25.8 6.8 %collective-permute-start.5 = (f32[72,512]{1,0:T(8,128)S(1)}, f32[72,512]{1,0:T(8,128)S(1)}, u32[]{:S(2)}, u32[]{:S(2)}) collective-permute-start(f32[72,512]{1,0:T(8,128)S(1)} %add.66), channel_id=1, source_target_pairs={{0,8},{4,12},{8,0},{12,4},{16,24},{20,28},{24,16},{28,20},{1,9},{5... | collective-permute-start | bytes 442376 | tf_op jit(solution)/shard_map/ppermute | solution.py:252
  27.3 8.6 %collective-permute-start.7 = (f32[72,512]{1,0:T(8,128)S(1)}, f32[72,512]{1,0:T(8,128)S(1)}, u32[]{:S(2)}, u32[]{:S(2)}) collective-permute-start(f32[72,512]{1,0:T(8,128)S(1)} %add.66), channel_id=1, source_target_pairs={{0,24},{4,28},{8,16},{12,20},{16,8},{20,12},{24,0},{28,4},{1,25},{... | collective-permute-start | bytes 442376 | tf_op jit(solution)/shard_map/ppermute | solution.py:252
  28.8 8.5 %collective-permute-start.6 = (f32[72,512]{1,0:T(8,128)S(1)}, f32[72,512]{1,0:T(8,128)S(1)}, u32[]{:S(2)}, u32[]{:S(2)}) collective-permute-start(f32[72,512]{1,0:T(8,128)S(1)} %add.66), channel_id=1, source_target_pairs={{0,16},{4,20},{8,24},{12,28},{16,0},{20,4},{24,8},{28,12},{1,17},{... | collective-permute-start | bytes 442376 | tf_op jit(solution)/shard_map/ppermute | solution.py:252
  44.3 5.9 %collective-permute-start.10 = (f32[80,256]{1,0:T(8,128)S(1)}, f32[80,256]{1,0:T(8,128)S(1)}, u32[]{:S(2)}, u32[]{:S(2)}) collective-permute-start(f32[80,256]{1,0:T(8,128)S(1)} %add.86.near), channel_id=1, source_target_pairs={{0,2},{1,3},{2,0},{3,1},{4,6},{5,7},{6,4},{7,5},{8,10},{9,11},{10,... | collective-permute-start | bytes 245768 | tf_op jit(solution)/shard_map/ppermute | solution.py:252
  46.8 6.1 %collective-permute-start.12 = (f32[64,256]{1,0:T(8,128)S(1)}, f32[64,256]{1,0:T(8,128)S(1)}, u32[]{:S(2)}, u32[]{:S(2)}) collective-permute-start(f32[64,256]{1,0:T(8,128)S(1)} %add.87.near), channel_id=1, source_target_pairs={{0,2},{1,3},{2,0},{3,1},{4,6},{5,7},{6,4},{7,5},{8,10},{9,11},{10,... | collective-permute-start | bytes 196616 | tf_op jit(solution)/shard_map/ppermute | solution.py:252
  55.1 6.8 %collective-permute-start.14 = (f32[72,512]{1,0:T(8,128)S(1)}, f32[72,512]{1,0:T(8,128)S(1)}, u32[]{:S(2)}, u32[]{:S(2)}) collective-permute-start(f32[72,512]{1,0:T(8,128)S(1)} %add.69), channel_id=1, source_target_pairs={{0,8},{4,12},{8,0},{12,4},{16,24},{20,28},{24,16},{28,20},{1,9},{5... | collective-permute-start | bytes 442376 | tf_op jit(solution)/shard_map/ppermute | solution.py:252
  56.7 7.6 %collective-permute-start.16 = (f32[72,512]{1,0:T(8,128)S(1)}, f32[72,512]{1,0:T(8,128)S(1)}, u32[]{:S(2)}, u32[]{:S(2)}) collective-permute-start(f32[72,512]{1,0:T(8,128)S(1)} %add.69), channel_id=1, source_target_pairs={{0,24},{4,28},{8,16},{12,20},{16,8},{20,12},{24,0},{28,4},{1,25},{... | collective-permute-start | bytes 442376 | tf_op jit(solution)/shard_map/ppermute | solution.py:252
  57.1 8.5 %collective-permute-start.15 = (f32[72,512]{1,0:T(8,128)S(1)}, f32[72,512]{1,0:T(8,128)S(1)}, u32[]{:S(2)}, u32[]{:S(2)}) collective-permute-start(f32[72,512]{1,0:T(8,128)S(1)} %add.69), channel_id=1, source_target_pairs={{0,16},{4,20},{8,24},{12,28},{16,0},{20,4},{24,8},{28,12},{1,17},{... | collective-permute-start | bytes 442376 | tf_op jit(solution)/shard_map/ppermute | solution.py:252
  72.7 6.5 %collective-permute-start.19 = (f32[80,256]{1,0:T(8,128)S(1)}, f32[80,256]{1,0:T(8,128)S(1)}, u32[]{:S(2)}, u32[]{:S(2)}) collective-permute-start(f32[80,256]{1,0:T(8,128)S(1)} %add.88.near), channel_id=1, source_target_pairs={{0,2},{1,3},{2,0},{3,1},{4,6},{5,7},{6,4},{7,5},{8,10},{9,11},{10,... | collective-permute-start | bytes 245768 | tf_op jit(solution)/shard_map/ppermute | solution.py:252
  75.8 6.1 %collective-permute-start.21 = (f32[64,256]{1,0:T(8,128)S(1)}, f32[64,256]{1,0:T(8,128)S(1)}, u32[]{:S(2)}, u32[]{:S(2)}) collective-permute-start(f32[64,256]{1,0:T(8,128)S(1)} %add.89.near), channel_id=1, source_target_pairs={{0,2},{1,3},{2,0},{3,1},{4,6},{5,7},{6,4},{7,5},{8,10},{9,11},{10,... | collective-permute-start | bytes 196616 | tf_op jit(solution)/shard_map/ppermute | solution.py:252
  84.1 6.8 %collective-permute-start.23 = (f32[72,512]{1,0:T(8,128)S(1)}, f32[72,512]{1,0:T(8,128)S(1)}, u32[]{:S(2)}, u32[]{:S(2)}) collective-permute-start(f32[72,512]{1,0:T(8,128)S(1)} %add.72), channel_id=1, source_target_pairs={{0,8},{4,12},{8,0},{12,4},{16,24},{20,28},{24,16},{28,20},{1,9},{5... | collective-permute-start | bytes 442376 | tf_op jit(solution)/shard_map/ppermute | solution.py:252
  85.7 8.6 %collective-permute-start.25 = (f32[72,512]{1,0:T(8,128)S(1)}, f32[72,512]{1,0:T(8,128)S(1)}, u32[]{:S(2)}, u32[]{:S(2)}) collective-permute-start(f32[72,512]{1,0:T(8,128)S(1)} %add.72), channel_id=1, source_target_pairs={{0,24},{4,28},{8,16},{12,20},{16,8},{20,12},{24,0},{28,4},{1,25},{... | collective-permute-start | bytes 442376 | tf_op jit(solution)/shard_map/ppermute | solution.py:252
  87.2 8.5 %collective-permute-start.24 = (f32[72,512]{1,0:T(8,128)S(1)}, f32[72,512]{1,0:T(8,128)S(1)}, u32[]{:S(2)}, u32[]{:S(2)}) collective-permute-start(f32[72,512]{1,0:T(8,128)S(1)} %add.72), channel_id=1, source_target_pairs={{0,16},{4,20},{8,24},{12,28},{16,0},{20,4},{24,8},{28,12},{1,17},{... | collective-permute-start | bytes 442376 | tf_op jit(solution)/shard_map/ppermute | solution.py:252
  100.1 5.6 %collective-permute-start.29 = (f32[64,256]{1,0:T(8,128)S(1)}, f32[64,256]{1,0:T(8,128)S(1)}, u32[]{:S(2)}, u32[]{:S(2)}) collective-permute-start(f32[64,256]{1,0:T(8,128)S(1)} %dest_lower.7.left), channel_id=1, source_target_pairs={{0,1},{1,0},{2,3},{3,2},{4,5},{5,4},{6,7},{7,6},{8,9},{9,8},{10,11... | collective-permute-start | bytes 196616 | tf_op jit(solution)/shard_map/ppermute | solution.py:252
  102.5 6.5 %collective-permute-start.28 = (f32[80,256]{1,0:T(8,128)S(1)}, f32[80,256]{1,0:T(8,128)S(1)}, u32[]{:S(2)}, u32[]{:S(2)}) collective-permute-start(f32[80,256]{1,0:T(8,128)S(1)} %add.90.near), channel_id=1, source_target_pairs={{0,2},{1,3},{2,0},{3,1},{4,6},{5,7},{6,4},{7,5},{8,10},{9,11},{10,... | collective-permute-start | bytes 245768 | tf_op jit(solution)/shard_map/ppermute | solution.py:252
  105.7 6.1 %collective-permute-start.30 = (f32[64,256]{1,0:T(8,128)S(1)}, f32[64,256]{1,0:T(8,128)S(1)}, u32[]{:S(2)}, u32[]{:S(2)}) collective-permute-start(f32[64,256]{1,0:T(8,128)S(1)} %add.91.near), channel_id=1, source_target_pairs={{0,2},{1,3},{2,0},{3,1},{4,6},{5,7},{6,4},{7,5},{8,10},{9,11},{10,... | collective-permute-start | bytes 196616 | tf_op jit(solution)/shard_map/ppermute | solution.py:252
  114.0 6.8 %collective-permute-start.32 = (f32[72,512]{1,0:T(8,128)S(1)}, f32[72,512]{1,0:T(8,128)S(1)}, u32[]{:S(2)}, u32[]{:S(2)}) collective-permute-start(f32[72,512]{1,0:T(8,128)S(1)} %add.75), channel_id=1, source_target_pairs={{0,8},{4,12},{8,0},{12,4},{16,24},{20,28},{24,16},{28,20},{1,9},{5... | collective-permute-start | bytes 442376 | tf_op jit(solution)/shard_map/ppermute | solution.py:252
  115.6 7.6 %collective-permute-start.34 = (f32[72,512]{1,0:T(8,128)S(1)}, f32[72,512]{1,0:T(8,128)S(1)}, u32[]{:S(2)}, u32[]{:S(2)}) collective-permute-start(f32[72,512]{1,0:T(8,128)S(1)} %add.75), channel_id=1, source_target_pairs={{0,24},{4,28},{8,16},{12,20},{16,8},{20,12},{24,0},{28,4},{1,25},{... | collective-permute-start | bytes 442376 | tf_op jit(solution)/shard_map/ppermute | solution.py:252
  116.0 8.5 %collective-permute-start.33 = (f32[72,512]{1,0:T(8,128)S(1)}, f32[72,512]{1,0:T(8,128)S(1)}, u32[]{:S(2)}, u32[]{:S(2)}) collective-permute-start(f32[72,512]{1,0:T(8,128)S(1)} %add.75), channel_id=1, source_target_pairs={{0,16},{4,20},{8,24},{12,28},{16,0},{20,4},{24,8},{28,12},{1,17},{... | collective-permute-start | bytes 442376 | tf_op jit(solution)/shard_map/ppermute | solution.py:252
  128.9 5.6 %collective-permute-start.38 = (f32[64,256]{1,0:T(8,128)S(1)}, f32[64,256]{1,0:T(8,128)S(1)}, u32[]{:S(2)}, u32[]{:S(2)}) collective-permute-start(f32[64,256]{1,0:T(8,128)S(1)} %dest_lower.8.left), channel_id=1, source_target_pairs={{0,1},{1,0},{2,3},{3,2},{4,5},{5,4},{6,7},{7,6},{8,9},{9,8},{10,11... | collective-permute-start | bytes 196616 | tf_op jit(solution)/shard_map/ppermute | solution.py:252
  131.4 6.5 %collective-permute-start.37 = (f32[80,256]{1,0:T(8,128)S(1)}, f32[80,256]{1,0:T(8,128)S(1)}, u32[]{:S(2)}, u32[]{:S(2)}) collective-permute-start(f32[80,256]{1,0:T(8,128)S(1)} %add.92.near), channel_id=1, source_target_pairs={{0,2},{1,3},{2,0},{3,1},{4,6},{5,7},{6,4},{7,5},{8,10},{9,11},{10,... | collective-permute-start | bytes 245768 | tf_op jit(solution)/shard_map/ppermute | solution.py:252
  134.5 6.1 %collective-permute-start.39 = (f32[64,256]{1,0:T(8,128)S(1)}, f32[64,256]{1,0:T(8,128)S(1)}, u32[]{:S(2)}, u32[]{:S(2)}) collective-permute-start(f32[64,256]{1,0:T(8,128)S(1)} %add.93.near), channel_id=1, source_target_pairs={{0,2},{1,3},{2,0},{3,1},{4,6},{5,7},{6,4},{7,5},{8,10},{9,11},{10,... | collective-permute-start | bytes 196616 | tf_op jit(solution)/shard_map/ppermute | solution.py:252
  142.9 6.8 %collective-permute-start.41 = (f32[72,512]{1,0:T(8,128)S(1)}, f32[72,512]{1,0:T(8,128)S(1)}, u32[]{:S(2)}, u32[]{:S(2)}) collective-permute-start(f32[72,512]{1,0:T(8,128)S(1)} %add.78), channel_id=1, source_target_pairs={{0,8},{4,12},{8,0},{12,4},{16,24},{20,28},{24,16},{28,20},{1,9},{5... | collective-permute-start | bytes 442376 | tf_op jit(solution)/shard_map/ppermute | solution.py:252
  144.4 8.6 %collective-permute-start.43 = (f32[72,512]{1,0:T(8,128)S(1)}, f32[72,512]{1,0:T(8,128)S(1)}, u32[]{:S(2)}, u32[]{:S(2)}) collective-permute-start(f32[72,512]{1,0:T(8,128)S(1)} %add.78), channel_id=1, source_target_pairs={{0,24},{4,28},{8,16},{12,20},{16,8},{20,12},{24,0},{28,4},{1,25},{... | collective-permute-start | bytes 442376 | tf_op jit(solution)/shard_map/ppermute | solution.py:252
  145.9 8.5 %collective-permute-start.42 = (f32[72,512]{1,0:T(8,128)S(1)}, f32[72,512]{1,0:T(8,128)S(1)}, u32[]{:S(2)}, u32[]{:S(2)}) collective-permute-start(f32[72,512]{1,0:T(8,128)S(1)} %add.78), channel_id=1, source_target_pairs={{0,16},{4,20},{8,24},{12,28},{16,0},{20,4},{24,8},{28,12},{1,17},{... | collective-permute-start | bytes 442376 | tf_op jit(solution)/shard_map/ppermute | solution.py:252
  161.3 6.4 %collective-permute-start.46 = (f32[80,256]{1,0:T(8,128)S(1)}, f32[80,256]{1,0:T(8,128)S(1)}, u32[]{:S(2)}, u32[]{:S(2)}) collective-permute-start(f32[80,256]{1,0:T(8,128)S(1)} %add.94.near), channel_id=1, source_target_pairs={{0,2},{1,3},{2,0},{3,1},{4,6},{5,7},{6,4},{7,5},{8,10},{9,11},{10,... | collective-permute-start | bytes 245768 | tf_op jit(solution)/shard_map/ppermute | solution.py:252
  164.4 6.1 %collective-permute-start.48 = (f32[64,256]{1,0:T(8,128)S(1)}, f32[64,256]{1,0:T(8,128)S(1)}, u32[]{:S(2)}, u32[]{:S(2)}) collective-permute-start(f32[64,256]{1,0:T(8,128)S(1)} %add.95.near), channel_id=1, source_target_pairs={{0,2},{1,3},{2,0},{3,1},{4,6},{5,7},{6,4},{7,5},{8,10},{9,11},{10,... | collective-permute-start | bytes 196616 | tf_op jit(solution)/shard_map/ppermute | solution.py:252
  172.7 6.8 %collective-permute-start.50 = (f32[72,512]{1,0:T(8,128)S(1)}, f32[72,512]{1,0:T(8,128)S(1)}, u32[]{:S(2)}, u32[]{:S(2)}) collective-permute-start(f32[72,512]{1,0:T(8,128)S(1)} %add.81), channel_id=1, source_target_pairs={{0,8},{4,12},{8,0},{12,4},{16,24},{20,28},{24,16},{28,20},{1,9},{5... | collective-permute-start | bytes 442376 | tf_op jit(solution)/shard_map/ppermute | solution.py:252
  174.3 7.6 %collective-permute-start.52 = (f32[72,512]{1,0:T(8,128)S(1)}, f32[72,512]{1,0:T(8,128)S(1)}, u32[]{:S(2)}, u32[]{:S(2)}) collective-permute-start(f32[72,512]{1,0:T(8,128)S(1)} %add.81), channel_id=1, source_target_pairs={{0,24},{4,28},{8,16},{12,20},{16,8},{20,12},{24,0},{28,4},{1,25},{... | collective-permute-start | bytes 442376 | tf_op jit(solution)/shard_map/ppermute | solution.py:252
  174.7 8.5 %collective-permute-start.51 = (f32[72,512]{1,0:T(8,128)S(1)}, f32[72,512]{1,0:T(8,128)S(1)}, u32[]{:S(2)}, u32[]{:S(2)}) collective-permute-start(f32[72,512]{1,0:T(8,128)S(1)} %add.81), channel_id=1, source_target_pairs={{0,16},{4,20},{8,24},{12,28},{16,0},{20,4},{24,8},{28,12},{1,17},{... | collective-permute-start | bytes 442376 | tf_op jit(solution)/shard_map/ppermute | solution.py:252
  (23 other events, 76.9 us)

commit v6 on v5

--- a/solution.py
+++ b/solution.py
@@ -71,10 +71,13 @@
     )
 
 
-def half(flip, size):
+def half(flip, size, part=None):
     core = lax.axis_index("org") % 2
     start = (1 - core if flip else core) * size
-    return pl.ds(pl.multiple_of(start, size), size)
+    if part is None:
+        return pl.ds(pl.multiple_of(start, size), size)
+    size //= 2
+    return pl.ds(pl.multiple_of(start + part * size, size), size)
 
 
 def hour_sum(parts, hour_t):
@@ -86,7 +89,7 @@
 
 
 def first_kernel(
-    counts, scales, dest, hour, tensor, message, message_low, dest_own, hour_gram, hour_t,
+    counts, scales, dest, hour, tensor, message, message_low, dest_own, dest_late, hour_gram, hour_t,
     buffer, scale_now, dest_now, hour_now, arrived, small_arrived,
 ):
     hours, rows, cols = counts.shape
@@ -103,7 +106,8 @@
         copy.wait()
     hour_t[...] = hour_now[...].T
     hour_gram[...] = own_gram(hour_t[...])
-    dest_own[...] = dest_now[:, half(False, cols // 2)]
+    dest_own[...] = dest_now[:, half(False, cols // 2, 0)]
+    dest_late[...] = dest_now[:, half(False, cols // 2, 1)]
     dest_low = dest_now[...].astype(BF16)
     put_gram(message, own_gram(dest_now[...]))
     total = None
@@ -143,24 +147,26 @@
         copy.wait()
 
 
-def store_own_kernel(upper, lower, own, anchor_out, dest_out, done):
+def store_own_kernel(upper, lower, own, late, anchor_out, dest_out, done):
     width = upper.shape[1]
+    size = 2 * own.shape[1]
     store(
         (
             (upper, anchor_out.at[:, pl.ds(0, width)]),
             (lower, anchor_out.at[:, pl.ds(width, width)]),
-            (own, dest_out.at[:, half(False, own.shape[1])]),
+            (own, dest_out.at[:, half(False, size, 0)]),
+            (late, dest_out.at[:, half(False, size, 1)]),
         ),
         done,
     )
 
 
-def store_other_kernel(other, _, dest_out, done):
-    store(((other, dest_out.at[:, half(True, other.shape[1])]),), done)
-
-
-def add_kernel(left, right, *rest):
-    total = rest[-1]
+def store_other_kernel(other, late, _, dest_out, done):
+    size = 2 * other.shape[1]
+    store(((other, dest_out.at[:, half(True, size, 0)]), (late, dest_out.at[:, half(True, size, 1)])), done)
+
+
+def add_kernel(left, right, total):
     total[...] = left[...] + right[...]
 
 
@@ -186,52 +192,70 @@
     gram[...] = own_gram(anchor_out[...])
 
 
-def lower_kernel(tensor, anchor, near, far, gram_part, hour_t, gram, before, _, anchor_out, sent):
-    rank, width = anchor.shape
+def lower_kernel(tensor, anchor, near, far, gram_part, hour_t, before, _, anchor_out, sent):
+    width = anchor.shape[1]
     anchor_out[...] = updated(anchor[...], near[...] + far[...], gram_part[...])
     low = anchor_out[...].astype(BF16)
-    size = tensor.shape[2] // 2
-    sent[:rank, :] = before[...] + products(low, tensor, pl.ds(width, width), half(True, size), hour_t)
-    put_gram(sent, gram[...] + own_gram(anchor_out[...]))
-
-
-def lower_kept_kernel(tensor, anchor, hour_t, before, sent, kept):
+    cols = half(True, tensor.shape[2] // 2, 0)
+    sent[...] = before[:, : cols.size] + products(low, tensor, pl.ds(width, width), cols, hour_t)
+
+
+def lower_late_kernel(tensor, anchor, hour_t, gram, before, sent):
+    rank, width = anchor.shape
+    low = anchor[...].astype(BF16)
+    cols = half(True, tensor.shape[2] // 2, 1)
+    sent[:rank, :] = before[:, cols.size :] + products(low, tensor, pl.ds(width, width), cols, hour_t)
+    put_gram(sent, gram[...] + own_gram(anchor[...]))
+
+
+def lower_kept_kernel(tensor, anchor, hour_t, before, sent, kept, kept_late):
     rank, width = anchor.shape
     low = anchor[...].astype(BF16)
     size = tensor.shape[2] // 2
-    kept[:rank, :] = before[...] + products(low, tensor, pl.ds(width, width), half(False, size), hour_t)
-    kept[rank:, :] = sent[rank:, :]
-
-
-def dest_kernel(dest, near, far, hour_gram, dest_out):
+    total = before[...] + products(low, tensor, pl.ds(width, width), half(False, size), hour_t)
+    kept[...] = total[:, : size // 2]
+    kept_late[:rank, :] = total[:, size // 2 :]
+    kept_late[rank:, :] = sent[rank:, :]
+
+
+def dest_late_kernel(dest, near, far, hour_gram, dest_out, gram_part):
     rank = dest.shape[0]
     message = near[...] + far[...]
-    gram_part = get_gram(message, rank) * hour_gram[...]
-    dest_out[...] = updated(dest[...], message[:rank, :], gram_part)
-
-
-def dest_own_kernel(flipped, dest, hour_t, upper, lower, gram):
-    low = dest[...].astype(BF16)
-    rows = half(False, flipped.shape[1] // 2)
-    width = flipped.shape[2] // 2
-    upper[...] = products(low, flipped, rows, pl.ds(0, width), hour_t)
-    lower[...] = products(low, flipped, rows, pl.ds(width, width), hour_t)
+    gram_part[...] = get_gram(message, rank) * hour_gram[...]
+    dest_out[...] = updated(dest[...], message[:rank, :], gram_part[...])
+
+
+def dest_kernel(dest, near, far, gram_part, dest_out):
+    dest_out[...] = updated(dest[...], near[...] + far[...], gram_part[...])
+
+
+def dest_products(dest, flipped, flip, part, width, index, hour_t):
+    rows = half(flip, flipped.shape[1] // 2, part)
+    return products(dest[...].astype(BF16), flipped, rows, pl.ds(index * width, width), hour_t)
+
+
+def own_late_kernel(flipped, dest, hour_t, upper, lower, gram):
+    width = upper.shape[1]
+    upper[...] = dest_products(dest, flipped, False, 1, width, 0, hour_t)
+    lower[...] = dest_products(dest, flipped, False, 1, width, 1, hour_t)
     gram[...] = own_gram(dest[...])
 
 
+def more_kernel(flip, part, flipped, dest, hour_t, upper, lower, gram, upper_out, lower_out, gram_out):
+    width = upper.shape[1]
+    upper_out[...] = upper[...] + dest_products(dest, flipped, flip, part, width, 0, hour_t)
+    lower_out[...] = lower[...] + dest_products(dest, flipped, flip, part, width, 1, hour_t)
+    gram_out[...] = gram[...] + own_gram(dest[...])
+
+
 def dest_upper_kernel(flipped, dest, hour_t, before, gram, message):
-    low = dest[...].astype(BF16)
-    rows = half(True, flipped.shape[1] // 2)
-    width = flipped.shape[2] // 2
-    message[: low.shape[0], :] = before[...] + products(low, flipped, rows, pl.ds(0, width), hour_t)
+    rank, width = before.shape
+    message[:rank, :] = before[...] + dest_products(dest, flipped, True, 0, width, 0, hour_t)
     put_gram(message, gram[...] + own_gram(dest[...]))
 
 
 def dest_lower_kernel(flipped, dest, hour_t, before, message):
-    low = dest[...].astype(BF16)
-    rows = half(True, flipped.shape[1] // 2)
-    width = flipped.shape[2] // 2
-    message[...] = before[...] + products(low, flipped, rows, pl.ds(width, width), hour_t)
+    message[...] = before[...] + dest_products(dest, flipped, True, 0, before.shape[1], 1, hour_t)
 
 
 def call(kernel, outs, name, flops, *args):
@@ -252,24 +276,22 @@
     return lax.ppermute(array, axis, [(index, index ^ mask) for index in range(size)])
 
 
-def sum_dest(message, *before):
-    size = lax.axis_size("dst")
-    mask = 1
+def add(left, right):
+    return call(add_kernel, [(left.shape, F32)], "add", HINT, left, right)
+
+
+def sum_steps(message, axis, mask):
+    size = lax.axis_size(axis)
     while 2 * mask < size:
-        message = call(add_kernel, [(message.shape, F32)], "add", HINT, message, swap(message, "dst", mask), *before)
+        message = add(message, swap(message, axis, mask))
         mask *= 2
-    return message, swap(message, "dst", mask)
-
-
-def sum_anchor(message):
-    size = lax.axis_size("org")
-    if size == 8:
-        return message + swap(message, "org", 2), swap(message, "org", 4) + swap(message, "org", 6)
-    mask = 2
-    while 2 * mask < size:
-        message = message + swap(message, "org", mask)
-        mask *= 2
-    return message, swap(message, "org", mask)
+    return message, swap(message, axis, mask)
+
+
+def sum_at_once(message):
+    if lax.axis_size("org") != 8:
+        return sum_steps(message, "org", 2)
+    return message + swap(message, "org", 2), swap(message, "org", 4) + swap(message, "org", 6)
 
 
 def body(counts, block_scales, anchor_factor, dest_factor, hour_factor):
@@ -278,18 +300,20 @@
     size = cols // 2
     width = rows // 2
     dest_rows = rank + gram_rows(rank, width)
-    anchor_rows = rank + gram_rows(rank, size)
+    part_size = size // 2
+    anchor_rows = rank + gram_rows(rank, part_size)
     half_flops = 2 * 4 * hours * rank * rows * size
 
-    tensor, message, message_low, dest_own, hour_gram, hour_t = pl.pallas_call(
+    tensor, message, message_low, dest_own, late_own, hour_gram, hour_t = pl.pallas_call(
         first_kernel,
         in_specs=[ANYWHERE] * 4,
-        out_specs=(WHOLE,) * 6,
+        out_specs=(WHOLE,) * 7,
         out_shape=(
             pltpu.VMEM((hours, rows, cols), BF16),
             pltpu.VMEM((dest_rows, width), F32),
             pltpu.VMEM((rank, width), F32),
-            pltpu.VMEM((rank, size), F32),
+            pltpu.VMEM((rank, part_size), F32),
+            pltpu.VMEM((rank, part_size), F32),
             pltpu.VMEM((rank, rank), F32),
             pltpu.VMEM((rank, hours), F32),
         ),
@@ -306,60 +330,76 @@
     )(*[pltpu.with_memory_space_constraint(x, pltpu.HBM) for x in (counts, block_scales, dest_factor, hour_factor)])
 
     upper, lower = anchor_factor[:, :width], anchor_factor[:, width:]
+    matrix, factor, part_factor = ((rank, rank), F32), ((rank, width), F32), ((rank, part_size), F32)
     for sweep in range(SWEEPS):
-        near, far = sum_dest(message)
-        near_low, far_low = sum_dest(message_low)
+        near, far = sum_steps(message, "dst", 1)
+        near_low, far_low = sum_steps(message_low, "dst", 1)
         if sweep == 0:
             flipped = call(flip_kernel, [((hours, cols, rows), BF16)], "flip", 4 * half_flops, tensor, near)
         upper, gram_part, gram, sent, kept = call(
-            upper_kernel,
-            [((rank, width), F32), ((rank, rank), F32), ((rank, rank), F32), ((rank, size), F32), ((rank, size), F32)],
+            upper_kernel, [factor, matrix, matrix, ((rank, size), F32), ((rank, size), F32)],
             "upper", half_flops, tensor, upper, near, far, hour_gram, hour_t,
         )
-        lower, sent = call(
-            lower_kernel, [((rank, width), F32), ((anchor_rows, size), F32)], "lower", half_flops // 2,
-            tensor, lower, near_low, far_low, gram_part, hour_t, gram, sent, flipped,
+        lower, sent_early = call(
+            lower_kernel, [factor, part_factor], "lower", half_flops // 4,
+            tensor, lower, near_low, far_low, gram_part, hour_t, sent, flipped,
         )
-        received = swap(sent, "org", 1)
-        kept = call(
-            lower_kept_kernel, [((anchor_rows, size), F32)], "lower_kept", half_flops // 2,
-            tensor, lower, hour_t, kept, sent,
+        received = swap(sent_early, "org", 1)
+        sent_late = call(
+            lower_late_kernel, [((anchor_rows, part_size), F32)], "lower_late", half_flops // 4,
+            tensor, lower, hour_t, gram, sent,
         )
-        near, far = sum_anchor(kept + received)
-        dest_own = call(dest_kernel, [((rank, size), F32)], "dest", 0, dest_own, near, far, hour_gram)
+        received_late = swap(sent_late, "org", 1)
+        kept, kept_late = call(
+            lower_kept_kernel, [part_factor, ((anchor_rows, part_size), F32)], "lower_kept", half_flops // 2,
+            tensor, lower, hour_t, kept, sent_late,
+        )
+        near, far = sum_steps(add(kept, received), "org", 2)
+        near_late, far_late = sum_at_once(add(kept_late, received_late))
+        late_own, gram_part = call(
+            dest_late_kernel, [part_factor, matrix], "dest_late", 0, late_own, near_late, far_late, hour_gram
+        )
+        late_other = swap(late_own, "org", 1)
+        dest_own = call(dest_kernel, [part_factor], "dest", 0, dest_own, near, far, gram_part)
         dest_other = swap(dest_own, "org", 1)
         if sweep + 1 < SWEEPS:
-            part, part_low, gram = call(
-                dest_own_kernel, [((rank, width), F32), ((rank, width), F32), ((rank, rank), F32)], "dest_own",
-                half_flops, flipped, dest_own, hour_t,
+            parts = call(
+                own_late_kernel, [factor, factor, matrix], "own_late", half_flops // 2, flipped, late_own, hour_t
+            )
+            parts = call(
+                functools.partial(more_kernel, False, 0), [factor, factor, matrix], "own", half_flops // 2,
+                flipped, dest_own, hour_t, *parts,
+            )
+            parts = call(
+                functools.partial(more_kernel, True, 1), [factor, factor, matrix], "other_late", half_flops // 2,
+                flipped, late_other, hour_t, *parts,
             )
             message = call(
-                dest_upper_kernel, [((dest_rows, width), F32)], "dest_upper", half_flops // 2,
-                flipped, dest_other, hour_t, part, gram,
+                dest_upper_kernel, [((dest_rows, width), F32)], "dest_upper", half_flops // 4,
+                flipped, dest_other, hour_t, parts[0], parts[2],
             )
             message_low = call(
-                dest_lower_kernel, [((rank, width), F32)], "dest_lower", half_flops // 2,
-                flipped, dest_other, hour_t, part_low,
+                dest_lower_kernel, [factor], "dest_lower", half_flops // 4, flipped, dest_other, hour_t, parts[1]
             )
     anchor_now, dest_now = pl.pallas_call(
         store_own_kernel,
-        in_specs=[WHOLE] * 3,
+        in_specs=[WHOLE] * 4,
         out_specs=(ANYWHERE,) * 2,
         out_shape=(pltpu.HBM((rank, rows), F32), pltpu.HBM((rank, cols), F32)),
-        scratch_shapes=[pltpu.SemaphoreType.DMA((3,))],
+        scratch_shapes=[pltpu.SemaphoreType.DMA((4,))],
         compiler_params=PARAMS,
         name="store_own",
-    )(in_vmem(upper), in_vmem(lower), in_vmem(dest_own))
+    )(*[in_vmem(x) for x in (upper, lower, dest_own, late_own)])
     dest_now = pl.pallas_call(
         store_other_kernel,
-        in_specs=[WHOLE, ANYWHERE],
+        in_specs=[WHOLE, WHOLE, ANYWHERE],
         out_specs=ANYWHERE,
         out_shape=pltpu.HBM((rank, cols), F32),
-        scratch_shapes=[pltpu.SemaphoreType.DMA((1,))],
-        input_output_aliases={1: 0},
+        scratch_shapes=[pltpu.SemaphoreType.DMA((2,))],
+        input_output_aliases={2: 0},
         compiler_params=PARAMS,
         name="store_other",
-    )(in_vmem(dest_other), pltpu.with_memory_space_constraint(dest_now, pltpu.HBM))
+    )(in_vmem(dest_other), in_vmem(late_other), pltpu.with_memory_space_constraint(dest_now, pltpu.HBM))
     return anchor_now, dest_now
 
 

time: 186 us -> 175 us (0.941)
  waiting for transfers between devices: 79.4 us -> 48.3 us
  starting transfers between devices: 67 us -> 83.8 us
  Pallas kernels: 37.7 us -> 41.1 us
    ppermute x54 -> x78, waiting for transfers between devices: 79.4 us -> 48.3 us  [swap(): lax.ppermute(array, axis, [(index, index ^ mask) for index in range(size)])]
    ppermute x54 -> x78, starting transfers between devices: 67 us -> 83.8 us  [swap(): lax.ppermute(array, axis, [(index, index ^ mask) for index in range(size)])]
    pallas_call x52 -> x92, Pallas kernels: 29 us -> 32.4 us  [call(): pl.pallas_call(kernel, in_specs=[WHOLE] * len(args), out_specs=tuple((WHO...]
  transfers between devices with their start and end apart: 54 -> 78, of which waited for: 47 -> 35; matrix products, arithmetic and copies ran while one was open for 0% -> 0% of each run, Pallas kernels for 11% -> 16%
where the time goes in v6:
time: 175 us
  starting transfers between devices  83.8 us (48%)
  waiting for transfers between devices  48.3 us (28%)
  Pallas kernels  41.1 us (23%)
    ppermute x78, starting transfers between devices, swap(): lax.ppermute(array, axis, [(index, index ^ mask) for index in range(size)])  83.8 us
    ppermute x78, waiting for transfers between devices, swap(): lax.ppermute(array, axis, [(index, index ^ mask) for index in range(size)])  48.3 us
    pallas_call x92, Pallas kernels, call(): pl.pallas_call(kernel, in_specs=[WHOLE] * len(args), out_specs=tuple((WHO...  32.4 us
    pallas_call x1, Pallas kernels, body(): pl.pallas_call(first_kernel, in_specs=[ANYWHERE] * 4, out_specs=(WHOLE,)...  7.31 us
  transfers between devices with their start and end apart: 78, of which 35 were waited for; matrix products, arithmetic and copies ran while one was open for 0% of the time, Pallas kernels for 16%

profile of v6, /device:TPU:0, one launch (start us, length us, event | category | flops | bytes accessed | tf_op | source)
XLA Modules:
  0.0 175.0 jit_solution(16613825887612212807)
XLA Ops:
  0.6 7.3 %first.1 = (bf16[8,512,1024]{2,1,0:T(8,128)(2,1)S(1)}, f32[80,256]{1,0:T(8,128)S(1)}, f32[64,256]{1,0:T(8,128)S(1)}, f32[64,256]{1,0:T(8,128)S(1)}, f32[64,256]{...) custom-call(s32[8,512,1024]{2,1,0:T(8,128)} %counts.1, f32[8,4,8]{2,1,0:T(4,128)} %scales.1, ...), custom_call_target="tpu_custom_call" | custom-call | tf_op jit(solution)/shard_map/first/pallas_call | solution.py:307
  8.0 3.1 %collective-permute-start.2 = (f32[64,256]{1,0:T(8,128)S(1)}, f32[64,256]{1,0:T(8,128)S(1)}, u32[]{:S(2)}, u32[]{:S(2)}) collective-permute-start(f32[64,256]{1,0:T(8,128)S(1)} %get-tuple-element.128.left), channel_id=1, source_target_pairs={{0,1},{1,0},{2,3},{3,2},{4,5},{5,4},{6,7},{7,6},{8,9},{9,8},{10,11... | collective-permute-start | bytes 196616 | tf_op jit(solution)/shard_map/ppermute | solution.py:276
  11.1 2.3 %collective-permute-done.2.right = f32[64,256]{1,0:T(8,128)S(1)} collective-permute-done((f32[64,256]{1,0:T(8,128)S(1)}, f32[64,256]{1,0:T(8,128)S(1)}, u32[]{:S(2)}, u32[]{:S(2)}) %collective-permute-start.2) | collective-permute-done | bytes 65568 | tf_op jit(solution)/shard_map/ppermute | solution.py:276
  13.5 3.5 %collective-permute-start.3 = (f32[64,256]{1,0:T(8,128)S(1)}, f32[64,256]{1,0:T(8,128)S(1)}, u32[]{:S(2)}, u32[]{:S(2)}) collective-permute-start(f32[64,256]{1,0:T(8,128)S(1)} %add.79.near), channel_id=1, source_target_pairs={{0,2},{1,3},{2,0},{3,1},{4,6},{5,7},{6,4},{7,5},{8,10},{9,11},{10,... | collective-permute-start | bytes 196616 | tf_op jit(solution)/shard_map/ppermute | solution.py:276
  17.0 1.8 %collective-permute-start.1 = (f32[80,256]{1,0:T(8,128)S(1)}, f32[80,256]{1,0:T(8,128)S(1)}, u32[]{:S(2)}, u32[]{:S(2)}) collective-permute-start(f32[80,256]{1,0:T(8,128)S(1)} %add.78.near.after), channel_id=1, source_target_pairs={{0,2},{1,3},{2,0},{3,1},{4,6},{5,7},{6,4},{7,5},{8,10},{9,11},{10,... | collective-permute-start | bytes 245768 | tf_op jit(solution)/shard_map/ppermute | solution.py:276
  18.8 2.2 %flip.1._.flipped = bf16[8,1024,512]{2,1,0:T(8,128)(2,1)S(1)} custom-call(bf16[8,512,1024]{2,1,0:T(8,128)(2,1)S(1)} %get-tuple-element.122.tensor, f32[80,256]{1,0:T(8,128)S(1)} %add.78.near.after), custom_call_target="tpu_custom_call" | custom-call | flops 4294967296 | tf_op jit(solution)/shard_map/flip/pallas_call | solution.py:262
  32.3 1.7 collective-permute-done.8
  40.1 2.5 %collective-permute-done.13.right = f32[80,256]{1,0:T(8,128)S(1)} collective-permute-done((f32[80,256]{1,0:T(8,128)S(1)}, f32[80,256]{1,0:T(8,128)S(1)}, u32[]{:S(2)}, u32[]{:S(2)}) %collective-permute-start.13) | collective-permute-done | bytes 81952 | tf_op jit(solution)/shard_map/ppermute | solution.py:276
  42.7 2.3 %collective-permute-start.14 = (f32[80,256]{1,0:T(8,128)S(1)}, f32[80,256]{1,0:T(8,128)S(1)}, u32[]{:S(2)}, u32[]{:S(2)}) collective-permute-start(f32[80,256]{1,0:T(8,128)S(1)} %add.83.near), channel_id=1, source_target_pairs={{0,2},{1,3},{2,0},{3,1},{4,6},{5,7},{6,4},{7,5},{8,10},{9,11},{10,... | collective-permute-start | bytes 245768 | tf_op jit(solution)/shard_map/ppermute | solution.py:276
  46.7 3.5 %collective-permute-done.14.far = f32[80,256]{1,0:T(8,128)S(1)} collective-permute-done((f32[80,256]{1,0:T(8,128)S(1)}, f32[80,256]{1,0:T(8,128)S(1)}, u32[]{:S(2)}, u32[]{:S(2)}) %collective-permute-start.14) | collective-permute-done | bytes 81952 | tf_op jit(solution)/shard_map/ppermute | solution.py:276
  59.4 2.1 %collective-permute-done.21 = f32[80,256]{1,0:T(8,128)S(1)} collective-permute-done((f32[80,256]{1,0:T(8,128)S(1)}, f32[80,256]{1,0:T(8,128)S(1)}, u32[]{:S(2)}, u32[]{:S(2)}) %collective-permute-start.21) | collective-permute-done | bytes 81952 | tf_op jit(solution)/shard_map/ppermute | solution.py:276
  64.7 1.7 collective-permute-start.26
  67.1 2.3 %collective-permute-done.26.right = f32[80,256]{1,0:T(8,128)S(1)} collective-permute-done((f32[80,256]{1,0:T(8,128)S(1)}, f32[80,256]{1,0:T(8,128)S(1)}, u32[]{:S(2)}, u32[]{:S(2)}) %collective-permute-start.26) | collective-permute-done | bytes 81952 | tf_op jit(solution)/shard_map/ppermute | solution.py:276
  69.5 3.0 %collective-permute-start.27 = (f32[80,256]{1,0:T(8,128)S(1)}, f32[80,256]{1,0:T(8,128)S(1)}, u32[]{:S(2)}, u32[]{:S(2)}) collective-permute-start(f32[80,256]{1,0:T(8,128)S(1)} %add.88.near), channel_id=1, source_target_pairs={{0,2},{1,3},{2,0},{3,1},{4,6},{5,7},{6,4},{7,5},{8,10},{9,11},{10,... | collective-permute-start | bytes 245768 | tf_op jit(solution)/shard_map/ppermute | solution.py:276
  72.5 1.7 collective-permute-start.29
  77.0 1.7 collective-permute-done.29.far
  86.7 2.2 %collective-permute-done.34 = f32[80,256]{1,0:T(8,128)S(1)} collective-permute-done((f32[80,256]{1,0:T(8,128)S(1)}, f32[80,256]{1,0:T(8,128)S(1)}, u32[]{:S(2)}, u32[]{:S(2)}) %collective-permute-start.34) | collective-permute-done | bytes 81952 | tf_op jit(solution)/shard_map/ppermute | solution.py:276
  95.0 2.2 %collective-permute-done.39.right = f32[80,256]{1,0:T(8,128)S(1)} collective-permute-done((f32[80,256]{1,0:T(8,128)S(1)}, f32[80,256]{1,0:T(8,128)S(1)}, u32[]{:S(2)}, u32[]{:S(2)}) %collective-permute-start.39) | collective-permute-done | bytes 81952 | tf_op jit(solution)/shard_map/ppermute | solution.py:276
  97.2 3.0 %collective-permute-start.40 = (f32[80,256]{1,0:T(8,128)S(1)}, f32[80,256]{1,0:T(8,128)S(1)}, u32[]{:S(2)}, u32[]{:S(2)}) collective-permute-start(f32[80,256]{1,0:T(8,128)S(1)} %add.93.near), channel_id=1, source_target_pairs={{0,2},{1,3},{2,0},{3,1},{4,6},{5,7},{6,4},{7,5},{8,10},{9,11},{10,... | collective-permute-start | bytes 245768 | tf_op jit(solution)/shard_map/ppermute | solution.py:276
  100.2 1.9 %collective-permute-start.42 = (f32[64,256]{1,0:T(8,128)S(1)}, f32[64,256]{1,0:T(8,128)S(1)}, u32[]{:S(2)}, u32[]{:S(2)}) collective-permute-start(f32[64,256]{1,0:T(8,128)S(1)} %add.94.near), channel_id=1, source_target_pairs={{0,2},{1,3},{2,0},{3,1},{4,6},{5,7},{6,4},{7,5},{8,10},{9,11},{10,... | collective-permute-start | bytes 196616 | tf_op jit(solution)/shard_map/ppermute | solution.py:276
  114.0 2.3 %collective-permute-done.47 = f32[80,256]{1,0:T(8,128)S(1)} collective-permute-done((f32[80,256]{1,0:T(8,128)S(1)}, f32[80,256]{1,0:T(8,128)S(1)}, u32[]{:S(2)}, u32[]{:S(2)}) %collective-permute-start.47) | collective-permute-done | bytes 81952 | tf_op jit(solution)/shard_map/ppermute | solution.py:276
  122.2 2.2 %collective-permute-done.52.right = f32[80,256]{1,0:T(8,128)S(1)} collective-permute-done((f32[80,256]{1,0:T(8,128)S(1)}, f32[80,256]{1,0:T(8,128)S(1)}, u32[]{:S(2)}, u32[]{:S(2)}) %collective-permute-start.52) | collective-permute-done | bytes 81952 | tf_op jit(solution)/shard_map/ppermute | solution.py:276
  124.4 3.0 %collective-permute-start.53 = (f32[80,256]{1,0:T(8,128)S(1)}, f32[80,256]{1,0:T(8,128)S(1)}, u32[]{:S(2)}, u32[]{:S(2)}) collective-permute-start(f32[80,256]{1,0:T(8,128)S(1)} %add.98.near), channel_id=1, source_target_pairs={{0,2},{1,3},{2,0},{3,1},{4,6},{5,7},{6,4},{7,5},{8,10},{9,11},{10,... | collective-permute-start | bytes 245768 | tf_op jit(solution)/shard_map/ppermute | solution.py:276
  127.5 2.1 %collective-permute-start.55 = (f32[64,256]{1,0:T(8,128)S(1)}, f32[64,256]{1,0:T(8,128)S(1)}, u32[]{:S(2)}, u32[]{:S(2)}) collective-permute-start(f32[64,256]{1,0:T(8,128)S(1)} %add.99.near), channel_id=1, source_target_pairs={{0,2},{1,3},{2,0},{3,1},{4,6},{5,7},{6,4},{7,5},{8,10},{9,11},{10,... | collective-permute-start | bytes 196616 | tf_op jit(solution)/shard_map/ppermute | solution.py:276
  131.7 1.9 %collective-permute-done.55.far = f32[64,256]{1,0:T(8,128)S(1)} collective-permute-done((f32[64,256]{1,0:T(8,128)S(1)}, f32[64,256]{1,0:T(8,128)S(1)}, u32[]{:S(2)}, u32[]{:S(2)}) %collective-permute-start.55) | collective-permute-done | bytes 65568 | tf_op jit(solution)/shard_map/ppermute | solution.py:276
  141.6 2.1 %collective-permute-done.60 = f32[80,256]{1,0:T(8,128)S(1)} collective-permute-done((f32[80,256]{1,0:T(8,128)S(1)}, f32[80,256]{1,0:T(8,128)S(1)}, u32[]{:S(2)}, u32[]{:S(2)}) %collective-permute-start.60) | collective-permute-done | bytes 81952 | tf_op jit(solution)/shard_map/ppermute | solution.py:276
  147.4 1.8 %collective-permute-start.65 = (f32[80,256]{1,0:T(8,128)S(1)}, f32[80,256]{1,0:T(8,128)S(1)}, u32[]{:S(2)}, u32[]{:S(2)}) collective-permute-start(f32[80,256]{1,0:T(8,128)S(1)} %dest_upper.9.left), channel_id=1, source_target_pairs={{0,1},{1,0},{2,3},{3,2},{4,5},{5,4},{6,7},{7,6},{8,9},{9,8},{10,11... | collective-permute-start | bytes 245768 | tf_op jit(solution)/shard_map/ppermute | solution.py:276
  149.8 2.1 %collective-permute-done.65.right = f32[80,256]{1,0:T(8,128)S(1)} collective-permute-done((f32[80,256]{1,0:T(8,128)S(1)}, f32[80,256]{1,0:T(8,128)S(1)}, u32[]{:S(2)}, u32[]{:S(2)}) %collective-permute-start.65) | collective-permute-done | bytes 81952 | tf_op jit(solution)/shard_map/ppermute | solution.py:276
  152.0 3.2 %collective-permute-start.66 = (f32[80,256]{1,0:T(8,128)S(1)}, f32[80,256]{1,0:T(8,128)S(1)}, u32[]{:S(2)}, u32[]{:S(2)}) collective-permute-start(f32[80,256]{1,0:T(8,128)S(1)} %add.103.near), channel_id=1, source_target_pairs={{0,2},{1,3},{2,0},{3,1},{4,6},{5,7},{6,4},{7,5},{8,10},{9,11},{10,... | collective-permute-start | bytes 245768 | tf_op jit(solution)/shard_map/ppermute | solution.py:276
  155.2 1.9 %collective-permute-start.68 = (f32[64,256]{1,0:T(8,128)S(1)}, f32[64,256]{1,0:T(8,128)S(1)}, u32[]{:S(2)}, u32[]{:S(2)}) collective-permute-start(f32[64,256]{1,0:T(8,128)S(1)} %add.104.near), channel_id=1, source_target_pairs={{0,2},{1,3},{2,0},{3,1},{4,6},{5,7},{6,4},{7,5},{8,10},{9,11},{10,... | collective-permute-start | bytes 196616 | tf_op jit(solution)/shard_map/ppermute | solution.py:276
  159.6 1.7 collective-permute-done.68.far
  169.1 2.3 %collective-permute-done.73 = f32[80,256]{1,0:T(8,128)S(1)} collective-permute-done((f32[80,256]{1,0:T(8,128)S(1)}, f32[80,256]{1,0:T(8,128)S(1)}, u32[]{:S(2)}, u32[]{:S(2)}) %collective-permute-start.73) | collective-permute-done | bytes 81952 | tf_op jit(solution)/shard_map/ppermute | solution.py:276
  (234 shorter events, 94.8 us)
Async XLA Ops:
  8.0 5.5 %collective-permute-start.2 = (f32[64,256]{1,0:T(8,128)S(1)}, f32[64,256]{1,0:T(8,128)S(1)}, u32[]{:S(2)}, u32[]{:S(2)}) collective-permute-start(f32[64,256]{1,0:T(8,128)S(1)} %get-tuple-element.128.left), channel_id=1, source_target_pairs={{0,1},{1,0},{2,3},{3,2},{4,5},{5,4},{6,7},{7,6},{8,9},{9,8},{10,11... | collective-permute-start | bytes 196616 | tf_op jit(solution)/shard_map/ppermute | solution.py:276
  11.1 5.9 %collective-permute-start = (f32[80,256]{1,0:T(8,128)S(1)}, f32[80,256]{1,0:T(8,128)S(1)}, u32[]{:S(2)}, u32[]{:S(2)}) collective-permute-start(f32[80,256]{1,0:T(8,128)S(1)} %get-tuple-element.123.left), channel_id=1, source_target_pairs={{0,1},{1,0},{2,3},{3,2},{4,5},{5,4},{6,7},{7,6},{8,9},{9,8},{10,11... | collective-permute-start | bytes 245768 | tf_op jit(solution)/shard_map/ppermute | solution.py:276
  13.5 10.1 %collective-permute-start.3 = (f32[64,256]{1,0:T(8,128)S(1)}, f32[64,256]{1,0:T(8,128)S(1)}, u32[]{:S(2)}, u32[]{:S(2)}) collective-permute-start(f32[64,256]{1,0:T(8,128)S(1)} %add.79.near), channel_id=1, source_target_pairs={{0,2},{1,3},{2,0},{3,1},{4,6},{5,7},{6,4},{7,5},{8,10},{9,11},{10,... | collective-permute-start | bytes 196616 | tf_op jit(solution)/shard_map/ppermute | solution.py:276
  17.0 5.5 %collective-permute-start.1 = (f32[80,256]{1,0:T(8,128)S(1)}, f32[80,256]{1,0:T(8,128)S(1)}, u32[]{:S(2)}, u32[]{:S(2)}) collective-permute-start(f32[80,256]{1,0:T(8,128)S(1)} %add.78.near.after), channel_id=1, source_target_pairs={{0,2},{1,3},{2,0},{3,1},{4,6},{5,7},{6,4},{7,5},{8,10},{9,11},{10,... | collective-permute-start | bytes 245768 | tf_op jit(solution)/shard_map/ppermute | solution.py:276
  25.6 5.1 %collective-permute-start.5 = (f32[64,256]{1,0:T(8,128)S(1)}, f32[64,256]{1,0:T(8,128)S(1)}, u32[]{:S(2)}, u32[]{:S(2)}) collective-permute-start(f32[64,256]{1,0:T(8,128)S(1)} %add.80.left), channel_id=1, source_target_pairs={{0,8},{4,12},{8,0},{12,4},{16,24},{20,28},{24,16},{28,20},{1,9},{5... | collective-permute-start | bytes 196616 | tf_op jit(solution)/shard_map/ppermute | solution.py:276
  27.2 6.9 %collective-permute-start.10 = (f32[80,256]{1,0:T(8,128)S(1)}, f32[80,256]{1,0:T(8,128)S(1)}, u32[]{:S(2)}, u32[]{:S(2)}) collective-permute-start(f32[80,256]{1,0:T(8,128)S(1)} %add.82), channel_id=1, source_target_pairs={{0,24},{4,28},{8,16},{12,20},{16,8},{20,12},{24,0},{28,4},{1,25},{... | collective-permute-start | bytes 245768 | tf_op jit(solution)/shard_map/ppermute | solution.py:276
  28.7 5.8 %collective-permute-start.9 = (f32[80,256]{1,0:T(8,128)S(1)}, f32[80,256]{1,0:T(8,128)S(1)}, u32[]{:S(2)}, u32[]{:S(2)}) collective-permute-start(f32[80,256]{1,0:T(8,128)S(1)} %add.82), channel_id=1, source_target_pairs={{0,16},{4,20},{8,24},{12,28},{16,0},{20,4},{24,8},{28,12},{1,17},{... | collective-permute-start | bytes 245768 | tf_op jit(solution)/shard_map/ppermute | solution.py:276
  39.5 5.5 %collective-permute-start.15 = (f32[64,256]{1,0:T(8,128)S(1)}, f32[64,256]{1,0:T(8,128)S(1)}, u32[]{:S(2)}, u32[]{:S(2)}) collective-permute-start(f32[64,256]{1,0:T(8,128)S(1)} %dest_lower.5.left), channel_id=1, source_target_pairs={{0,1},{1,0},{2,3},{3,2},{4,5},{5,4},{6,7},{7,6},{8,9},{9,8},{10,11... | collective-permute-start | bytes 196616 | tf_op jit(solution)/shard_map/ppermute | solution.py:276
  42.7 7.5 %collective-permute-start.14 = (f32[80,256]{1,0:T(8,128)S(1)}, f32[80,256]{1,0:T(8,128)S(1)}, u32[]{:S(2)}, u32[]{:S(2)}) collective-permute-start(f32[80,256]{1,0:T(8,128)S(1)} %add.83.near), channel_id=1, source_target_pairs={{0,2},{1,3},{2,0},{3,1},{4,6},{5,7},{6,4},{7,5},{8,10},{9,11},{10,... | collective-permute-start | bytes 245768 | tf_op jit(solution)/shard_map/ppermute | solution.py:276
  45.0 6.3 %collective-permute-start.16 = (f32[64,256]{1,0:T(8,128)S(1)}, f32[64,256]{1,0:T(8,128)S(1)}, u32[]{:S(2)}, u32[]{:S(2)}) collective-permute-start(f32[64,256]{1,0:T(8,128)S(1)} %add.84.near), channel_id=1, source_target_pairs={{0,2},{1,3},{2,0},{3,1},{4,6},{5,7},{6,4},{7,5},{8,10},{9,11},{10,... | collective-permute-start | bytes 196616 | tf_op jit(solution)/shard_map/ppermute | solution.py:276
  54.3 7.1 %collective-permute-start.23 = (f32[80,256]{1,0:T(8,128)S(1)}, f32[80,256]{1,0:T(8,128)S(1)}, u32[]{:S(2)}, u32[]{:S(2)}) collective-permute-start(f32[80,256]{1,0:T(8,128)S(1)} %add.87), channel_id=1, source_target_pairs={{0,24},{4,28},{8,16},{12,20},{16,8},{20,12},{24,0},{28,4},{1,25},{... | collective-permute-start | bytes 245768 | tf_op jit(solution)/shard_map/ppermute | solution.py:276
  55.6 5.9 %collective-permute-start.22 = (f32[80,256]{1,0:T(8,128)S(1)}, f32[80,256]{1,0:T(8,128)S(1)}, u32[]{:S(2)}, u32[]{:S(2)}) collective-permute-start(f32[80,256]{1,0:T(8,128)S(1)} %add.87), channel_id=1, source_target_pairs={{0,16},{4,20},{8,24},{12,28},{16,0},{20,4},{24,8},{28,12},{1,17},{... | collective-permute-start | bytes 245768 | tf_op jit(solution)/shard_map/ppermute | solution.py:276
  66.8 5.7 %collective-permute-start.28 = (f32[64,256]{1,0:T(8,128)S(1)}, f32[64,256]{1,0:T(8,128)S(1)}, u32[]{:S(2)}, u32[]{:S(2)}) collective-permute-start(f32[64,256]{1,0:T(8,128)S(1)} %dest_lower.6.left), channel_id=1, source_target_pairs={{0,1},{1,0},{2,3},{3,2},{4,5},{5,4},{6,7},{7,6},{8,9},{9,8},{10,11... | collective-permute-start | bytes 196616 | tf_op jit(solution)/shard_map/ppermute | solution.py:276
  69.5 6.4 %collective-permute-start.27 = (f32[80,256]{1,0:T(8,128)S(1)}, f32[80,256]{1,0:T(8,128)S(1)}, u32[]{:S(2)}, u32[]{:S(2)}) collective-permute-start(f32[80,256]{1,0:T(8,128)S(1)} %add.88.near), channel_id=1, source_target_pairs={{0,2},{1,3},{2,0},{3,1},{4,6},{5,7},{6,4},{7,5},{8,10},{9,11},{10,... | collective-permute-start | bytes 245768 | tf_op jit(solution)/shard_map/ppermute | solution.py:276
  72.5 6.2 %collective-permute-start.29 = (f32[64,256]{1,0:T(8,128)S(1)}, f32[64,256]{1,0:T(8,128)S(1)}, u32[]{:S(2)}, u32[]{:S(2)}) collective-permute-start(f32[64,256]{1,0:T(8,128)S(1)} %add.89.near), channel_id=1, source_target_pairs={{0,2},{1,3},{2,0},{3,1},{4,6},{5,7},{6,4},{7,5},{8,10},{9,11},{10,... | collective-permute-start | bytes 196616 | tf_op jit(solution)/shard_map/ppermute | solution.py:276
  82.0 6.9 %collective-permute-start.36 = (f32[80,256]{1,0:T(8,128)S(1)}, f32[80,256]{1,0:T(8,128)S(1)}, u32[]{:S(2)}, u32[]{:S(2)}) collective-permute-start(f32[80,256]{1,0:T(8,128)S(1)} %add.92), channel_id=1, source_target_pairs={{0,24},{4,28},{8,16},{12,20},{16,8},{20,12},{24,0},{28,4},{1,25},{... | collective-permute-start | bytes 245768 | tf_op jit(solution)/shard_map/ppermute | solution.py:276
  83.4 5.9 %collective-permute-start.35 = (f32[80,256]{1,0:T(8,128)S(1)}, f32[80,256]{1,0:T(8,128)S(1)}, u32[]{:S(2)}, u32[]{:S(2)}) collective-permute-start(f32[80,256]{1,0:T(8,128)S(1)} %add.92), channel_id=1, source_target_pairs={{0,16},{4,20},{8,24},{12,28},{16,0},{20,4},{24,8},{28,12},{1,17},{... | collective-permute-start | bytes 245768 | tf_op jit(solution)/shard_map/ppermute | solution.py:276
  94.4 5.7 %collective-permute-start.41 = (f32[64,256]{1,0:T(8,128)S(1)}, f32[64,256]{1,0:T(8,128)S(1)}, u32[]{:S(2)}, u32[]{:S(2)}) collective-permute-start(f32[64,256]{1,0:T(8,128)S(1)} %dest_lower.7.left), channel_id=1, source_target_pairs={{0,1},{1,0},{2,3},{3,2},{4,5},{5,4},{6,7},{7,6},{8,9},{9,8},{10,11... | collective-permute-start | bytes 196616 | tf_op jit(solution)/shard_map/ppermute | solution.py:276
  97.2 6.3 %collective-permute-start.40 = (f32[80,256]{1,0:T(8,128)S(1)}, f32[80,256]{1,0:T(8,128)S(1)}, u32[]{:S(2)}, u32[]{:S(2)}) collective-permute-start(f32[80,256]{1,0:T(8,128)S(1)} %add.93.near), channel_id=1, source_target_pairs={{0,2},{1,3},{2,0},{3,1},{4,6},{5,7},{6,4},{7,5},{8,10},{9,11},{10,... | collective-permute-start | bytes 245768 | tf_op jit(solution)/shard_map/ppermute | solution.py:276
  100.2 6.1 %collective-permute-start.42 = (f32[64,256]{1,0:T(8,128)S(1)}, f32[64,256]{1,0:T(8,128)S(1)}, u32[]{:S(2)}, u32[]{:S(2)}) collective-permute-start(f32[64,256]{1,0:T(8,128)S(1)} %add.94.near), channel_id=1, source_target_pairs={{0,2},{1,3},{2,0},{3,1},{4,6},{5,7},{6,4},{7,5},{8,10},{9,11},{10,... | collective-permute-start | bytes 196616 | tf_op jit(solution)/shard_map/ppermute | solution.py:276
  109.2 7.2 %collective-permute-start.49 = (f32[80,256]{1,0:T(8,128)S(1)}, f32[80,256]{1,0:T(8,128)S(1)}, u32[]{:S(2)}, u32[]{:S(2)}) collective-permute-start(f32[80,256]{1,0:T(8,128)S(1)} %add.97), channel_id=1, source_target_pairs={{0,24},{4,28},{8,16},{12,20},{16,8},{20,12},{24,0},{28,4},{1,25},{... | collective-permute-start | bytes 245768 | tf_op jit(solution)/shard_map/ppermute | solution.py:276
  110.8 5.9 %collective-permute-start.48 = (f32[80,256]{1,0:T(8,128)S(1)}, f32[80,256]{1,0:T(8,128)S(1)}, u32[]{:S(2)}, u32[]{:S(2)}) collective-permute-start(f32[80,256]{1,0:T(8,128)S(1)} %add.97), channel_id=1, source_target_pairs={{0,16},{4,20},{8,24},{12,28},{16,0},{20,4},{24,8},{28,12},{1,17},{... | collective-permute-start | bytes 245768 | tf_op jit(solution)/shard_map/ppermute | solution.py:276
  121.7 5.7 %collective-permute-start.54 = (f32[64,256]{1,0:T(8,128)S(1)}, f32[64,256]{1,0:T(8,128)S(1)}, u32[]{:S(2)}, u32[]{:S(2)}) collective-permute-start(f32[64,256]{1,0:T(8,128)S(1)} %dest_lower.8.left), channel_id=1, source_target_pairs={{0,1},{1,0},{2,3},{3,2},{4,5},{5,4},{6,7},{7,6},{8,9},{9,8},{10,11... | collective-permute-start | bytes 196616 | tf_op jit(solution)/shard_map/ppermute | solution.py:276
  124.4 6.1 %collective-permute-start.53 = (f32[80,256]{1,0:T(8,128)S(1)}, f32[80,256]{1,0:T(8,128)S(1)}, u32[]{:S(2)}, u32[]{:S(2)}) collective-permute-start(f32[80,256]{1,0:T(8,128)S(1)} %add.98.near), channel_id=1, source_target_pairs={{0,2},{1,3},{2,0},{3,1},{4,6},{5,7},{6,4},{7,5},{8,10},{9,11},{10,... | collective-permute-start | bytes 245768 | tf_op jit(solution)/shard_map/ppermute | solution.py:276
  127.5 6.1 %collective-permute-start.55 = (f32[64,256]{1,0:T(8,128)S(1)}, f32[64,256]{1,0:T(8,128)S(1)}, u32[]{:S(2)}, u32[]{:S(2)}) collective-permute-start(f32[64,256]{1,0:T(8,128)S(1)} %add.99.near), channel_id=1, source_target_pairs={{0,2},{1,3},{2,0},{3,1},{4,6},{5,7},{6,4},{7,5},{8,10},{9,11},{10,... | collective-permute-start | bytes 196616 | tf_op jit(solution)/shard_map/ppermute | solution.py:276
  136.8 6.8 %collective-permute-start.62 = (f32[80,256]{1,0:T(8,128)S(1)}, f32[80,256]{1,0:T(8,128)S(1)}, u32[]{:S(2)}, u32[]{:S(2)}) collective-permute-start(f32[80,256]{1,0:T(8,128)S(1)} %add.102), channel_id=1, source_target_pairs={{0,24},{4,28},{8,16},{12,20},{16,8},{20,12},{24,0},{28,4},{1,25},{... | collective-permute-start | bytes 245768 | tf_op jit(solution)/shard_map/ppermute | solution.py:276
  138.3 5.9 %collective-permute-start.61 = (f32[80,256]{1,0:T(8,128)S(1)}, f32[80,256]{1,0:T(8,128)S(1)}, u32[]{:S(2)}, u32[]{:S(2)}) collective-permute-start(f32[80,256]{1,0:T(8,128)S(1)} %add.102), channel_id=1, source_target_pairs={{0,16},{4,20},{8,24},{12,28},{16,0},{20,4},{24,8},{28,12},{1,17},{... | collective-permute-start | bytes 245768 | tf_op jit(solution)/shard_map/ppermute | solution.py:276
  149.5 5.7 %collective-permute-start.67 = (f32[64,256]{1,0:T(8,128)S(1)}, f32[64,256]{1,0:T(8,128)S(1)}, u32[]{:S(2)}, u32[]{:S(2)}) collective-permute-start(f32[64,256]{1,0:T(8,128)S(1)} %dest_lower.9.left), channel_id=1, source_target_pairs={{0,1},{1,0},{2,3},{3,2},{4,5},{5,4},{6,7},{7,6},{8,9},{9,8},{10,11... | collective-permute-start | bytes 196616 | tf_op jit(solution)/shard_map/ppermute | solution.py:276
  152.0 6.5 %collective-permute-start.66 = (f32[80,256]{1,0:T(8,128)S(1)}, f32[80,256]{1,0:T(8,128)S(1)}, u32[]{:S(2)}, u32[]{:S(2)}) collective-permute-start(f32[80,256]{1,0:T(8,128)S(1)} %add.103.near), channel_id=1, source_target_pairs={{0,2},{1,3},{2,0},{3,1},{4,6},{5,7},{6,4},{7,5},{8,10},{9,11},{10,... | collective-permute-start | bytes 245768 | tf_op jit(solution)/shard_map/ppermute | solution.py:276
  155.2 6.1 %collective-permute-start.68 = (f32[64,256]{1,0:T(8,128)S(1)}, f32[64,256]{1,0:T(8,128)S(1)}, u32[]{:S(2)}, u32[]{:S(2)}) collective-permute-start(f32[64,256]{1,0:T(8,128)S(1)} %add.104.near), channel_id=1, source_target_pairs={{0,2},{1,3},{2,0},{3,1},{4,6},{5,7},{6,4},{7,5},{8,10},{9,11},{10,... | collective-permute-start | bytes 196616 | tf_op jit(solution)/shard_map/ppermute | solution.py:276
  164.4 7.1 %collective-permute-start.75 = (f32[80,256]{1,0:T(8,128)S(1)}, f32[80,256]{1,0:T(8,128)S(1)}, u32[]{:S(2)}, u32[]{:S(2)}) collective-permute-start(f32[80,256]{1,0:T(8,128)S(1)} %add.107), channel_id=1, source_target_pairs={{0,24},{4,28},{8,16},{12,20},{16,8},{20,12},{24,0},{28,4},{1,25},{... | collective-permute-start | bytes 245768 | tf_op jit(solution)/shard_map/ppermute | solution.py:276
  165.8 5.8 %collective-permute-start.74 = (f32[80,256]{1,0:T(8,128)S(1)}, f32[80,256]{1,0:T(8,128)S(1)}, u32[]{:S(2)}, u32[]{:S(2)}) collective-permute-start(f32[80,256]{1,0:T(8,128)S(1)} %add.107), channel_id=1, source_target_pairs={{0,16},{4,20},{8,24},{12,28},{16,0},{20,4},{24,8},{28,12},{1,17},{... | collective-permute-start | bytes 245768 | tf_op jit(solution)/shard_map/ppermute | solution.py:276
  (47 other events, 155.2 us)

commit v7 on v6

--- a/solution.py
+++ b/solution.py
@@ -280,17 +280,24 @@
     return call(add_kernel, [(left.shape, F32)], "add", HINT, left, right)
 
 
-def sum_steps(message, axis, mask):
+def masks(axis, first):
     size = lax.axis_size(axis)
-    while 2 * mask < size:
+    return [1 << bit for bit in range(size.bit_length() - 1) if 1 << bit >= first]
+
+
+def far_first(axis):
+    return [lax.axis_size(axis) - 1, *masks(axis, 1)[-2::-1]]
+
+
+def sum_steps(message, axis, steps):
+    for mask in steps[:-1]:
         message = add(message, swap(message, axis, mask))
-        mask *= 2
-    return message, swap(message, axis, mask)
+    return message, swap(message, axis, steps[-1])
 
 
 def sum_at_once(message):
     if lax.axis_size("org") != 8:
-        return sum_steps(message, "org", 2)
+        return sum_steps(message, "org", masks("org", 2))
     return message + swap(message, "org", 2), swap(message, "org", 4) + swap(message, "org", 6)
 
 
@@ -332,8 +339,8 @@
     upper, lower = anchor_factor[:, :width], anchor_factor[:, width:]
     matrix, factor, part_factor = ((rank, rank), F32), ((rank, width), F32), ((rank, part_size), F32)
     for sweep in range(SWEEPS):
-        near, far = sum_steps(message, "dst", 1)
-        near_low, far_low = sum_steps(message_low, "dst", 1)
+        near, far = sum_steps(message, "dst", masks("dst", 1))
+        near_low, far_low = sum_steps(message_low, "dst", far_first("dst"))
         if sweep == 0:
             flipped = call(flip_kernel, [((hours, cols, rows), BF16)], "flip", 4 * half_flops, tensor, near)
         upper, gram_part, gram, sent, kept = call(
@@ -354,7 +361,7 @@
             lower_kept_kernel, [part_factor, ((anchor_rows, part_size), F32)], "lower_kept", half_flops // 2,
             tensor, lower, hour_t, kept, sent_late,
         )
-        near, far = sum_steps(add(kept, received), "org", 2)
+        near, far = sum_steps(add(kept, received), "org", masks("org", 2))
         near_late, far_late = sum_at_once(add(kept_late, received_late))
         late_own, gram_part = call(
             dest_late_kernel, [part_factor, matrix], "dest_late", 0, late_own, near_late, far_late, hour_gram

time: 175 us -> 169 us (0.966)
  starting transfers between devices: 83.8 us -> 71.3 us
  waiting for transfers between devices: 48.3 us -> 54.9 us
    ppermute x78, starting transfers between devices: 83.8 us -> 71.3 us  [swap(): lax.ppermute(array, axis, [(index, index ^ mask) for index in range(size)])]
    ppermute x78, waiting for transfers between devices: 48.3 us -> 54.9 us  [swap(): lax.ppermute(array, axis, [(index, index ^ mask) for index in range(size)])]
  transfers between devices with their start and end apart: 78 -> 78, of which waited for: 35 -> 37; matrix products, arithmetic and copies ran while one was open for 0% -> 0% of each run, Pallas kernels for 16% -> 17%
where the time goes in v7:
time: 169 us
  starting transfers between devices  71.3 us (42%)
  waiting for transfers between devices  54.9 us (32%)
  Pallas kernels  41.1 us (24%)
  between operations  1.71 us (1%)
    ppermute x78, starting transfers between devices, swap(): lax.ppermute(array, axis, [(index, index ^ mask) for index in range(size)])  71.3 us
    ppermute x78, waiting for transfers between devices, swap(): lax.ppermute(array, axis, [(index, index ^ mask) for index in range(size)])  54.9 us
    pallas_call x92, Pallas kernels, call(): pl.pallas_call(kernel, in_specs=[WHOLE] * len(args), out_specs=tuple((WHO...  32.4 us
    pallas_call x1, Pallas kernels, body(): pl.pallas_call(first_kernel, in_specs=[ANYWHERE] * 4, out_specs=(WHOLE,)...  7.31 us
  transfers between devices with their start and end apart: 78, of which 37 were waited for; matrix products, arithmetic and copies ran while one was open for 0% of the time, Pallas kernels for 17%

profile of v7, /device:TPU:0, one launch (start us, length us, event | category | flops | bytes accessed | tf_op | source)
XLA Modules:
  0.0 169.2 jit_solution(3342251877004697156)
XLA Ops:
  0.6 7.3 %first.1 = (bf16[8,512,1024]{2,1,0:T(8,128)(2,1)S(1)}, f32[80,256]{1,0:T(8,128)S(1)}, f32[64,256]{1,0:T(8,128)S(1)}, f32[64,256]{1,0:T(8,128)S(1)}, f32[64,256]{...) custom-call(s32[8,512,1024]{2,1,0:T(8,128)} %counts.1, f32[8,4,8]{2,1,0:T(4,128)} %scales.1, ...), custom_call_target="tpu_custom_call" | custom-call | tf_op jit(solution)/shard_map/first/pallas_call | solution.py:314
  8.0 5.1 %collective-permute-start.2 = (f32[64,256]{1,0:T(8,128)S(1)}, f32[64,256]{1,0:T(8,128)S(1)}, u32[]{:S(2)}, u32[]{:S(2)}) collective-permute-start(f32[64,256]{1,0:T(8,128)S(1)} %get-tuple-element.128.left), channel_id=1, source_target_pairs={{0,3},{1,2},{2,1},{3,0},{4,7},{5,6},{6,5},{7,4},{8,11},{9,10},{10,... | collective-permute-start | bytes 196616 | tf_op jit(solution)/shard_map/ppermute | solution.py:276
  13.1 2.9 %collective-permute-done.2.right = f32[64,256]{1,0:T(8,128)S(1)} collective-permute-done((f32[64,256]{1,0:T(8,128)S(1)}, f32[64,256]{1,0:T(8,128)S(1)}, u32[]{:S(2)}, u32[]{:S(2)}) %collective-permute-start.2) | collective-permute-done | bytes 65568 | tf_op jit(solution)/shard_map/ppermute | solution.py:276
  16.4 1.8 %collective-permute-done.right = f32[80,256]{1,0:T(8,128)S(1)} collective-permute-done((f32[80,256]{1,0:T(8,128)S(1)}, f32[80,256]{1,0:T(8,128)S(1)}, u32[]{:S(2)}, u32[]{:S(2)}) %collective-permute-start) | collective-permute-done | bytes 81952 | tf_op jit(solution)/shard_map/ppermute | solution.py:276
  18.2 2.4 %collective-permute-start.1 = (f32[80,256]{1,0:T(8,128)S(1)}, f32[80,256]{1,0:T(8,128)S(1)}, u32[]{:S(2)}, u32[]{:S(2)}) collective-permute-start(f32[80,256]{1,0:T(8,128)S(1)} %add.78.near.after), channel_id=1, source_target_pairs={{0,2},{1,3},{2,0},{3,1},{4,6},{5,7},{6,4},{7,5},{8,10},{9,11},{10,... | collective-permute-start | bytes 245768 | tf_op jit(solution)/shard_map/ppermute | solution.py:276
  20.6 2.2 %flip.1._.flipped = bf16[8,1024,512]{2,1,0:T(8,128)(2,1)S(1)} custom-call(bf16[8,512,1024]{2,1,0:T(8,128)(2,1)S(1)} %get-tuple-element.122.tensor, f32[80,256]{1,0:T(8,128)S(1)} %add.78.near.after), custom_call_target="tpu_custom_call" | custom-call | flops 4294967296 | tf_op jit(solution)/shard_map/flip/pallas_call | solution.py:262
  22.8 1.6 collective-permute-done.1.far
  27.6 1.5 collective-permute-start.5
  29.2 1.6 collective-permute-start.10
  32.7 1.6 collective-permute-start.6
  34.3 1.7 %collective-permute-done.8 = f32[80,256]{1,0:T(8,128)S(1)} collective-permute-done((f32[80,256]{1,0:T(8,128)S(1)}, f32[80,256]{1,0:T(8,128)S(1)}, u32[]{:S(2)}, u32[]{:S(2)}) %collective-permute-start.8) | collective-permute-done | bytes 81952 | tf_op jit(solution)/shard_map/ppermute | solution.py:276
  40.5 2.6 %collective-permute-start.15 = (f32[64,256]{1,0:T(8,128)S(1)}, f32[64,256]{1,0:T(8,128)S(1)}, u32[]{:S(2)}, u32[]{:S(2)}) collective-permute-start(f32[64,256]{1,0:T(8,128)S(1)} %dest_lower.5.left), channel_id=1, source_target_pairs={{0,3},{1,2},{2,1},{3,0},{4,7},{5,6},{6,5},{7,4},{8,11},{9,10},{10,... | collective-permute-start | bytes 196616 | tf_op jit(solution)/shard_map/ppermute | solution.py:276
  44.4 1.9 %collective-permute-start.14 = (f32[80,256]{1,0:T(8,128)S(1)}, f32[80,256]{1,0:T(8,128)S(1)}, u32[]{:S(2)}, u32[]{:S(2)}) collective-permute-start(f32[80,256]{1,0:T(8,128)S(1)} %add.83.near), channel_id=1, source_target_pairs={{0,2},{1,3},{2,0},{3,1},{4,6},{5,7},{6,4},{7,5},{8,10},{9,11},{10,... | collective-permute-start | bytes 245768 | tf_op jit(solution)/shard_map/ppermute | solution.py:276
  47.8 3.2 %collective-permute-done.14.far = f32[80,256]{1,0:T(8,128)S(1)} collective-permute-done((f32[80,256]{1,0:T(8,128)S(1)}, f32[80,256]{1,0:T(8,128)S(1)}, u32[]{:S(2)}, u32[]{:S(2)}) %collective-permute-start.14) | collective-permute-done | bytes 81952 | tf_op jit(solution)/shard_map/ppermute | solution.py:276
  60.2 2.1 %collective-permute-done.21 = f32[80,256]{1,0:T(8,128)S(1)} collective-permute-done((f32[80,256]{1,0:T(8,128)S(1)}, f32[80,256]{1,0:T(8,128)S(1)}, u32[]{:S(2)}, u32[]{:S(2)}) %collective-permute-start.21) | collective-permute-done | bytes 81952 | tf_op jit(solution)/shard_map/ppermute | solution.py:276
  68.6 1.6 collective-permute-done.26.right
  71.3 2.0 %collective-permute-done.28.right = f32[64,256]{1,0:T(8,128)S(1)} collective-permute-done((f32[64,256]{1,0:T(8,128)S(1)}, f32[64,256]{1,0:T(8,128)S(1)}, u32[]{:S(2)}, u32[]{:S(2)}) %collective-permute-start.28) | collective-permute-done | bytes 65568 | tf_op jit(solution)/shard_map/ppermute | solution.py:276
  73.4 3.4 %collective-permute-done.27.far = f32[80,256]{1,0:T(8,128)S(1)} collective-permute-done((f32[80,256]{1,0:T(8,128)S(1)}, f32[80,256]{1,0:T(8,128)S(1)}, u32[]{:S(2)}, u32[]{:S(2)}) %collective-permute-start.27) | collective-permute-done | bytes 81952 | tf_op jit(solution)/shard_map/ppermute | solution.py:276
  85.8 2.3 %collective-permute-done.34 = f32[80,256]{1,0:T(8,128)S(1)} collective-permute-done((f32[80,256]{1,0:T(8,128)S(1)}, f32[80,256]{1,0:T(8,128)S(1)}, u32[]{:S(2)}, u32[]{:S(2)}) %collective-permute-start.34) | collective-permute-done | bytes 81952 | tf_op jit(solution)/shard_map/ppermute | solution.py:276
  92.3 2.3 %collective-permute-start.41 = (f32[64,256]{1,0:T(8,128)S(1)}, f32[64,256]{1,0:T(8,128)S(1)}, u32[]{:S(2)}, u32[]{:S(2)}) collective-permute-start(f32[64,256]{1,0:T(8,128)S(1)} %dest_lower.7.left), channel_id=1, source_target_pairs={{0,3},{1,2},{2,1},{3,0},{4,7},{5,6},{6,5},{7,4},{8,11},{9,10},{10,... | collective-permute-start | bytes 196616 | tf_op jit(solution)/shard_map/ppermute | solution.py:276
  94.6 1.8 %collective-permute-done.39.right = f32[80,256]{1,0:T(8,128)S(1)} collective-permute-done((f32[80,256]{1,0:T(8,128)S(1)}, f32[80,256]{1,0:T(8,128)S(1)}, u32[]{:S(2)}, u32[]{:S(2)}) %collective-permute-start.39) | collective-permute-done | bytes 81952 | tf_op jit(solution)/shard_map/ppermute | solution.py:276
  99.6 3.1 %collective-permute-done.40.far = f32[80,256]{1,0:T(8,128)S(1)} collective-permute-done((f32[80,256]{1,0:T(8,128)S(1)}, f32[80,256]{1,0:T(8,128)S(1)}, u32[]{:S(2)}, u32[]{:S(2)}) %collective-permute-start.40) | collective-permute-done | bytes 81952 | tf_op jit(solution)/shard_map/ppermute | solution.py:276
  111.6 2.5 %collective-permute-done.47 = f32[80,256]{1,0:T(8,128)S(1)} collective-permute-done((f32[80,256]{1,0:T(8,128)S(1)}, f32[80,256]{1,0:T(8,128)S(1)}, u32[]{:S(2)}, u32[]{:S(2)}) %collective-permute-start.47) | collective-permute-done | bytes 81952 | tf_op jit(solution)/shard_map/ppermute | solution.py:276
  118.3 2.2 %collective-permute-start.54 = (f32[64,256]{1,0:T(8,128)S(1)}, f32[64,256]{1,0:T(8,128)S(1)}, u32[]{:S(2)}, u32[]{:S(2)}) collective-permute-start(f32[64,256]{1,0:T(8,128)S(1)} %dest_lower.8.left), channel_id=1, source_target_pairs={{0,3},{1,2},{2,1},{3,0},{4,7},{5,6},{6,5},{7,4},{8,11},{9,10},{10,... | collective-permute-start | bytes 196616 | tf_op jit(solution)/shard_map/ppermute | solution.py:276
  125.6 2.7 %collective-permute-done.53.far = f32[80,256]{1,0:T(8,128)S(1)} collective-permute-done((f32[80,256]{1,0:T(8,128)S(1)}, f32[80,256]{1,0:T(8,128)S(1)}, u32[]{:S(2)}, u32[]{:S(2)}) %collective-permute-start.53) | collective-permute-done | bytes 81952 | tf_op jit(solution)/shard_map/ppermute | solution.py:276
  132.8 1.6 collective-permute-start.62
  137.7 1.9 %collective-permute-done.60 = f32[80,256]{1,0:T(8,128)S(1)} collective-permute-done((f32[80,256]{1,0:T(8,128)S(1)}, f32[80,256]{1,0:T(8,128)S(1)}, u32[]{:S(2)}, u32[]{:S(2)}) %collective-permute-start.60) | collective-permute-done | bytes 81952 | tf_op jit(solution)/shard_map/ppermute | solution.py:276
  145.7 2.4 %collective-permute-done.65.right = f32[80,256]{1,0:T(8,128)S(1)} collective-permute-done((f32[80,256]{1,0:T(8,128)S(1)}, f32[80,256]{1,0:T(8,128)S(1)}, u32[]{:S(2)}, u32[]{:S(2)}) %collective-permute-start.65) | collective-permute-done | bytes 81952 | tf_op jit(solution)/shard_map/ppermute | solution.py:276
  148.5 1.8 %collective-permute-done.67.right = f32[64,256]{1,0:T(8,128)S(1)} collective-permute-done((f32[64,256]{1,0:T(8,128)S(1)}, f32[64,256]{1,0:T(8,128)S(1)}, u32[]{:S(2)}, u32[]{:S(2)}) %collective-permute-start.67) | collective-permute-done | bytes 65568 | tf_op jit(solution)/shard_map/ppermute | solution.py:276
  151.3 3.0 %collective-permute-done.66.far = f32[80,256]{1,0:T(8,128)S(1)} collective-permute-done((f32[80,256]{1,0:T(8,128)S(1)}, f32[80,256]{1,0:T(8,128)S(1)}, u32[]{:S(2)}, u32[]{:S(2)}) %collective-permute-start.66) | collective-permute-done | bytes 81952 | tf_op jit(solution)/shard_map/ppermute | solution.py:276
  158.3 1.5 collective-permute-start.75
  163.2 2.4 %collective-permute-done.73 = f32[80,256]{1,0:T(8,128)S(1)} collective-permute-done((f32[80,256]{1,0:T(8,128)S(1)}, f32[80,256]{1,0:T(8,128)S(1)}, u32[]{:S(2)}, u32[]{:S(2)}) %collective-permute-start.73) | collective-permute-done | bytes 81952 | tf_op jit(solution)/shard_map/ppermute | solution.py:276
  (234 shorter events, 89.3 us)
Async XLA Ops:
  8.0 8.0 %collective-permute-start.2 = (f32[64,256]{1,0:T(8,128)S(1)}, f32[64,256]{1,0:T(8,128)S(1)}, u32[]{:S(2)}, u32[]{:S(2)}) collective-permute-start(f32[64,256]{1,0:T(8,128)S(1)} %get-tuple-element.128.left), channel_id=1, source_target_pairs={{0,3},{1,2},{2,1},{3,0},{4,7},{5,6},{6,5},{7,4},{8,11},{9,10},{10,... | collective-permute-start | bytes 196616 | tf_op jit(solution)/shard_map/ppermute | solution.py:276
  13.1 5.1 %collective-permute-start = (f32[80,256]{1,0:T(8,128)S(1)}, f32[80,256]{1,0:T(8,128)S(1)}, u32[]{:S(2)}, u32[]{:S(2)}) collective-permute-start(f32[80,256]{1,0:T(8,128)S(1)} %get-tuple-element.123.left), channel_id=1, source_target_pairs={{0,1},{1,0},{2,3},{3,2},{4,5},{5,4},{6,7},{7,6},{8,9},{9,8},{10,11... | collective-permute-start | bytes 245768 | tf_op jit(solution)/shard_map/ppermute | solution.py:276
  16.0 9.6 %collective-permute-start.3 = (f32[64,256]{1,0:T(8,128)S(1)}, f32[64,256]{1,0:T(8,128)S(1)}, u32[]{:S(2)}, u32[]{:S(2)}) collective-permute-start(f32[64,256]{1,0:T(8,128)S(1)} %add.79.near), channel_id=1, source_target_pairs={{0,1},{1,0},{2,3},{3,2},{4,5},{5,4},{6,7},{7,6},{8,9},{9,8},{10,11... | collective-permute-start | bytes 196616 | tf_op jit(solution)/shard_map/ppermute | solution.py:276
  18.2 6.3 %collective-permute-start.1 = (f32[80,256]{1,0:T(8,128)S(1)}, f32[80,256]{1,0:T(8,128)S(1)}, u32[]{:S(2)}, u32[]{:S(2)}) collective-permute-start(f32[80,256]{1,0:T(8,128)S(1)} %add.78.near.after), channel_id=1, source_target_pairs={{0,2},{1,3},{2,0},{3,1},{4,6},{5,7},{6,4},{7,5},{8,10},{9,11},{10,... | collective-permute-start | bytes 245768 | tf_op jit(solution)/shard_map/ppermute | solution.py:276
  27.6 5.1 %collective-permute-start.5 = (f32[64,256]{1,0:T(8,128)S(1)}, f32[64,256]{1,0:T(8,128)S(1)}, u32[]{:S(2)}, u32[]{:S(2)}) collective-permute-start(f32[64,256]{1,0:T(8,128)S(1)} %add.80.left), channel_id=1, source_target_pairs={{0,8},{4,12},{8,0},{12,4},{16,24},{20,28},{24,16},{28,20},{1,9},{5... | collective-permute-start | bytes 196616 | tf_op jit(solution)/shard_map/ppermute | solution.py:276
  29.2 6.9 %collective-permute-start.10 = (f32[80,256]{1,0:T(8,128)S(1)}, f32[80,256]{1,0:T(8,128)S(1)}, u32[]{:S(2)}, u32[]{:S(2)}) collective-permute-start(f32[80,256]{1,0:T(8,128)S(1)} %add.82), channel_id=1, source_target_pairs={{0,24},{4,28},{8,16},{12,20},{16,8},{20,12},{24,0},{28,4},{1,25},{... | collective-permute-start | bytes 245768 | tf_op jit(solution)/shard_map/ppermute | solution.py:276
  30.7 5.8 %collective-permute-start.9 = (f32[80,256]{1,0:T(8,128)S(1)}, f32[80,256]{1,0:T(8,128)S(1)}, u32[]{:S(2)}, u32[]{:S(2)}) collective-permute-start(f32[80,256]{1,0:T(8,128)S(1)} %add.82), channel_id=1, source_target_pairs={{0,16},{4,20},{8,24},{12,28},{16,0},{20,4},{24,8},{28,12},{1,17},{... | collective-permute-start | bytes 245768 | tf_op jit(solution)/shard_map/ppermute | solution.py:276
  32.7 5.0 %collective-permute-start.6 = (f32[64,256]{1,0:T(8,128)S(1)}, f32[64,256]{1,0:T(8,128)S(1)}, u32[]{:S(2)}, u32[]{:S(2)}) collective-permute-start(f32[64,256]{1,0:T(8,128)S(1)} %add.81.near), channel_id=1, source_target_pairs={{0,16},{4,20},{8,24},{12,28},{16,0},{20,4},{24,8},{28,12},{1,17},{... | collective-permute-start | bytes 196616 | tf_op jit(solution)/shard_map/ppermute | solution.py:276
  40.5 6.4 %collective-permute-start.15 = (f32[64,256]{1,0:T(8,128)S(1)}, f32[64,256]{1,0:T(8,128)S(1)}, u32[]{:S(2)}, u32[]{:S(2)}) collective-permute-start(f32[64,256]{1,0:T(8,128)S(1)} %dest_lower.5.left), channel_id=1, source_target_pairs={{0,3},{1,2},{2,1},{3,0},{4,7},{5,6},{6,5},{7,4},{8,11},{9,10},{10,... | collective-permute-start | bytes 196616 | tf_op jit(solution)/shard_map/ppermute | solution.py:276
  44.4 6.6 %collective-permute-start.14 = (f32[80,256]{1,0:T(8,128)S(1)}, f32[80,256]{1,0:T(8,128)S(1)}, u32[]{:S(2)}, u32[]{:S(2)}) collective-permute-start(f32[80,256]{1,0:T(8,128)S(1)} %add.83.near), channel_id=1, source_target_pairs={{0,2},{1,3},{2,0},{3,1},{4,6},{5,7},{6,4},{7,5},{8,10},{9,11},{10,... | collective-permute-start | bytes 245768 | tf_op jit(solution)/shard_map/ppermute | solution.py:276
  46.9 5.3 %collective-permute-start.16 = (f32[64,256]{1,0:T(8,128)S(1)}, f32[64,256]{1,0:T(8,128)S(1)}, u32[]{:S(2)}, u32[]{:S(2)}) collective-permute-start(f32[64,256]{1,0:T(8,128)S(1)} %add.84.near), channel_id=1, source_target_pairs={{0,1},{1,0},{2,3},{3,2},{4,5},{5,4},{6,7},{7,6},{8,9},{9,8},{10,11... | collective-permute-start | bytes 196616 | tf_op jit(solution)/shard_map/ppermute | solution.py:276
  55.2 7.1 %collective-permute-start.23 = (f32[80,256]{1,0:T(8,128)S(1)}, f32[80,256]{1,0:T(8,128)S(1)}, u32[]{:S(2)}, u32[]{:S(2)}) collective-permute-start(f32[80,256]{1,0:T(8,128)S(1)} %add.87), channel_id=1, source_target_pairs={{0,24},{4,28},{8,16},{12,20},{16,8},{20,12},{24,0},{28,4},{1,25},{... | collective-permute-start | bytes 245768 | tf_op jit(solution)/shard_map/ppermute | solution.py:276
  56.5 5.9 %collective-permute-start.22 = (f32[80,256]{1,0:T(8,128)S(1)}, f32[80,256]{1,0:T(8,128)S(1)}, u32[]{:S(2)}, u32[]{:S(2)}) collective-permute-start(f32[80,256]{1,0:T(8,128)S(1)} %add.87), channel_id=1, source_target_pairs={{0,16},{4,20},{8,24},{12,28},{16,0},{20,4},{24,8},{28,12},{1,17},{... | collective-permute-start | bytes 245768 | tf_op jit(solution)/shard_map/ppermute | solution.py:276
  67.2 6.1 %collective-permute-start.28 = (f32[64,256]{1,0:T(8,128)S(1)}, f32[64,256]{1,0:T(8,128)S(1)}, u32[]{:S(2)}, u32[]{:S(2)}) collective-permute-start(f32[64,256]{1,0:T(8,128)S(1)} %dest_lower.6.left), channel_id=1, source_target_pairs={{0,3},{1,2},{2,1},{3,0},{4,7},{5,6},{6,5},{7,4},{8,11},{9,10},{10,... | collective-permute-start | bytes 196616 | tf_op jit(solution)/shard_map/ppermute | solution.py:276
  70.2 6.6 %collective-permute-start.27 = (f32[80,256]{1,0:T(8,128)S(1)}, f32[80,256]{1,0:T(8,128)S(1)}, u32[]{:S(2)}, u32[]{:S(2)}) collective-permute-start(f32[80,256]{1,0:T(8,128)S(1)} %add.88.near), channel_id=1, source_target_pairs={{0,2},{1,3},{2,0},{3,1},{4,6},{5,7},{6,4},{7,5},{8,10},{9,11},{10,... | collective-permute-start | bytes 245768 | tf_op jit(solution)/shard_map/ppermute | solution.py:276
  81.3 6.8 %collective-permute-start.36 = (f32[80,256]{1,0:T(8,128)S(1)}, f32[80,256]{1,0:T(8,128)S(1)}, u32[]{:S(2)}, u32[]{:S(2)}) collective-permute-start(f32[80,256]{1,0:T(8,128)S(1)} %add.92), channel_id=1, source_target_pairs={{0,24},{4,28},{8,16},{12,20},{16,8},{20,12},{24,0},{28,4},{1,25},{... | collective-permute-start | bytes 245768 | tf_op jit(solution)/shard_map/ppermute | solution.py:276
  82.6 6.1 %collective-permute-start.35 = (f32[80,256]{1,0:T(8,128)S(1)}, f32[80,256]{1,0:T(8,128)S(1)}, u32[]{:S(2)}, u32[]{:S(2)}) collective-permute-start(f32[80,256]{1,0:T(8,128)S(1)} %add.92), channel_id=1, source_target_pairs={{0,16},{4,20},{8,24},{12,28},{16,0},{20,4},{24,8},{28,12},{1,17},{... | collective-permute-start | bytes 245768 | tf_op jit(solution)/shard_map/ppermute | solution.py:276
  92.3 6.2 %collective-permute-start.41 = (f32[64,256]{1,0:T(8,128)S(1)}, f32[64,256]{1,0:T(8,128)S(1)}, u32[]{:S(2)}, u32[]{:S(2)}) collective-permute-start(f32[64,256]{1,0:T(8,128)S(1)} %dest_lower.7.left), channel_id=1, source_target_pairs={{0,3},{1,2},{2,1},{3,0},{4,7},{5,6},{6,5},{7,4},{8,11},{9,10},{10,... | collective-permute-start | bytes 196616 | tf_op jit(solution)/shard_map/ppermute | solution.py:276
  96.4 6.4 %collective-permute-start.40 = (f32[80,256]{1,0:T(8,128)S(1)}, f32[80,256]{1,0:T(8,128)S(1)}, u32[]{:S(2)}, u32[]{:S(2)}) collective-permute-start(f32[80,256]{1,0:T(8,128)S(1)} %add.93.near), channel_id=1, source_target_pairs={{0,2},{1,3},{2,0},{3,1},{4,6},{5,7},{6,4},{7,5},{8,10},{9,11},{10,... | collective-permute-start | bytes 245768 | tf_op jit(solution)/shard_map/ppermute | solution.py:276
  98.5 5.5 %collective-permute-start.42 = (f32[64,256]{1,0:T(8,128)S(1)}, f32[64,256]{1,0:T(8,128)S(1)}, u32[]{:S(2)}, u32[]{:S(2)}) collective-permute-start(f32[64,256]{1,0:T(8,128)S(1)} %add.94.near), channel_id=1, source_target_pairs={{0,1},{1,0},{2,3},{3,2},{4,5},{5,4},{6,7},{7,6},{8,9},{9,8},{10,11... | collective-permute-start | bytes 196616 | tf_op jit(solution)/shard_map/ppermute | solution.py:276
  106.8 7.2 %collective-permute-start.49 = (f32[80,256]{1,0:T(8,128)S(1)}, f32[80,256]{1,0:T(8,128)S(1)}, u32[]{:S(2)}, u32[]{:S(2)}) collective-permute-start(f32[80,256]{1,0:T(8,128)S(1)} %add.97), channel_id=1, source_target_pairs={{0,24},{4,28},{8,16},{12,20},{16,8},{20,12},{24,0},{28,4},{1,25},{... | collective-permute-start | bytes 245768 | tf_op jit(solution)/shard_map/ppermute | solution.py:276
  108.3 5.8 %collective-permute-start.48 = (f32[80,256]{1,0:T(8,128)S(1)}, f32[80,256]{1,0:T(8,128)S(1)}, u32[]{:S(2)}, u32[]{:S(2)}) collective-permute-start(f32[80,256]{1,0:T(8,128)S(1)} %add.97), channel_id=1, source_target_pairs={{0,16},{4,20},{8,24},{12,28},{16,0},{20,4},{24,8},{28,12},{1,17},{... | collective-permute-start | bytes 245768 | tf_op jit(solution)/shard_map/ppermute | solution.py:276
  118.3 6.2 %collective-permute-start.54 = (f32[64,256]{1,0:T(8,128)S(1)}, f32[64,256]{1,0:T(8,128)S(1)}, u32[]{:S(2)}, u32[]{:S(2)}) collective-permute-start(f32[64,256]{1,0:T(8,128)S(1)} %dest_lower.8.left), channel_id=1, source_target_pairs={{0,3},{1,2},{2,1},{3,0},{4,7},{5,6},{6,5},{7,4},{8,11},{9,10},{10,... | collective-permute-start | bytes 196616 | tf_op jit(solution)/shard_map/ppermute | solution.py:276
  121.9 6.4 %collective-permute-start.53 = (f32[80,256]{1,0:T(8,128)S(1)}, f32[80,256]{1,0:T(8,128)S(1)}, u32[]{:S(2)}, u32[]{:S(2)}) collective-permute-start(f32[80,256]{1,0:T(8,128)S(1)} %add.98.near), channel_id=1, source_target_pairs={{0,2},{1,3},{2,0},{3,1},{4,6},{5,7},{6,4},{7,5},{8,10},{9,11},{10,... | collective-permute-start | bytes 245768 | tf_op jit(solution)/shard_map/ppermute | solution.py:276
  124.5 5.0 %collective-permute-start.55 = (f32[64,256]{1,0:T(8,128)S(1)}, f32[64,256]{1,0:T(8,128)S(1)}, u32[]{:S(2)}, u32[]{:S(2)}) collective-permute-start(f32[64,256]{1,0:T(8,128)S(1)} %add.99.near), channel_id=1, source_target_pairs={{0,1},{1,0},{2,3},{3,2},{4,5},{5,4},{6,7},{7,6},{8,9},{9,8},{10,11... | collective-permute-start | bytes 196616 | tf_op jit(solution)/shard_map/ppermute | solution.py:276
  132.8 6.8 %collective-permute-start.62 = (f32[80,256]{1,0:T(8,128)S(1)}, f32[80,256]{1,0:T(8,128)S(1)}, u32[]{:S(2)}, u32[]{:S(2)}) collective-permute-start(f32[80,256]{1,0:T(8,128)S(1)} %add.102), channel_id=1, source_target_pairs={{0,24},{4,28},{8,16},{12,20},{16,8},{20,12},{24,0},{28,4},{1,25},{... | collective-permute-start | bytes 245768 | tf_op jit(solution)/shard_map/ppermute | solution.py:276
  134.4 5.9 %collective-permute-start.61 = (f32[80,256]{1,0:T(8,128)S(1)}, f32[80,256]{1,0:T(8,128)S(1)}, u32[]{:S(2)}, u32[]{:S(2)}) collective-permute-start(f32[80,256]{1,0:T(8,128)S(1)} %add.102), channel_id=1, source_target_pairs={{0,16},{4,20},{8,24},{12,28},{16,0},{20,4},{24,8},{28,12},{1,17},{... | collective-permute-start | bytes 245768 | tf_op jit(solution)/shard_map/ppermute | solution.py:276
  144.2 6.2 %collective-permute-start.67 = (f32[64,256]{1,0:T(8,128)S(1)}, f32[64,256]{1,0:T(8,128)S(1)}, u32[]{:S(2)}, u32[]{:S(2)}) collective-permute-start(f32[64,256]{1,0:T(8,128)S(1)} %dest_lower.9.left), channel_id=1, source_target_pairs={{0,3},{1,2},{2,1},{3,0},{4,7},{5,6},{6,5},{7,4},{8,11},{9,10},{10,... | collective-permute-start | bytes 196616 | tf_op jit(solution)/shard_map/ppermute | solution.py:276
  148.0 6.2 %collective-permute-start.66 = (f32[80,256]{1,0:T(8,128)S(1)}, f32[80,256]{1,0:T(8,128)S(1)}, u32[]{:S(2)}, u32[]{:S(2)}) collective-permute-start(f32[80,256]{1,0:T(8,128)S(1)} %add.103.near), channel_id=1, source_target_pairs={{0,2},{1,3},{2,0},{3,1},{4,6},{5,7},{6,4},{7,5},{8,10},{9,11},{10,... | collective-permute-start | bytes 245768 | tf_op jit(solution)/shard_map/ppermute | solution.py:276
  150.4 5.1 %collective-permute-start.68 = (f32[64,256]{1,0:T(8,128)S(1)}, f32[64,256]{1,0:T(8,128)S(1)}, u32[]{:S(2)}, u32[]{:S(2)}) collective-permute-start(f32[64,256]{1,0:T(8,128)S(1)} %add.104.near), channel_id=1, source_target_pairs={{0,1},{1,0},{2,3},{3,2},{4,5},{5,4},{6,7},{7,6},{8,9},{9,8},{10,11... | collective-permute-start | bytes 196616 | tf_op jit(solution)/shard_map/ppermute | solution.py:276
  158.3 7.2 %collective-permute-start.75 = (f32[80,256]{1,0:T(8,128)S(1)}, f32[80,256]{1,0:T(8,128)S(1)}, u32[]{:S(2)}, u32[]{:S(2)}) collective-permute-start(f32[80,256]{1,0:T(8,128)S(1)} %add.107), channel_id=1, source_target_pairs={{0,24},{4,28},{8,16},{12,20},{16,8},{20,12},{24,0},{28,4},{1,25},{... | collective-permute-start | bytes 245768 | tf_op jit(solution)/shard_map/ppermute | solution.py:276
  159.9 5.8 %collective-permute-start.74 = (f32[80,256]{1,0:T(8,128)S(1)}, f32[80,256]{1,0:T(8,128)S(1)}, u32[]{:S(2)}, u32[]{:S(2)}) collective-permute-start(f32[80,256]{1,0:T(8,128)S(1)} %add.107), channel_id=1, source_target_pairs={{0,16},{4,20},{8,24},{12,28},{16,0},{20,4},{24,8},{28,12},{1,17},{... | collective-permute-start | bytes 245768 | tf_op jit(solution)/shard_map/ppermute | solution.py:276
  (47 other events, 156.4 us)

commit v8 on v7

--- a/solution.py
+++ b/solution.py
@@ -339,8 +339,9 @@
     upper, lower = anchor_factor[:, :width], anchor_factor[:, width:]
     matrix, factor, part_factor = ((rank, rank), F32), ((rank, width), F32), ((rank, part_size), F32)
     for sweep in range(SWEEPS):
-        near, far = sum_steps(message, "dst", masks("dst", 1))
-        near_low, far_low = sum_steps(message_low, "dst", far_first("dst"))
+        steps = [masks("dst", 1), far_first("dst")]
+        near, far = sum_steps(message, "dst", steps[sweep == 0])
+        near_low, far_low = sum_steps(message_low, "dst", steps[sweep > 0])
         if sweep == 0:
             flipped = call(flip_kernel, [((hours, cols, rows), BF16)], "flip", 4 * half_flops, tensor, near)
         upper, gram_part, gram, sent, kept = call(

time: 169 us -> 168 us (level)
  waiting for transfers between devices: 54.9 us -> 44.3 us
  starting transfers between devices: 71.3 us -> 80 us
    ppermute x78, waiting for transfers between devices: 54.9 us -> 44.3 us  [swap(): lax.ppermute(array, axis, [(index, index ^ mask) for index in range(size)])]
    ppermute x78, starting transfers between devices: 71.3 us -> 80 us  [swap(): lax.ppermute(array, axis, [(index, index ^ mask) for index in range(size)])]
  transfers between devices with their start and end apart: 78 -> 78, of which waited for: 37 -> 34; matrix products, arithmetic and copies ran while one was open for 0% -> 0% of each run, Pallas kernels for 17% -> 17%
where the time goes in v8:
time: 168 us; the launch traced here: 167 us
  starting transfers between devices  80 us (48%)
  waiting for transfers between devices  44.3 us (26%)
  Pallas kernels  41.1 us (24%)
  between operations  1.73 us (1%)
    ppermute x78, starting transfers between devices, swap(): lax.ppermute(array, axis, [(index, index ^ mask) for index in range(size)])  80 us
    ppermute x78, waiting for transfers between devices, swap(): lax.ppermute(array, axis, [(index, index ^ mask) for index in range(size)])  44.3 us
    pallas_call x92, Pallas kernels, call(): pl.pallas_call(kernel, in_specs=[WHOLE] * len(args), out_specs=tuple((WHO...  32.4 us
    pallas_call x1, Pallas kernels, body(): pl.pallas_call(first_kernel, in_specs=[ANYWHERE] * 4, out_specs=(WHOLE,)...  7.31 us
  transfers between devices with their start and end apart: 78, of which 34 were waited for; matrix products, arithmetic and copies ran while one was open for 0% of the time, Pallas kernels for 17%

profile of v8, /device:TPU:0, one launch (start us, length us, event | category | flops | bytes accessed | tf_op | source)
XLA Modules:
  0.0 167.4 jit_solution(553749210976555207)
XLA Ops:
  0.6 7.3 %first.1 = (bf16[8,512,1024]{2,1,0:T(8,128)(2,1)S(1)}, f32[80,256]{1,0:T(8,128)S(1)}, f32[64,256]{1,0:T(8,128)S(1)}, f32[64,256]{1,0:T(8,128)S(1)}, f32[64,256]{...) custom-call(s32[8,512,1024]{2,1,0:T(8,128)} %counts.1, f32[8,4,8]{2,1,0:T(4,128)} %scales.1, ...), custom_call_target="tpu_custom_call" | custom-call | tf_op jit(solution)/shard_map/first/pallas_call | solution.py:314
  8.0 3.1 %collective-permute-start.2 = (f32[64,256]{1,0:T(8,128)S(1)}, f32[64,256]{1,0:T(8,128)S(1)}, u32[]{:S(2)}, u32[]{:S(2)}) collective-permute-start(f32[64,256]{1,0:T(8,128)S(1)} %get-tuple-element.128.left), channel_id=1, source_target_pairs={{0,1},{1,0},{2,3},{3,2},{4,5},{5,4},{6,7},{7,6},{8,9},{9,8},{10,11... | collective-permute-start | bytes 196616 | tf_op jit(solution)/shard_map/ppermute | solution.py:276
  11.1 2.5 %collective-permute-start = (f32[80,256]{1,0:T(8,128)S(1)}, f32[80,256]{1,0:T(8,128)S(1)}, u32[]{:S(2)}, u32[]{:S(2)}) collective-permute-start(f32[80,256]{1,0:T(8,128)S(1)} %get-tuple-element.123.left), channel_id=1, source_target_pairs={{0,3},{1,2},{2,1},{3,0},{4,7},{5,6},{6,5},{7,4},{8,11},{9,10},{10,... | collective-permute-start | bytes 245768 | tf_op jit(solution)/shard_map/ppermute | solution.py:276
  13.6 3.5 %collective-permute-start.3 = (f32[64,256]{1,0:T(8,128)S(1)}, f32[64,256]{1,0:T(8,128)S(1)}, u32[]{:S(2)}, u32[]{:S(2)}) collective-permute-start(f32[64,256]{1,0:T(8,128)S(1)} %add.79.near), channel_id=1, source_target_pairs={{0,2},{1,3},{2,0},{3,1},{4,6},{5,7},{6,4},{7,5},{8,10},{9,11},{10,... | collective-permute-start | bytes 196616 | tf_op jit(solution)/shard_map/ppermute | solution.py:276
  19.3 2.2 %flip.1._.flipped = bf16[8,1024,512]{2,1,0:T(8,128)(2,1)S(1)} custom-call(bf16[8,512,1024]{2,1,0:T(8,128)(2,1)S(1)} %get-tuple-element.122.tensor, f32[80,256]{1,0:T(8,128)S(1)} %add.78.near.after), custom_call_target="tpu_custom_call" | custom-call | flops 4294967296 | tf_op jit(solution)/shard_map/flip/pallas_call | solution.py:262
  25.6 1.6 collective-permute-start.5
  27.2 1.6 collective-permute-start.10
  29.3 1.5 collective-permute-start.8
  30.8 1.6 collective-permute-start.6
  32.4 1.7 %collective-permute-done.8 = f32[80,256]{1,0:T(8,128)S(1)} collective-permute-done((f32[80,256]{1,0:T(8,128)S(1)}, f32[80,256]{1,0:T(8,128)S(1)}, u32[]{:S(2)}, u32[]{:S(2)}) %collective-permute-start.8) | collective-permute-done | bytes 81952 | tf_op jit(solution)/shard_map/ppermute | solution.py:276
  39.3 2.6 %collective-permute-start.15 = (f32[64,256]{1,0:T(8,128)S(1)}, f32[64,256]{1,0:T(8,128)S(1)}, u32[]{:S(2)}, u32[]{:S(2)}) collective-permute-start(f32[64,256]{1,0:T(8,128)S(1)} %dest_lower.5.left), channel_id=1, source_target_pairs={{0,3},{1,2},{2,1},{3,0},{4,7},{5,6},{6,5},{7,4},{8,11},{9,10},{10,... | collective-permute-start | bytes 196616 | tf_op jit(solution)/shard_map/ppermute | solution.py:276
  42.5 2.9 %collective-permute-start.14 = (f32[80,256]{1,0:T(8,128)S(1)}, f32[80,256]{1,0:T(8,128)S(1)}, u32[]{:S(2)}, u32[]{:S(2)}) collective-permute-start(f32[80,256]{1,0:T(8,128)S(1)} %add.83.near), channel_id=1, source_target_pairs={{0,2},{1,3},{2,0},{3,1},{4,6},{5,7},{6,4},{7,5},{8,10},{9,11},{10,... | collective-permute-start | bytes 245768 | tf_op jit(solution)/shard_map/ppermute | solution.py:276
  45.8 3.4 %collective-permute-done.14.far = f32[80,256]{1,0:T(8,128)S(1)} collective-permute-done((f32[80,256]{1,0:T(8,128)S(1)}, f32[80,256]{1,0:T(8,128)S(1)}, u32[]{:S(2)}, u32[]{:S(2)}) %collective-permute-start.14) | collective-permute-done | bytes 81952 | tf_op jit(solution)/shard_map/ppermute | solution.py:276
  58.4 2.0 %collective-permute-done.21 = f32[80,256]{1,0:T(8,128)S(1)} collective-permute-done((f32[80,256]{1,0:T(8,128)S(1)}, f32[80,256]{1,0:T(8,128)S(1)}, u32[]{:S(2)}, u32[]{:S(2)}) %collective-permute-start.21) | collective-permute-done | bytes 81952 | tf_op jit(solution)/shard_map/ppermute | solution.py:276
  65.0 2.7 %collective-permute-start.28 = (f32[64,256]{1,0:T(8,128)S(1)}, f32[64,256]{1,0:T(8,128)S(1)}, u32[]{:S(2)}, u32[]{:S(2)}) collective-permute-start(f32[64,256]{1,0:T(8,128)S(1)} %dest_lower.6.left), channel_id=1, source_target_pairs={{0,3},{1,2},{2,1},{3,0},{4,7},{5,6},{6,5},{7,4},{8,11},{9,10},{10,... | collective-permute-start | bytes 196616 | tf_op jit(solution)/shard_map/ppermute | solution.py:276
  68.5 2.4 %collective-permute-start.27 = (f32[80,256]{1,0:T(8,128)S(1)}, f32[80,256]{1,0:T(8,128)S(1)}, u32[]{:S(2)}, u32[]{:S(2)}) collective-permute-start(f32[80,256]{1,0:T(8,128)S(1)} %add.88.near), channel_id=1, source_target_pairs={{0,2},{1,3},{2,0},{3,1},{4,6},{5,7},{6,4},{7,5},{8,10},{9,11},{10,... | collective-permute-start | bytes 245768 | tf_op jit(solution)/shard_map/ppermute | solution.py:276
  72.0 2.9 %collective-permute-done.27.far = f32[80,256]{1,0:T(8,128)S(1)} collective-permute-done((f32[80,256]{1,0:T(8,128)S(1)}, f32[80,256]{1,0:T(8,128)S(1)}, u32[]{:S(2)}, u32[]{:S(2)}) %collective-permute-start.27) | collective-permute-done | bytes 81952 | tf_op jit(solution)/shard_map/ppermute | solution.py:276
  79.4 1.5 collective-permute-start.36
  84.1 2.1 %collective-permute-done.34 = f32[80,256]{1,0:T(8,128)S(1)} collective-permute-done((f32[80,256]{1,0:T(8,128)S(1)}, f32[80,256]{1,0:T(8,128)S(1)}, u32[]{:S(2)}, u32[]{:S(2)}) %collective-permute-start.34) | collective-permute-done | bytes 81952 | tf_op jit(solution)/shard_map/ppermute | solution.py:276
  90.6 2.1 %collective-permute-start.41 = (f32[64,256]{1,0:T(8,128)S(1)}, f32[64,256]{1,0:T(8,128)S(1)}, u32[]{:S(2)}, u32[]{:S(2)}) collective-permute-start(f32[64,256]{1,0:T(8,128)S(1)} %dest_lower.7.left), channel_id=1, source_target_pairs={{0,3},{1,2},{2,1},{3,0},{4,7},{5,6},{6,5},{7,4},{8,11},{9,10},{10,... | collective-permute-start | bytes 196616 | tf_op jit(solution)/shard_map/ppermute | solution.py:276
  92.7 1.8 %collective-permute-done.39.right = f32[80,256]{1,0:T(8,128)S(1)} collective-permute-done((f32[80,256]{1,0:T(8,128)S(1)}, f32[80,256]{1,0:T(8,128)S(1)}, u32[]{:S(2)}, u32[]{:S(2)}) %collective-permute-start.39) | collective-permute-done | bytes 81952 | tf_op jit(solution)/shard_map/ppermute | solution.py:276
  97.8 2.9 %collective-permute-done.40.far = f32[80,256]{1,0:T(8,128)S(1)} collective-permute-done((f32[80,256]{1,0:T(8,128)S(1)}, f32[80,256]{1,0:T(8,128)S(1)}, u32[]{:S(2)}, u32[]{:S(2)}) %collective-permute-start.40) | collective-permute-done | bytes 81952 | tf_op jit(solution)/shard_map/ppermute | solution.py:276
  109.7 2.3 %collective-permute-done.47 = f32[80,256]{1,0:T(8,128)S(1)} collective-permute-done((f32[80,256]{1,0:T(8,128)S(1)}, f32[80,256]{1,0:T(8,128)S(1)}, u32[]{:S(2)}, u32[]{:S(2)}) %collective-permute-start.47) | collective-permute-done | bytes 81952 | tf_op jit(solution)/shard_map/ppermute | solution.py:276
  116.5 2.0 %collective-permute-start.54 = (f32[64,256]{1,0:T(8,128)S(1)}, f32[64,256]{1,0:T(8,128)S(1)}, u32[]{:S(2)}, u32[]{:S(2)}) collective-permute-start(f32[64,256]{1,0:T(8,128)S(1)} %dest_lower.8.left), channel_id=1, source_target_pairs={{0,3},{1,2},{2,1},{3,0},{4,7},{5,6},{6,5},{7,4},{8,11},{9,10},{10,... | collective-permute-start | bytes 196616 | tf_op jit(solution)/shard_map/ppermute | solution.py:276
  118.5 1.6 collective-permute-done.52.right
  123.8 2.7 %collective-permute-done.53.far = f32[80,256]{1,0:T(8,128)S(1)} collective-permute-done((f32[80,256]{1,0:T(8,128)S(1)}, f32[80,256]{1,0:T(8,128)S(1)}, u32[]{:S(2)}, u32[]{:S(2)}) %collective-permute-start.53) | collective-permute-done | bytes 81952 | tf_op jit(solution)/shard_map/ppermute | solution.py:276
  135.6 2.2 %collective-permute-done.60 = f32[80,256]{1,0:T(8,128)S(1)} collective-permute-done((f32[80,256]{1,0:T(8,128)S(1)}, f32[80,256]{1,0:T(8,128)S(1)}, u32[]{:S(2)}, u32[]{:S(2)}) %collective-permute-start.60) | collective-permute-done | bytes 81952 | tf_op jit(solution)/shard_map/ppermute | solution.py:276
  142.1 2.0 %collective-permute-start.67 = (f32[64,256]{1,0:T(8,128)S(1)}, f32[64,256]{1,0:T(8,128)S(1)}, u32[]{:S(2)}, u32[]{:S(2)}) collective-permute-start(f32[64,256]{1,0:T(8,128)S(1)} %dest_lower.9.left), channel_id=1, source_target_pairs={{0,3},{1,2},{2,1},{3,0},{4,7},{5,6},{6,5},{7,4},{8,11},{9,10},{10,... | collective-permute-start | bytes 196616 | tf_op jit(solution)/shard_map/ppermute | solution.py:276
  144.2 1.8 %collective-permute-done.65.right = f32[80,256]{1,0:T(8,128)S(1)} collective-permute-done((f32[80,256]{1,0:T(8,128)S(1)}, f32[80,256]{1,0:T(8,128)S(1)}, u32[]{:S(2)}, u32[]{:S(2)}) %collective-permute-start.65) | collective-permute-done | bytes 81952 | tf_op jit(solution)/shard_map/ppermute | solution.py:276
  149.2 2.9 %collective-permute-done.66.far = f32[80,256]{1,0:T(8,128)S(1)} collective-permute-done((f32[80,256]{1,0:T(8,128)S(1)}, f32[80,256]{1,0:T(8,128)S(1)}, u32[]{:S(2)}, u32[]{:S(2)}) %collective-permute-start.66) | collective-permute-done | bytes 81952 | tf_op jit(solution)/shard_map/ppermute | solution.py:276
  156.7 1.5 collective-permute-start.75
  161.3 2.1 %collective-permute-done.73 = f32[80,256]{1,0:T(8,128)S(1)} collective-permute-done((f32[80,256]{1,0:T(8,128)S(1)}, f32[80,256]{1,0:T(8,128)S(1)}, u32[]{:S(2)}, u32[]{:S(2)}) %collective-permute-start.73) | collective-permute-done | bytes 81952 | tf_op jit(solution)/shard_map/ppermute | solution.py:276
  (234 shorter events, 88.7 us)
Async XLA Ops:
  8.0 5.6 %collective-permute-start.2 = (f32[64,256]{1,0:T(8,128)S(1)}, f32[64,256]{1,0:T(8,128)S(1)}, u32[]{:S(2)}, u32[]{:S(2)}) collective-permute-start(f32[64,256]{1,0:T(8,128)S(1)} %get-tuple-element.128.left), channel_id=1, source_target_pairs={{0,1},{1,0},{2,3},{3,2},{4,5},{5,4},{6,7},{7,6},{8,9},{9,8},{10,11... | collective-permute-start | bytes 196616 | tf_op jit(solution)/shard_map/ppermute | solution.py:276
  11.1 6.9 %collective-permute-start = (f32[80,256]{1,0:T(8,128)S(1)}, f32[80,256]{1,0:T(8,128)S(1)}, u32[]{:S(2)}, u32[]{:S(2)}) collective-permute-start(f32[80,256]{1,0:T(8,128)S(1)} %get-tuple-element.123.left), channel_id=1, source_target_pairs={{0,3},{1,2},{2,1},{3,0},{4,7},{5,6},{6,5},{7,4},{8,11},{9,10},{10,... | collective-permute-start | bytes 245768 | tf_op jit(solution)/shard_map/ppermute | solution.py:276
  13.6 10.0 %collective-permute-start.3 = (f32[64,256]{1,0:T(8,128)S(1)}, f32[64,256]{1,0:T(8,128)S(1)}, u32[]{:S(2)}, u32[]{:S(2)}) collective-permute-start(f32[64,256]{1,0:T(8,128)S(1)} %add.79.near), channel_id=1, source_target_pairs={{0,2},{1,3},{2,0},{3,1},{4,6},{5,7},{6,4},{7,5},{8,10},{9,11},{10,... | collective-permute-start | bytes 196616 | tf_op jit(solution)/shard_map/ppermute | solution.py:276
  25.6 5.1 %collective-permute-start.5 = (f32[64,256]{1,0:T(8,128)S(1)}, f32[64,256]{1,0:T(8,128)S(1)}, u32[]{:S(2)}, u32[]{:S(2)}) collective-permute-start(f32[64,256]{1,0:T(8,128)S(1)} %add.80.left), channel_id=1, source_target_pairs={{0,8},{4,12},{8,0},{12,4},{16,24},{20,28},{24,16},{28,20},{1,9},{5... | collective-permute-start | bytes 196616 | tf_op jit(solution)/shard_map/ppermute | solution.py:276
  27.2 6.9 %collective-permute-start.10 = (f32[80,256]{1,0:T(8,128)S(1)}, f32[80,256]{1,0:T(8,128)S(1)}, u32[]{:S(2)}, u32[]{:S(2)}) collective-permute-start(f32[80,256]{1,0:T(8,128)S(1)} %add.82), channel_id=1, source_target_pairs={{0,24},{4,28},{8,16},{12,20},{16,8},{20,12},{24,0},{28,4},{1,25},{... | collective-permute-start | bytes 245768 | tf_op jit(solution)/shard_map/ppermute | solution.py:276
  28.8 5.8 %collective-permute-start.9 = (f32[80,256]{1,0:T(8,128)S(1)}, f32[80,256]{1,0:T(8,128)S(1)}, u32[]{:S(2)}, u32[]{:S(2)}) collective-permute-start(f32[80,256]{1,0:T(8,128)S(1)} %add.82), channel_id=1, source_target_pairs={{0,16},{4,20},{8,24},{12,28},{16,0},{20,4},{24,8},{28,12},{1,17},{... | collective-permute-start | bytes 245768 | tf_op jit(solution)/shard_map/ppermute | solution.py:276
  30.8 5.0 %collective-permute-start.6 = (f32[64,256]{1,0:T(8,128)S(1)}, f32[64,256]{1,0:T(8,128)S(1)}, u32[]{:S(2)}, u32[]{:S(2)}) collective-permute-start(f32[64,256]{1,0:T(8,128)S(1)} %add.81.near), channel_id=1, source_target_pairs={{0,16},{4,20},{8,24},{12,28},{16,0},{20,4},{24,8},{28,12},{1,17},{... | collective-permute-start | bytes 196616 | tf_op jit(solution)/shard_map/ppermute | solution.py:276
  39.3 6.4 %collective-permute-start.15 = (f32[64,256]{1,0:T(8,128)S(1)}, f32[64,256]{1,0:T(8,128)S(1)}, u32[]{:S(2)}, u32[]{:S(2)}) collective-permute-start(f32[64,256]{1,0:T(8,128)S(1)} %dest_lower.5.left), channel_id=1, source_target_pairs={{0,3},{1,2},{2,1},{3,0},{4,7},{5,6},{6,5},{7,4},{8,11},{9,10},{10,... | collective-permute-start | bytes 196616 | tf_op jit(solution)/shard_map/ppermute | solution.py:276
  42.5 6.7 %collective-permute-start.14 = (f32[80,256]{1,0:T(8,128)S(1)}, f32[80,256]{1,0:T(8,128)S(1)}, u32[]{:S(2)}, u32[]{:S(2)}) collective-permute-start(f32[80,256]{1,0:T(8,128)S(1)} %add.83.near), channel_id=1, source_target_pairs={{0,2},{1,3},{2,0},{3,1},{4,6},{5,7},{6,4},{7,5},{8,10},{9,11},{10,... | collective-permute-start | bytes 245768 | tf_op jit(solution)/shard_map/ppermute | solution.py:276
  53.5 6.9 %collective-permute-start.23 = (f32[80,256]{1,0:T(8,128)S(1)}, f32[80,256]{1,0:T(8,128)S(1)}, u32[]{:S(2)}, u32[]{:S(2)}) collective-permute-start(f32[80,256]{1,0:T(8,128)S(1)} %add.87), channel_id=1, source_target_pairs={{0,24},{4,28},{8,16},{12,20},{16,8},{20,12},{24,0},{28,4},{1,25},{... | collective-permute-start | bytes 245768 | tf_op jit(solution)/shard_map/ppermute | solution.py:276
  54.8 5.9 %collective-permute-start.22 = (f32[80,256]{1,0:T(8,128)S(1)}, f32[80,256]{1,0:T(8,128)S(1)}, u32[]{:S(2)}, u32[]{:S(2)}) collective-permute-start(f32[80,256]{1,0:T(8,128)S(1)} %add.87), channel_id=1, source_target_pairs={{0,16},{4,20},{8,24},{12,28},{16,0},{20,4},{24,8},{28,12},{1,17},{... | collective-permute-start | bytes 245768 | tf_op jit(solution)/shard_map/ppermute | solution.py:276
  65.0 6.3 %collective-permute-start.28 = (f32[64,256]{1,0:T(8,128)S(1)}, f32[64,256]{1,0:T(8,128)S(1)}, u32[]{:S(2)}, u32[]{:S(2)}) collective-permute-start(f32[64,256]{1,0:T(8,128)S(1)} %dest_lower.6.left), channel_id=1, source_target_pairs={{0,3},{1,2},{2,1},{3,0},{4,7},{5,6},{6,5},{7,4},{8,11},{9,10},{10,... | collective-permute-start | bytes 196616 | tf_op jit(solution)/shard_map/ppermute | solution.py:276
  68.5 6.4 %collective-permute-start.27 = (f32[80,256]{1,0:T(8,128)S(1)}, f32[80,256]{1,0:T(8,128)S(1)}, u32[]{:S(2)}, u32[]{:S(2)}) collective-permute-start(f32[80,256]{1,0:T(8,128)S(1)} %add.88.near), channel_id=1, source_target_pairs={{0,2},{1,3},{2,0},{3,1},{4,6},{5,7},{6,4},{7,5},{8,10},{9,11},{10,... | collective-permute-start | bytes 245768 | tf_op jit(solution)/shard_map/ppermute | solution.py:276
  78.1 4.9 %collective-permute-start.31 = (f32[64,256]{1,0:T(8,128)S(1)}, f32[64,256]{1,0:T(8,128)S(1)}, u32[]{:S(2)}, u32[]{:S(2)}) collective-permute-start(f32[64,256]{1,0:T(8,128)S(1)} %add.90.left), channel_id=1, source_target_pairs={{0,8},{4,12},{8,0},{12,4},{16,24},{20,28},{24,16},{28,20},{1,9},{5... | collective-permute-start | bytes 196616 | tf_op jit(solution)/shard_map/ppermute | solution.py:276
  79.4 6.8 %collective-permute-start.36 = (f32[80,256]{1,0:T(8,128)S(1)}, f32[80,256]{1,0:T(8,128)S(1)}, u32[]{:S(2)}, u32[]{:S(2)}) collective-permute-start(f32[80,256]{1,0:T(8,128)S(1)} %add.92), channel_id=1, source_target_pairs={{0,24},{4,28},{8,16},{12,20},{16,8},{20,12},{24,0},{28,4},{1,25},{... | collective-permute-start | bytes 245768 | tf_op jit(solution)/shard_map/ppermute | solution.py:276
  80.9 5.9 %collective-permute-start.35 = (f32[80,256]{1,0:T(8,128)S(1)}, f32[80,256]{1,0:T(8,128)S(1)}, u32[]{:S(2)}, u32[]{:S(2)}) collective-permute-start(f32[80,256]{1,0:T(8,128)S(1)} %add.92), channel_id=1, source_target_pairs={{0,16},{4,20},{8,24},{12,28},{16,0},{20,4},{24,8},{28,12},{1,17},{... | collective-permute-start | bytes 245768 | tf_op jit(solution)/shard_map/ppermute | solution.py:276
  90.6 6.2 %collective-permute-start.41 = (f32[64,256]{1,0:T(8,128)S(1)}, f32[64,256]{1,0:T(8,128)S(1)}, u32[]{:S(2)}, u32[]{:S(2)}) collective-permute-start(f32[64,256]{1,0:T(8,128)S(1)} %dest_lower.7.left), channel_id=1, source_target_pairs={{0,3},{1,2},{2,1},{3,0},{4,7},{5,6},{6,5},{7,4},{8,11},{9,10},{10,... | collective-permute-start | bytes 196616 | tf_op jit(solution)/shard_map/ppermute | solution.py:276
  94.5 6.2 %collective-permute-start.40 = (f32[80,256]{1,0:T(8,128)S(1)}, f32[80,256]{1,0:T(8,128)S(1)}, u32[]{:S(2)}, u32[]{:S(2)}) collective-permute-start(f32[80,256]{1,0:T(8,128)S(1)} %add.93.near), channel_id=1, source_target_pairs={{0,2},{1,3},{2,0},{3,1},{4,6},{5,7},{6,4},{7,5},{8,10},{9,11},{10,... | collective-permute-start | bytes 245768 | tf_op jit(solution)/shard_map/ppermute | solution.py:276
  96.8 5.0 %collective-permute-start.42 = (f32[64,256]{1,0:T(8,128)S(1)}, f32[64,256]{1,0:T(8,128)S(1)}, u32[]{:S(2)}, u32[]{:S(2)}) collective-permute-start(f32[64,256]{1,0:T(8,128)S(1)} %add.94.near), channel_id=1, source_target_pairs={{0,1},{1,0},{2,3},{3,2},{4,5},{5,4},{6,7},{7,6},{8,9},{9,8},{10,11... | collective-permute-start | bytes 196616 | tf_op jit(solution)/shard_map/ppermute | solution.py:276
  105.1 6.9 %collective-permute-start.49 = (f32[80,256]{1,0:T(8,128)S(1)}, f32[80,256]{1,0:T(8,128)S(1)}, u32[]{:S(2)}, u32[]{:S(2)}) collective-permute-start(f32[80,256]{1,0:T(8,128)S(1)} %add.97), channel_id=1, source_target_pairs={{0,24},{4,28},{8,16},{12,20},{16,8},{20,12},{24,0},{28,4},{1,25},{... | collective-permute-start | bytes 245768 | tf_op jit(solution)/shard_map/ppermute | solution.py:276
  106.5 6.0 %collective-permute-start.48 = (f32[80,256]{1,0:T(8,128)S(1)}, f32[80,256]{1,0:T(8,128)S(1)}, u32[]{:S(2)}, u32[]{:S(2)}) collective-permute-start(f32[80,256]{1,0:T(8,128)S(1)} %add.97), channel_id=1, source_target_pairs={{0,16},{4,20},{8,24},{12,28},{16,0},{20,4},{24,8},{28,12},{1,17},{... | collective-permute-start | bytes 245768 | tf_op jit(solution)/shard_map/ppermute | solution.py:276
  116.5 6.2 %collective-permute-start.54 = (f32[64,256]{1,0:T(8,128)S(1)}, f32[64,256]{1,0:T(8,128)S(1)}, u32[]{:S(2)}, u32[]{:S(2)}) collective-permute-start(f32[64,256]{1,0:T(8,128)S(1)} %dest_lower.8.left), channel_id=1, source_target_pairs={{0,3},{1,2},{2,1},{3,0},{4,7},{5,6},{6,5},{7,4},{8,11},{9,10},{10,... | collective-permute-start | bytes 196616 | tf_op jit(solution)/shard_map/ppermute | solution.py:276
  120.2 6.4 %collective-permute-start.53 = (f32[80,256]{1,0:T(8,128)S(1)}, f32[80,256]{1,0:T(8,128)S(1)}, u32[]{:S(2)}, u32[]{:S(2)}) collective-permute-start(f32[80,256]{1,0:T(8,128)S(1)} %add.98.near), channel_id=1, source_target_pairs={{0,2},{1,3},{2,0},{3,1},{4,6},{5,7},{6,4},{7,5},{8,10},{9,11},{10,... | collective-permute-start | bytes 245768 | tf_op jit(solution)/shard_map/ppermute | solution.py:276
  122.7 5.0 %collective-permute-start.55 = (f32[64,256]{1,0:T(8,128)S(1)}, f32[64,256]{1,0:T(8,128)S(1)}, u32[]{:S(2)}, u32[]{:S(2)}) collective-permute-start(f32[64,256]{1,0:T(8,128)S(1)} %add.99.near), channel_id=1, source_target_pairs={{0,1},{1,0},{2,3},{3,2},{4,5},{5,4},{6,7},{7,6},{8,9},{9,8},{10,11... | collective-permute-start | bytes 196616 | tf_op jit(solution)/shard_map/ppermute | solution.py:276
  130.9 6.9 %collective-permute-start.62 = (f32[80,256]{1,0:T(8,128)S(1)}, f32[80,256]{1,0:T(8,128)S(1)}, u32[]{:S(2)}, u32[]{:S(2)}) collective-permute-start(f32[80,256]{1,0:T(8,128)S(1)} %add.102), channel_id=1, source_target_pairs={{0,24},{4,28},{8,16},{12,20},{16,8},{20,12},{24,0},{28,4},{1,25},{... | collective-permute-start | bytes 245768 | tf_op jit(solution)/shard_map/ppermute | solution.py:276
  132.3 5.9 %collective-permute-start.61 = (f32[80,256]{1,0:T(8,128)S(1)}, f32[80,256]{1,0:T(8,128)S(1)}, u32[]{:S(2)}, u32[]{:S(2)}) collective-permute-start(f32[80,256]{1,0:T(8,128)S(1)} %add.102), channel_id=1, source_target_pairs={{0,16},{4,20},{8,24},{12,28},{16,0},{20,4},{24,8},{28,12},{1,17},{... | collective-permute-start | bytes 245768 | tf_op jit(solution)/shard_map/ppermute | solution.py:276
  142.1 6.2 %collective-permute-start.67 = (f32[64,256]{1,0:T(8,128)S(1)}, f32[64,256]{1,0:T(8,128)S(1)}, u32[]{:S(2)}, u32[]{:S(2)}) collective-permute-start(f32[64,256]{1,0:T(8,128)S(1)} %dest_lower.9.left), channel_id=1, source_target_pairs={{0,3},{1,2},{2,1},{3,0},{4,7},{5,6},{6,5},{7,4},{8,11},{9,10},{10,... | collective-permute-start | bytes 196616 | tf_op jit(solution)/shard_map/ppermute | solution.py:276
  146.0 6.2 %collective-permute-start.66 = (f32[80,256]{1,0:T(8,128)S(1)}, f32[80,256]{1,0:T(8,128)S(1)}, u32[]{:S(2)}, u32[]{:S(2)}) collective-permute-start(f32[80,256]{1,0:T(8,128)S(1)} %add.103.near), channel_id=1, source_target_pairs={{0,2},{1,3},{2,0},{3,1},{4,6},{5,7},{6,4},{7,5},{8,10},{9,11},{10,... | collective-permute-start | bytes 245768 | tf_op jit(solution)/shard_map/ppermute | solution.py:276
  148.3 5.0 %collective-permute-start.68 = (f32[64,256]{1,0:T(8,128)S(1)}, f32[64,256]{1,0:T(8,128)S(1)}, u32[]{:S(2)}, u32[]{:S(2)}) collective-permute-start(f32[64,256]{1,0:T(8,128)S(1)} %add.104.near), channel_id=1, source_target_pairs={{0,1},{1,0},{2,3},{3,2},{4,5},{5,4},{6,7},{7,6},{8,9},{9,8},{10,11... | collective-permute-start | bytes 196616 | tf_op jit(solution)/shard_map/ppermute | solution.py:276
  155.4 4.9 %collective-permute-start.70 = (f32[64,256]{1,0:T(8,128)S(1)}, f32[64,256]{1,0:T(8,128)S(1)}, u32[]{:S(2)}, u32[]{:S(2)}) collective-permute-start(f32[64,256]{1,0:T(8,128)S(1)} %add.105.left), channel_id=1, source_target_pairs={{0,8},{4,12},{8,0},{12,4},{16,24},{20,28},{24,16},{28,20},{1,9},{5... | collective-permute-start | bytes 196616 | tf_op jit(solution)/shard_map/ppermute | solution.py:276
  156.7 6.7 %collective-permute-start.75 = (f32[80,256]{1,0:T(8,128)S(1)}, f32[80,256]{1,0:T(8,128)S(1)}, u32[]{:S(2)}, u32[]{:S(2)}) collective-permute-start(f32[80,256]{1,0:T(8,128)S(1)} %add.107), channel_id=1, source_target_pairs={{0,24},{4,28},{8,16},{12,20},{16,8},{20,12},{24,0},{28,4},{1,25},{... | collective-permute-start | bytes 245768 | tf_op jit(solution)/shard_map/ppermute | solution.py:276
  158.2 5.9 %collective-permute-start.74 = (f32[80,256]{1,0:T(8,128)S(1)}, f32[80,256]{1,0:T(8,128)S(1)}, u32[]{:S(2)}, u32[]{:S(2)}) collective-permute-start(f32[80,256]{1,0:T(8,128)S(1)} %add.107), channel_id=1, source_target_pairs={{0,16},{4,20},{8,24},{12,28},{16,0},{20,4},{24,8},{28,12},{1,17},{... | collective-permute-start | bytes 245768 | tf_op jit(solution)/shard_map/ppermute | solution.py:276
  (47 other events, 157.5 us)
